TPU v7x, 32 devices: a whole 2x2x4 slice. The times are simulated.
32 devices in a mesh: seq: 8 (over y, x, core), hid: 4 (over z).
Axes of the slice: x: 2, y: 2, z: 4, core: 2. Of those that a mesh axis runs over, the one named last changes fastest.
Arguments:
- tokens_in: bfloat16 [32, 1024, 768], P('hid', 'seq'), may hold values from -6 to 6
- image_lengths: int32 [32, 64], P('hid'), may hold values from 0 to 1024, as said below
- attn_weight: float32 [3072, 768], P('hid')
- attn_moment: float32 [3072, 768], P('hid'), may hold values from -512 to 512
- attn_average: float32 [3072, 768], P('hid')
- mlp_weight: float32 [2, 3072, 768], P(None, 'hid'), may hold values from -0.21875 to 0.21875
- mlp_moment: float32 [2, 3072, 768], P(None, 'hid'), may hold values from -512 to 512
- mlp_average: float32 [2, 3072, 768], P(None, 'hid'), may hold values from -0.21875 to 0.21875
- vector_params: float32 [12, 768], replicated
- vector_moment: float32 [12, 768], replicated, may hold values from -512 to 512
- vector_average: float32 [12, 768], replicated
- out_grad: bfloat16 [32, 1024, 768], P('hid', 'seq'), may hold values from -6 to 6
Outputs:
- block_out: float32 [32, 1024, 768], P('hid', 'seq')
- input_grad: float32 [32, 1024, 768], P('hid', 'seq')
- attn_grad: float32 [3072, 768], P('hid')
- attn_moment_new: float32 [3072, 768], P('hid')
- attn_weight_new: float32 [3072, 768], P('hid')
- attn_average_new: float32 [3072, 768], P('hid')
- mlp_grad: float32 [2, 3072, 768], P(None, 'hid')
- mlp_moment_new: float32 [2, 3072, 768], P(None, 'hid')
- mlp_weight_new: float32 [2, 3072, 768], P(None, 'hid')
- mlp_average_new: float32 [2, 3072, 768], P(None, 'hid')
- vector_grad: float32 [12, 768], replicated
- vector_moment_new: float32 [12, 768], replicated
- vector_params_new: float32 [12, 768], replicated
- vector_average_new: float32 [12, 768], replicated
Inputs may be any that keep to these rules, and one draw needn't show every extreme that they name: `image_lengths`: the nonzero entries of a row come first; a row sums to between 897 and 1024, and the positions after its sum are padding. Among the 8 rows of each index of hid, one holds a single image of 1024 patches.
All inputs are finite; a program needn't handle non-finite values.
Results may differ from a plain program's by a relative error of at most 0.019.
Values may be sent and summed in bfloat16 or wider, within the bound.
No kernel may reach another device: no remote copies, remote signals or barrier semaphores. Data moves between devices by JAX's collectives and lax.ppermute only.
A program may use at most 320 MiB of HBM per device.

v0:
```python
import functools

import jax
import jax.numpy as jnp
from jax import lax
from jax.experimental import pallas as pl
from jax.experimental.pallas import tpu as pltpu
from jax.sharding import PartitionSpec as P

HEADS = 12
HEAD_DIM = 64

score_scale = 0.125
norm_eps = 1e-06
big_negative = -1e30
matrix_rate = 0.0001
vector_rate = 0.001
momentum_decay = 0.9
weight_decay = 0.0001
average_decay = 0.9

low = jnp.bfloat16
wide = jnp.float32
kernel_vmem = 56 * 1024 * 1024


def cost(microseconds):
    return pl.CostEstimate(
        flops=int(4e+08 * microseconds) + 1000, bytes_accessed=1000, transcendentals=0
    )


def rows_by_rows(a, b):
    return lax.dot_general(a, b, (((1,), (1,)), ((), ())), preferred_element_type=wide)


def rows_by_cols(a, b):
    return lax.dot_general(a, b, (((1,), (0,)), ((), ())), preferred_element_type=wide)


def cols_by_cols(a, b):
    return lax.dot_general(a, b, (((0,), (0,)), ((), ())), preferred_element_type=wide)


def normalize(inputs, gain_row, offset):
    center = inputs - jnp.mean(inputs, axis=-1, keepdims=True)
    spread = jnp.mean(center * center, axis=-1, keepdims=True)
    return center * lax.rsqrt(spread + norm_eps) * gain_row + offset


def renew(weight, moment, average, gradient, decay_rate, step_rate):
    step_grad = gradient + decay_rate * weight
    moment_new = momentum_decay * moment + step_grad
    weight_new = weight - step_rate * (step_grad + momentum_decay * moment_new)
    average_new = average_decay * average + (1.0 - average_decay) * weight_new
    return (gradient, moment_new, weight_new, average_new)


def params(**kwargs):
    return pltpu.CompilerParams(vmem_limit_bytes=kernel_vmem, **kwargs)


def smem():
    return pl.BlockSpec(memory_space=pltpu.SMEM)


def whole_vmem():
    return pl.BlockSpec(memory_space=pltpu.VMEM)


def in_place():
    return pl.BlockSpec(memory_space=pl.ANY)


def attention_forward_kernel(tile, q_ref, k_ref, v_ref, query_seg, key_seg, valid_ref, *refs):
    o_ref, lse_ref = refs[-2:]
    rows = q_ref.shape[0]
    lane = lax.broadcasted_iota(jnp.int32, (1, 128), 1)
    k = k_ref[...]
    v = v_ref[...]
    v_and_ones = jnp.concatenate([v, jnp.ones_like(v)], axis=1)
    for start in range(0, rows, tile):
        part = pl.ds(start, tile)
        q = q_ref[part, :]
        same = query_seg[part, :] == key_seg[...]
        heads = []
        for head in range(2):
            mine = (lane // HEAD_DIM) == head
            scores = rows_by_rows(jnp.where(mine, q, jnp.zeros_like(q)), k)
            scores = jnp.where(same, scores, big_negative)
            top = jnp.max(scores, axis=1, keepdims=True)
            weights = jnp.exp(scores - top).astype(low)
            sums = rows_by_cols(weights, v_and_ones)
            total = sums[:, 128:]
            heads.append(sums[:, :128] / total)
            lse_ref[0, head : head + 1, part] = jnp.transpose(top + jnp.log(total))[:1, :]
        joined = jnp.where(lane < HEAD_DIM, heads[0], heads[1]) * valid_ref[part, :]
        o_ref[part, :] = joined.astype(low)


def attention_forward(q, k, v, query_seg, key_seg, valid, pairs, earlier=(), after=()):
    rows, width = q.shape
    keys = k.shape[0]
    column = lambda n: pl.BlockSpec((n, 128), lambda g: (0, pairs[0] + g))
    whole = lambda a: pl.BlockSpec(a.shape, lambda g: (0, 0))
    return pl.pallas_call(
        functools.partial(attention_forward_kernel, min(128, rows)),
        grid=(len(pairs),),
        in_specs=[
            column(rows),
            column(keys),
            column(keys),
            whole(query_seg),
            whole(key_seg),
            whole(valid),
        ]
        + [in_place()] * (len(earlier) + len(after)),
        out_specs=[
            column(rows),
            pl.BlockSpec((1, 2, rows), lambda g: (pairs[0] + g, 0, 0)),
        ],
        out_shape=[
            jax.ShapeDtypeStruct((rows, width), low),
            jax.ShapeDtypeStruct((width // 128, 2, rows), wide),
        ],
        input_output_aliases={6 + i: i for i in range(len(earlier))},
        compiler_params=params(),
        cost_estimate=cost(4 * len(pairs)),
        name="attention_forward",
    )(q, k, v, query_seg, key_seg, valid, *earlier, *after)


def attention_backward_pair(
    tile, q_ref, k_ref, v_ref, do_ref, lse_ref, delta_ref, query_seg, key_seg, sums
):
    dq, dk, dv = sums
    rows = q_ref.shape[0]
    lane = lax.broadcasted_iota(jnp.int32, (1, 128), 1)
    k = k_ref[...]
    v = v_ref[...]
    k_turned = jnp.transpose(k)
    q_turned = jnp.transpose(q_ref[...])
    do_turned = jnp.transpose(do_ref[...])
    for start in range(0, rows, tile):
        part = pl.ds(start, tile)
        q = q_ref[part, :]
        do = do_ref[part, :]
        same = key_seg[...] == query_seg[:, part]
        for head in range(2):
            mine = (lane // HEAD_DIM) == head
            features = slice(head * HEAD_DIM, (head + 1) * HEAD_DIM)
            scores = rows_by_rows(k, jnp.where(mine, q, jnp.zeros_like(q)))
            scores = jnp.where(same, scores, big_negative)
            probs = jnp.exp(scores - lse_ref[0, head : head + 1, part])
            grads = rows_by_rows(v, jnp.where(mine, do, jnp.zeros_like(do)))
            grads = (probs * (grads - delta_ref[0, head : head + 1, part])).astype(low)
            here = slice(start, start + tile)
            dv_term = rows_by_rows(do_turned[features, here], probs.astype(low))
            dk_term = rows_by_rows(q_turned[features, here], grads)
            dq[features, part] = score_scale * rows_by_cols(k_turned[features, :], grads)
            if start == 0:
                dk[features, :] = dk_term
                dv[features, :] = dv_term
            else:
                dk[features, :] += dk_term
                dv[features, :] += dv_term


def attention_backward_kernel(tile, *refs):
    dq_ref, dk_ref, dv_ref, dq, dk, dv = refs[-6:]
    attention_backward_pair(tile, *refs[:8], (dq, dk, dv))
    for out, total in zip((dq_ref, dk_ref, dv_ref), (dq, dk, dv)):
        out[...] = jnp.transpose(total[...].astype(low))


def attention_backward(q, k, v, do, lse, delta, query_seg, key_seg):
    rows, width = q.shape
    keys = k.shape[0]
    pairs = width // 128
    column = lambda n: pl.BlockSpec((n, 128), lambda g: (0, g))
    whole = lambda a: pl.BlockSpec(a.shape, lambda g: (0, 0))
    stat = pl.BlockSpec((1, 2, rows), lambda g: (g, 0, 0))
    return pl.pallas_call(
        functools.partial(attention_backward_kernel, min(256, rows)),
        grid=(pairs,),
        in_specs=[
            column(rows),
            column(keys),
            column(keys),
            column(rows),
            stat,
            stat,
            whole(query_seg),
            whole(key_seg),
        ],
        out_specs=[column(rows), column(keys), column(keys)],
        out_shape=[
            jax.ShapeDtypeStruct((rows, width), low),
            jax.ShapeDtypeStruct((keys, width), low),
            jax.ShapeDtypeStruct((keys, width), low),
        ],
        scratch_shapes=[
            pltpu.VMEM((128, rows), wide),
            pltpu.VMEM((128, keys), wide),
            pltpu.VMEM((128, keys), wide),
        ],
        compiler_params=params(),
        cost_estimate=cost(6 * pairs),
        name="attention_backward",
    )(q, k, v, do, lse, delta, query_seg, key_seg)


def attention_grads_kernel(tile, seqs, place, *refs):
    dt_ref, a_ref, o_ref = refs[8:11]
    dq_ref, dk_ref, dv_ref, even_ref, odd_ref, dq, dk, dv, dq_all, dk_all, dv_all, grads = refs[-12:]
    attention_backward_pair(tile, *refs[:8], (dq, dk, dv))
    pair = pl.program_id(0)
    band = pl.ds(pl.multiple_of(pair * 128, 128), 128)
    for out, total, group in zip(
        (dq_ref, dk_ref, dv_ref), (dq, dk, dv), (dq_all, dk_all, dv_all)
    ):
        rounded = total[...].astype(low)
        out[...] = jnp.transpose(rounded)
        group[band, :] = rounded

    @pl.when(pair == pl.num_programs(0) - 1)
    def _():
        grads[0] = rows_by_cols(dq_all[...], a_ref[...]).astype(low)
        grads[1] = rows_by_cols(dk_all[...], a_ref[...]).astype(low)
        grads[2] = rows_by_cols(dv_all[...], a_ref[...]).astype(low)
        grads[3] = cols_by_cols(dt_ref[...], o_ref[...]).astype(low)
        piece = even_ref.shape[2]
        for other in range(seqs):
            source = pl.ds(pl.multiple_of((place[1] ^ other) * piece, 16), piece)
            target = odd_ref if other % 2 else even_ref
            for matrix in range(4):
                target[other // 2, matrix ^ place[0]] = grads[matrix, source, :]


def attention_grads(
    place, seqs, q, k, v, do, lse, delta, query_seg, key_seg, dt, a, o, pairs, earlier=()
):
    rows, width = q.shape
    count = len(pairs)
    piece = count * 128 // seqs
    group = pairs[0] // count
    column = pl.BlockSpec((rows, 128), lambda g, p: (0, pairs[0] + g))
    fixed = lambda a: pl.BlockSpec(a.shape, lambda g, p: (0,) * len(a.shape))
    stat = pl.BlockSpec((1, 2, rows), lambda g, p: (pairs[0] + g, 0, 0))
    grad = jax.ShapeDtypeStruct((rows, width), low)
    result = jax.ShapeDtypeStruct((seqs // 2, 4, piece, width), low)
    return pl.pallas_call(
        functools.partial(attention_grads_kernel, min(256, rows), seqs),
        grid_spec=pltpu.PrefetchScalarGridSpec(
            num_scalar_prefetch=1,
            grid=(count,),
            in_specs=[column] * 4
            + [
                stat,
                stat,
                fixed(query_seg),
                fixed(key_seg),
                pl.BlockSpec((rows, count * 128), lambda g, p: (0, group)),
                fixed(a),
                fixed(o),
            ]
            + [in_place()] * len(earlier),
            out_specs=[column] * 3 + [fixed(result)] * 2,
            scratch_shapes=[pltpu.VMEM((128, rows), wide)] * 3
            + [pltpu.VMEM((count * 128, rows), low)] * 3
            + [pltpu.VMEM((4, count * 128, width), low)],
        ),
        out_shape=[grad] * 3 + [result] * 2,
        input_output_aliases={12 + i: i for i in range(len(earlier))},
        compiler_params=params(),
        cost_estimate=cost(7 * count),
        name="attention_backward",
    )(place, q, k, v, do, lse, delta, query_seg, key_seg, dt, a, o, *earlier)


def mlp_step(a, dy, up, down, bias):
    before = rows_by_rows(a, up) + bias
    grad_active = rows_by_rows(dy, down)
    density = 0.3989422804014327 * jnp.exp(-0.5 * before * before)
    below = 0.5 * (1.0 + lax.erf(before * 0.7071067811865476))
    active = (before * below).astype(low)
    grad_before = ((below + before * density) * grad_active).astype(low)
    bias_grad = jnp.sum(grad_before.astype(wide), axis=0, keepdims=True)
    up_grad = cols_by_cols(grad_before, a)
    down_grad = cols_by_cols(active, dy)
    return (
        rows_by_cols(active, down),
        rows_by_cols(grad_before, up),
        up_grad,
        down_grad,
        bias_grad,
    )


def add_up(step, steps, h_ref, vec_ref, out_ref, da_ref, out_sum, da_sum, out_term, da_term):
    @pl.when(step == 0)
    def _():
        out_sum[...] = out_term
        da_sum[...] = da_term

    @pl.when(step > 0)
    def _():
        out_sum[...] += out_term
        da_sum[...] += da_term

    @pl.when(step == steps - 1)
    def _():
        out_ref[...] = (h_ref[...] + out_sum[...] + vec_ref[7:8, :]).astype(low)
        da_ref[...] = da_sum[...]


def mlp_plain_kernel(
    a_ref,
    dy_ref,
    h_ref,
    vec_ref,
    up_ref,
    dn_ref,
    hb_ref,
    out_ref,
    da_ref,
    gup,
    gdn,
    ghb,
    out_sum,
    da_sum,
):
    out_term, da_term, up_grad, down_grad, bias_grad = mlp_step(
        a_ref[...], dy_ref[...], up_ref[...], dn_ref[...], hb_ref[0]
    )
    gup[...] = up_grad.astype(low)
    gdn[...] = down_grad.astype(low)
    ghb[0] = bias_grad
    step, steps = pl.program_id(0), pl.num_programs(0)
    add_up(step, steps, h_ref, vec_ref, out_ref, da_ref, out_sum, da_sum, out_term, da_term)


def mlp_plain(a, dy, h, vec, up, down, bias, step_width=768):
    rows, width = a.shape
    hidden = up.shape[0]
    steps = hidden // step_width
    whole = pl.BlockSpec((rows, width), lambda i: (0, 0))
    chunk = pl.BlockSpec((step_width, width), lambda i: (i, 0))
    strip = pl.BlockSpec((1, 1, step_width), lambda i: (i, 0, 0))
    return pl.pallas_call(
        mlp_plain_kernel,
        grid=(steps,),
        in_specs=[whole, whole, whole, pl.BlockSpec(vec.shape, lambda i: (0, 0))]
        + [chunk, chunk, strip],
        out_specs=[whole, whole, chunk, chunk, strip],
        out_shape=[
            jax.ShapeDtypeStruct((rows, width), low),
            jax.ShapeDtypeStruct((rows, width), wide),
        ]
        + [jax.ShapeDtypeStruct((hidden, width), low)] * 2
        + [jax.ShapeDtypeStruct((steps, 1, step_width), wide)],
        scratch_shapes=[pltpu.VMEM((rows, width), wide)] * 2,
        compiler_params=params(),
        name="mlp_both_ways",
    )(a, dy, h, vec, up, down, bias.reshape(steps, 1, step_width))


def norm_parts(rows):
    center = rows - jnp.mean(rows, axis=-1, keepdims=True)
    scale = lax.rsqrt(jnp.mean(center * center, axis=-1, keepdims=True) + norm_eps)
    return center * scale, scale


def norm_back(unit, scale, gain, grad):
    inner = grad * gain
    return scale * (
        inner
        - jnp.mean(inner, axis=-1, keepdims=True)
        - unit * jnp.mean(inner * unit, axis=-1, keepdims=True)
    )


def add_rows(ref, rows, first):
    total = [jnp.sum(row, axis=0, keepdims=True) for row in rows]
    total = jnp.concatenate(total + [jnp.zeros_like(total[0])] * (8 - len(total)), axis=0)

    @pl.when(first)
    def _():
        ref[...] = total

    @pl.when(jnp.logical_not(first))
    def _():
        ref[...] += total


def gather_rows(place, local_ref, piece_refs, out_ref):
    hid_index, seq_index = place[0], place[1]
    quarter = local_ref.shape[0]
    steps, _, rows, _ = piece_refs[0].shape
    out_ref[pl.ds(pl.multiple_of(hid_index * quarter, 16), quarter), :] = local_ref[...]
    for step in range(steps):
        for number, piece_ref in enumerate(piece_refs):
            for chunk, away in enumerate(((0, 4), (2, 6), (0, 2), (4, 6))[number // 2]):
                away += number % 2
                start = (hid_index ^ (step + 1)) * quarter + (seq_index ^ away) * (2 * rows)
                start += (number // 4) * rows
                target = pl.ds(pl.multiple_of(start, 16), rows)
                out_ref[target, :] = piece_ref[step, chunk]


def project_kernel(pieces, place, x_ref, vec_ref, *refs):
    if pieces:
        w_ref, a_ref, q_ref, k_ref, v_ref = refs[pieces:]

        @pl.when(pl.program_id(0) == 0)
        def _():
            gather_rows(place, refs[0], refs[1:pieces], w_ref)

    else:
        w_ref, a_ref, q_ref, k_ref, v_ref = refs
    width = x_ref.shape[1]
    unit, _ = norm_parts(x_ref[...].astype(wide))
    first = (unit * vec_ref[0:1, :] + vec_ref[1:2, :]).astype(low)
    a_ref[...] = first
    q = (rows_by_rows(first, w_ref[0:width, :]) + vec_ref[2:3, :]).astype(low)
    q_ref[...] = (q.astype(wide) * score_scale).astype(low)
    k_ref[...] = rows_by_rows(first, w_ref[width : 2 * width, :]).astype(low)
    v = rows_by_rows(first, w_ref[2 * width : 3 * width, :]) + vec_ref[3:4, :]
    v_ref[...] = v.astype(low)


def row_tile(rows):
    return min(256, rows)


def project(place, x, vec, pieces, whole):
    rows, width = x.shape
    tile = row_tile(rows)
    strip = pl.BlockSpec((tile, width), lambda i, p: (i, 0))
    fixed = lambda a: pl.BlockSpec(a.shape, lambda i, p: (0,) * len(a.shape))
    arrays = pieces if whole is None else [whole]
    matrix = jax.ShapeDtypeStruct((4 * width, width), low)
    strips = [jax.ShapeDtypeStruct((rows, width), low)] * 4
    results = pl.pallas_call(
        functools.partial(project_kernel, len(pieces)),
        grid_spec=pltpu.PrefetchScalarGridSpec(
            num_scalar_prefetch=1,
            grid=(rows // tile,),
            in_specs=[strip, fixed(vec)] + [fixed(a) for a in arrays],
            out_specs=([fixed(matrix)] if whole is None else []) + [strip] * 4,
        ),
        out_shape=([matrix] if whole is None else []) + strips,
        compiler_params=params(),
        cost_estimate=cost(10),
        name="norm_and_project",
    )(place, x, vec, *arrays)
    return results if whole is None else [whole] + list(results)


def join_kernel(o_ref, x_ref, w_ref, vec_ref, h_ref, a_ref):
    joined = x_ref[...].astype(wide) + rows_by_rows(o_ref[...], w_ref[...]) + vec_ref[4:5, :]
    h_ref[...] = joined
    unit, _ = norm_parts(joined)
    a_ref[...] = (unit * vec_ref[5:6, :] + vec_ref[6:7, :]).astype(low)


def join(o, x, w, vec):
    rows, width = x.shape
    tile = row_tile(rows)
    strip = pl.BlockSpec((tile, width), lambda i: (i, 0))
    return pl.pallas_call(
        join_kernel,
        grid=(rows // tile,),
        in_specs=[
            strip,
            strip,
            pl.BlockSpec((width, width), lambda i: (3, 0)),
            pl.BlockSpec(vec.shape, lambda i: (0, 0)),
        ],
        out_specs=[strip, strip],
        out_shape=[
            jax.ShapeDtypeStruct((rows, width), wide),
            jax.ShapeDtypeStruct((rows, width), low),
        ],
        compiler_params=params(),
        cost_estimate=cost(6),
        name="join_and_norm",
    )(o, x, w, vec)


def branch_back_rows(da, h, dy, o, valid, w, vec_ref):
    unit, scale = norm_parts(h)
    dy = dy.astype(wide)
    dh = dy + norm_back(unit, scale, vec_ref[5:6, :], da)
    dt = dh.astype(low)
    do = (rows_by_cols(dt, w) * valid).astype(low)
    product = do.astype(wide) * o.astype(wide)
    width = product.shape[1]
    lane = lax.broadcasted_iota(jnp.int32, (width, 128), 0)
    head = lax.broadcasted_iota(jnp.int32, (width, 128), 1)
    pick = (lane // HEAD_DIM == head).astype(low)
    high = product.astype(low)
    rest = (product - high.astype(wide)).astype(low)
    delta = jnp.transpose(rows_by_cols(high, pick) + rows_by_cols(rest, pick))
    return dh, dt, do, delta, [da * unit, da, dt.astype(wide), dy]


def branch_back_kernel(
    da_ref, h_ref, dy_ref, o_ref, valid_ref, w_ref, vec_ref, dh_ref, dt_ref, do_ref, delta_ref, sums
):
    dh, dt, do, delta, rows = branch_back_rows(
        da_ref[...], h_ref[...], dy_ref[...], o_ref[...], valid_ref[...], w_ref[...], vec_ref
    )
    dh_ref[...] = dh
    dt_ref[...] = dt
    do_ref[...] = do
    for pair in range(delta_ref.shape[0]):
        delta_ref[pair] = delta[2 * pair : 2 * pair + 2, :]
    add_rows(sums, rows, pl.program_id(0) == 0)


def branch_back(da, h, dy, o, valid, w, vec):
    rows, width = h.shape
    tile = row_tile(rows)
    pairs = width // 128
    strip = pl.BlockSpec((tile, width), lambda i: (i, 0))
    return pl.pallas_call(
        branch_back_kernel,
        grid=(rows // tile,),
        in_specs=[
            strip,
            strip,
            strip,
            strip,
            pl.BlockSpec((tile, 1), lambda i: (i, 0)),
            pl.BlockSpec((width, width), lambda i: (3, 0)),
            pl.BlockSpec(vec.shape, lambda i: (0, 0)),
        ],
        out_specs=[
            strip,
            strip,
            strip,
            pl.BlockSpec((pairs, 2, tile), lambda i: (0, 0, i)),
            pl.BlockSpec((8, width), lambda i: (0, 0)),
        ],
        out_shape=[
            jax.ShapeDtypeStruct((rows, width), wide),
            jax.ShapeDtypeStruct((rows, width), low),
            jax.ShapeDtypeStruct((rows, width), low),
            jax.ShapeDtypeStruct((pairs, 2, rows), wide),
            jax.ShapeDtypeStruct((8, width), wide),
        ],
        compiler_params=params(),
        cost_estimate=cost(11),
        name="branch_backward",
    )(da, h, dy, o, valid, w, vec)


def mlp_rows_kernel(count, steps, place, *refs):
    a_ref, dy_ref, h_ref, o_ref, valid_ref, wo_ref, vec_ref, hb_ref, local_ref = refs[:9]
    up_refs, down_refs = refs[9 : 9 + count], refs[9 + count : 9 + 2 * count]
    out_ref, dh_ref, dt_ref, do_ref, delta_ref, sums = refs[9 + 2 * count : 15 + 2 * count]
    even_grad, odd_grad, ghb, active, inner, up, down, a_turned, dy_turned = refs[
        15 + 2 * count : 24 + 2 * count
    ]
    local_done, piece_done = refs[24 + 2 * count :]
    step = pl.program_id(0)
    seq_index = place[1]
    piece = up_refs[0].shape[1]
    units = count * piece
    share = a_turned.shape[0] // count
    tile = h_ref.shape[0]

    def local_copies():
        return [
            pltpu.make_async_copy(
                local_ref.at[matrix], target.at[pl.ds(0, units), :], local_done.at[matrix]
            )
            for matrix, target in enumerate((up, down))
        ]

    def piece_copies(number):
        copies = []
        for other in range(count):
            start = pl.multiple_of(number * units + (seq_index ^ other) * piece, 16)
            for matrix, (sources, target) in enumerate(((up_refs, up), (down_refs, down))):
                copies.append(
                    pltpu.make_async_copy(
                        sources[other].at[number - 1],
                        target.at[pl.ds(start, piece), :],
                        piece_done.at[number - 1, matrix, other],
                    )
                )
        return copies

    @pl.when(step == 0)
    def _():
        for copy in local_copies():
            copy.start()
        for number in range(1, steps):
            for copy in piece_copies(number):
                copy.start()
        for source, target in ((a_ref, a_turned), (dy_ref, dy_turned)):
            turned = jnp.transpose(source[...])
            for owner in range(count):
                start = pl.multiple_of((seq_index ^ owner) * share, 16)
                target[pl.ds(start, share), :] = turned[owner * share : (owner + 1) * share, :]
        for copy in local_copies():
            copy.wait()

    for number in range(1, steps):

        @pl.when(step == number)
        def _(number=number):
            for copy in piece_copies(number):
                copy.wait()

    @pl.when(step < steps)
    def _():
        here = pl.ds(pl.multiple_of(step * units, 128), units)
        before = rows_by_rows(a_ref[...], up[here, :]) + hb_ref[0]
        grad_active = rows_by_rows(dy_ref[...], down[here, :])
        density = 0.3989422804014327 * jnp.exp(-0.5 * before * before)
        below = 0.5 * (1.0 + lax.erf(before * 0.7071067811865476))
        active_now = (before * below).astype(low)
        inner_now = ((below + before * density) * grad_active).astype(low)
        active[:, here] = active_now
        inner[:, here] = inner_now
        ghb[0] = jnp.sum(inner_now.astype(wide), axis=0, keepdims=True)
        up_grad = rows_by_cols(a_turned[...], inner_now).astype(low)
        down_grad = rows_by_cols(dy_turned[...], active_now).astype(low)
        for other in range(count):
            part = slice(other * share, (other + 1) * share)
            target = odd_grad if other % 2 else even_grad
            target[other // 2, 0, 0] = up_grad[part, :]
            target[other // 2, 0, 1] = down_grad[part, :]

    @pl.when(step >= steps)
    def _():
        rows = pl.ds(pl.multiple_of((step - steps) * tile, 16), tile)
        out = h_ref[...] + rows_by_cols(active[rows, :], down[...]) + vec_ref[7:8, :]
        out_ref[...] = out.astype(low)
        da = rows_by_cols(inner[rows, :], up[...])
        dh, dt, do, delta, row_sums = branch_back_rows(
            da, h_ref[...], dy_ref[rows, :], o_ref[...], valid_ref[...], wo_ref[...], vec_ref
        )
        dh_ref[...] = dh
        dt_ref[...] = dt
        do_ref[...] = do
        for pair in range(delta_ref.shape[0]):
            delta_ref[pair] = delta[2 * pair : 2 * pair + 2, :]
        add_rows(sums, row_sums, step == steps)


def mlp_rows(place, a, dy, h, o, valid, w, vec, local, bias, ups, downs):
    rows, width = a.shape
    steps, count, piece = bias.shape[0], len(ups), ups[0].shape[1]
    share = width // count
    tile = row_tile(rows)
    pairs = width // 128
    hidden = steps * count * piece
    once = dict(pipeline_mode=pl.Buffered(1))
    fixed = lambda a: pl.BlockSpec(a.shape, lambda i, p: (0,) * len(a.shape), **once)
    late = lambda i: jnp.maximum(i - steps, 0)
    early = lambda i: jnp.minimum(i, steps - 1)
    strip = pl.BlockSpec((tile, width), lambda i, p: (late(i), 0))
    units = count * piece
    bias_strip = pl.BlockSpec((1, 1, units), lambda i, p: (p[0] ^ early(i), 0, 0))
    grads = pl.BlockSpec((count // 2, 1, 2, share, units), lambda i, p: (0, early(i), 0, 0, 0))
    return pl.pallas_call(
        functools.partial(mlp_rows_kernel, count, steps),
        grid_spec=pltpu.PrefetchScalarGridSpec(
            num_scalar_prefetch=1,
            grid=(steps + rows // tile,),
            in_specs=[
                fixed(a),
                fixed(dy),
                strip,
                strip,
                pl.BlockSpec((tile, 1), lambda i, p: (late(i), 0)),
                pl.BlockSpec((width, width), lambda i, p: (3, 0), **once),
                fixed(vec),
                bias_strip,
            ]
            + [in_place()] * (1 + 2 * count),
            out_specs=[
                strip,
                strip,
                strip,
                strip,
                pl.BlockSpec((pairs, 2, tile), lambda i, p: (0, 0, late(i))),
                pl.BlockSpec((8, width), lambda i, p: (0, 0)),
                grads,
                grads,
                bias_strip,
            ],
            scratch_shapes=[pltpu.VMEM((rows, hidden), low)] * 2
            + [pltpu.VMEM((hidden, width), low)] * 2
            + [pltpu.VMEM((width, rows), low)] * 2
            + [pltpu.SemaphoreType.DMA((2,)), pltpu.SemaphoreType.DMA((steps - 1, 2, count))],
        ),
        out_shape=[
            jax.ShapeDtypeStruct((rows, width), low),
            jax.ShapeDtypeStruct((rows, width), wide),
            jax.ShapeDtypeStruct((rows, width), low),
            jax.ShapeDtypeStruct((rows, width), low),
            jax.ShapeDtypeStruct((pairs, 2, rows), wide),
            jax.ShapeDtypeStruct((8, width), wide),
        ]
        + [jax.ShapeDtypeStruct((count // 2, steps, 2, share, units), low)] * 2
        + [jax.ShapeDtypeStruct(bias.shape, wide)],
        compiler_params=params(),
        cost_estimate=cost(36),
        name="mlp_both_ways",
    )(place, a, dy, h, o, valid, w, vec, bias, local, *ups, *downs)


def input_back_kernel(dq_ref, dk_ref, dv_ref, w_ref, x_ref, dh_ref, vec_ref, out_ref, sums):
    width = x_ref.shape[1]
    da = rows_by_cols(dq_ref[...], w_ref[0:width, :])
    da += rows_by_cols(dk_ref[...], w_ref[width : 2 * width, :])
    da += rows_by_cols(dv_ref[...], w_ref[2 * width : 3 * width, :])
    unit, scale = norm_parts(x_ref[...].astype(wide))
    grad = dh_ref[...] + norm_back(unit, scale, vec_ref[0:1, :], da)
    out_ref[...] = grad.astype(low)
    rows = [da * unit, da, dq_ref[...].astype(wide), dv_ref[...].astype(wide)]
    add_rows(sums, rows, pl.program_id(0) == 0)


def input_back(dq, dk, dv, w, x, dh, vec):
    rows, width = x.shape
    tile = row_tile(rows)
    strip = pl.BlockSpec((tile, width), lambda i: (i, 0))
    return pl.pallas_call(
        input_back_kernel,
        grid=(rows // tile,),
        in_specs=[
            strip,
            strip,
            strip,
            pl.BlockSpec((3 * width, width), lambda i: (0, 0)),
            strip,
            strip,
            pl.BlockSpec(vec.shape, lambda i: (0, 0)),
        ],
        out_specs=[strip, pl.BlockSpec((8, width), lambda i: (0, 0))],
        out_shape=[
            jax.ShapeDtypeStruct((rows, width), low),
            jax.ShapeDtypeStruct((8, width), wide),
        ],
        compiler_params=params(),
        cost_estimate=cost(10),
        name="input_backward",
    )(dq, dk, dv, w, x, dh, vec)


def renew_kernel(count, parts, turned, place, *refs):
    pieces = refs[:count]
    weight, moment, average = refs[count : count + 3]
    outs = refs[count + 3 : count + 7]
    grads = refs[count + 7]
    block = weight.shape[1]

    @pl.when(pl.program_id(0) == 0)
    def _():
        base = 0
        for start, rows in parts:
            for other, piece in enumerate(pieces):
                first = base + (place[1] ^ other) * rows
                target = pl.ds(pl.multiple_of(first, 16), rows)
                grads[:, target, :] = piece[:, start : start + rows, :]
            base += count * rows
        if turned:
            for matrix in range(grads.shape[0]):
                grads[matrix] = jnp.transpose(grads[matrix])

    here = pl.ds(pl.multiple_of(pl.program_id(0) * block, 16), block)
    results = renew(
        weight[...],
        moment[...],
        average[...],
        grads[:, here, :].astype(wide),
        weight_decay,
        matrix_rate,
    )
    for out, value in zip(outs, results):
        out[...] = value


def renew_pieces(place, pieces, parts, weight, moment, average, turned=False):
    matrices, rows, width = weight.shape
    steps = 4
    block = pl.BlockSpec((matrices, rows // steps, width), lambda i, p: (0, i, 0))
    fixed = pl.BlockSpec(pieces[0].shape, lambda i, p: (0, 0, 0))
    return pl.pallas_call(
        functools.partial(renew_kernel, len(pieces), parts, turned),
        grid_spec=pltpu.PrefetchScalarGridSpec(
            num_scalar_prefetch=1,
            grid=(steps,),
            in_specs=[fixed] * len(pieces) + [block] * 3,
            out_specs=[block] * 4,
            scratch_shapes=[pltpu.VMEM(weight.shape, low)],
        ),
        out_shape=[jax.ShapeDtypeStruct(weight.shape, wide)] * 4,
        compiler_params=params(),
        cost_estimate=cost(10),
        name="renew_matrices",
    )(place, *pieces, weight, moment, average)


def add_low(a, b):
    return (a.astype(wide) + b.astype(wide)).astype(low)


def fold_mlp_kernel(even_ref, other_ref, up_keep, up_send, down_keep, down_send):
    for half in range(4):
        up = add_low(even_ref[half, 0, 0], other_ref[half, 0, 0])
        down = add_low(even_ref[half, 0, 1], other_ref[half, 0, 1])
        (up_send if half % 2 else up_keep)[half // 2, 0] = up
        (down_send if half // 2 else down_keep)[half % 2, 0] = down


def fold_mlp(evens, others):
    halves, steps, matrices, piece, width = evens.shape
    block = pl.BlockSpec((halves, 1, matrices, piece, width), lambda i: (0, i, 0, 0, 0))
    part = pl.BlockSpec((2, 1, piece, width), lambda i: (0, i, 0, 0))
    return pl.pallas_call(
        fold_mlp_kernel,
        grid=(steps,),
        in_specs=[block, block],
        out_specs=[part] * 4,
        out_shape=[jax.ShapeDtypeStruct((2, steps, piece, width), low)] * 4,
        compiler_params=params(),
        cost_estimate=cost(4),
        name="fold_cores",
    )(evens, others)


def fold_chips_kernel(up, up_other, down, down_other, up_keep, up_send, down_keep, down_send):
    up_keep[...] = add_low(up[0], up_other[0])
    up_send[...] = add_low(up[1], up_other[1])
    down_keep[...] = add_low(down[0], down_other[0])
    down_send[...] = add_low(down[1], down_other[1])


def fold_chips(up, up_other, down, down_other):
    _, steps, piece, width = up.shape
    return pl.pallas_call(
        fold_chips_kernel,
        in_specs=[whole_vmem()] * 4,
        out_specs=[whole_vmem()] * 4,
        out_shape=[jax.ShapeDtypeStruct((steps, piece, width), low)] * 4,
        compiler_params=params(),
        cost_estimate=cost(4),
        name="fold_chips",
    )(up, up_other, down, down_other)


def fold_last_kernel(up, up_other, down, down_other, *outs):
    for step, out in enumerate(outs):
        out[0] = add_low(up[step], up_other[step])
        out[1] = add_low(down[step], down_other[step])


def fold_last(up, up_other, down, down_other):
    steps, piece, width = up.shape
    return pl.pallas_call(
        fold_last_kernel,
        in_specs=[whole_vmem()] * 4,
        out_specs=[whole_vmem()] * steps,
        out_shape=[jax.ShapeDtypeStruct((2, piece, width), low)] * steps,
        compiler_params=params(),
        cost_estimate=cost(3),
        name="fold_last",
    )(up, up_other, down, down_other)


def fold_kernel(halves, groups, *refs):
    evens, others, outs = refs[:groups], refs[groups : 2 * groups], refs[2 * groups :]
    for half, out in enumerate(outs):
        at = 0
        for step in range(evens[0].shape[1]):
            for even_ref, other_ref in zip(evens, others):
                rows = pl.ds(at, even_ref.shape[2])
                out[rows, :] = add_low(even_ref[half, step], other_ref[half, step])
                at += even_ref.shape[2]


def fold_pairs(evens, others):
    halves, steps, _, width = evens[0].shape
    rows = steps * sum(array.shape[2] for array in evens)
    return pl.pallas_call(
        functools.partial(fold_kernel, halves, len(evens)),
        in_specs=[whole_vmem()] * (2 * len(evens)),
        out_specs=[whole_vmem()] * halves,
        out_shape=[jax.ShapeDtypeStruct((rows, width), low)] * halves,
        compiler_params=params(),
        cost_estimate=cost(4),
        name="fold_cores",
    )(*evens, *others)


def sum_all(values):
    values = [value.astype(wide) for value in values]
    while len(values) > 1:
        values = [values[i] + values[i + 1] for i in range(0, len(values), 2)]
    return values[0].astype(low)


def sum_steps_kernel(terms, *refs):
    extra, outs = refs[terms : terms + 2], refs[terms + 2 :]
    total = sum_all([ref[...] for ref in refs[:terms]])
    tail = jnp.concatenate([ref[...] for ref in extra], axis=0).astype(low)
    rows = total.shape[0] // len(outs)
    for step, out in enumerate(outs):
        out[pl.ds(0, rows), :] = total[step * rows : (step + 1) * rows]
        out[pl.ds(rows, tail.shape[0]), :] = tail


def sum_steps(terms, steps, *extra):
    rows, width = terms[0].shape
    rows = rows // steps + sum(array.shape[0] for array in extra)
    return pl.pallas_call(
        functools.partial(sum_steps_kernel, len(terms)),
        in_specs=[whole_vmem()] * (len(terms) + 2),
        out_specs=[whole_vmem()] * steps,
        out_shape=[jax.ShapeDtypeStruct((rows, width), low)] * steps,
        compiler_params=params(),
        cost_estimate=cost(2),
        name="sum_steps",
    )(*terms, *extra)


def solution(mesh):
    seqs = mesh.shape["seq"]
    hids = mesh.shape["hid"]

    def swap(value, axis, step):
        count = mesh.shape[axis]
        return lax.ppermute(value, axis, [(i, i ^ step) for i in range(count)])

    def after(value, *others):
        return lax.optimization_barrier((value, others))[0]

    def spread_chips(array):
        return [array] + [swap(array, "seq", other) for other in range(2, seqs, 2)]

    def spread_pairs(evens):
        pieces = []
        for even in evens:
            pieces += [even, swap(even, "seq", 1)]
        return pieces

    def tree_sum(values):
        while len(values) > 1:
            values = [values[i] + values[i + 1] for i in range(0, len(values), 2)]
        return values[0]

    def hid_terms(arrays):
        return [arrays[0]] + [swap(arrays[i], "hid", i) for i in range(1, hids)]

    def seq_terms(arrays):
        return [arrays[0]] + [swap(arrays[i], "seq", 2 * i) for i in range(1, seqs // 2)]

    def exchange(array, packs, rows):
        teams = [[r * packs + b for b in range(packs)] for r in range(seqs // packs)]
        array = array.reshape(packs, rows, array.shape[-1])
        return lax.all_to_all(array, "seq", 0, 0, axis_index_groups=teams)

    def image_parts(image_lengths, packs, rows):
        seq_index = lax.axis_index("seq")
        first = (seq_index // packs) * (packs * rows)
        positions = first + jnp.arange(packs * rows, dtype=jnp.int32)
        lengths = lax.dynamic_index_in_dim(image_lengths, seq_index % packs, 0, keepdims=False)
        ends = jnp.cumsum(lengths)
        query_seg = jnp.sum((ends[None, :] <= positions[:, None]).astype(jnp.int32), axis=1)
        return query_seg, (positions < ends[-1]).astype(wide)[:, None]

    def vector_rows(small):
        return jnp.concatenate([small[:4], small[10:11], small[8:10], small[11:16]], axis=0)

    def shards_general(
        tokens_in,
        image_lengths,
        attn_weight,
        attn_moment,
        attn_average,
        mlp_weight,
        mlp_moment,
        mlp_average,
        vector_params,
        vector_moment,
        vector_average,
        out_grad,
    ):
        packs, rows, width = tokens_in.shape
        share = seqs // packs

        def across_share(array):
            return [array] + [swap(array, "seq", packs * m) for m in range(1, share)]

        place = jnp.stack([lax.axis_index("hid"), lax.axis_index("seq")]).astype(jnp.int32)
        tokens = exchange(tokens_in, packs, rows).reshape(packs * rows, width)
        grad_low = exchange(out_grad, packs, rows).reshape(packs * rows, width)
        query_seg, valid = image_parts(image_lengths, packs, rows)
        key_seg = jnp.concatenate(across_share(query_seg))
        whole_attn = lax.all_gather(attn_weight.astype(low), "hid", axis=0, tiled=True)
        whole_mlp = lax.all_gather(mlp_weight.astype(low), "hid", axis=1, tiled=True)
        whole_attn, first_low, queries, keys, values = project(
            place, tokens, vector_params, [], whole_attn
        )
        keys = jnp.concatenate(across_share(keys))
        values = jnp.concatenate(across_share(values))
        pairs = range(width // 128)
        mixed, log_total = attention_forward(
            queries, keys, values, query_seg[:, None], key_seg[None, :], valid, pairs
        )
        residual, second_low = join(mixed, tokens, whole_attn, vector_params)
        hidden_bias = vector_params[8:].reshape(-1)
        mlp_out, second_grad, up_grad, down_grad, bias_grad = mlp_plain(
            second_low,
            grad_low,
            residual,
            vector_params,
            whole_mlp[0],
            whole_mlp[1],
            hidden_bias,
        )
        block_out = exchange(mlp_out, packs, rows).astype(wide)
        mlp_grad = lax.psum_scatter(
            jnp.stack([up_grad, down_grad]), "hid", scatter_dimension=1, tiled=True
        )
        mlp_grad = lax.psum(mlp_grad, "seq").astype(wide)
        residual_grad, branch_grad, mixed_grad, delta, branch_sums = branch_back(
            second_grad, residual, grad_low, mixed, valid, whole_attn, vector_params
        )
        query_grad, key_grad, value_grad = attention_backward(
            queries,
            keys,
            values,
            mixed_grad,
            log_total,
            delta,
            query_seg[None, :],
            key_seg[:, None],
        )
        count = queries.shape[0]

        def own_share(array):
            terms = [array[:count]]
            for m in range(1, share):
                terms.append(swap(array[m * count : (m + 1) * count], "seq", packs * m))
            return sum_all(terms)

        key_grad = own_share(key_grad)
        value_grad = own_share(value_grad)
        input_grad, input_sums = input_back(
            query_grad, key_grad, value_grad, whole_attn, tokens, residual_grad, vector_params
        )
        input_grad = exchange(input_grad, packs, rows).astype(wide)
        attn_grad = [
            cols_by_cols(query_grad, first_low),
            cols_by_cols(key_grad, first_low),
            cols_by_cols(value_grad, first_low),
            cols_by_cols(branch_grad, mixed),
        ]
        attn_grad = lax.psum_scatter(
            jnp.concatenate(attn_grad).astype(low), "hid", scatter_dimension=0, tiled=True
        )
        attn_grad = lax.psum(attn_grad, "seq").astype(wide)
        small = jnp.concatenate([input_sums, branch_sums[:4], bias_grad.reshape(-1, width)])
        copies = jnp.broadcast_to(small[None], (hids * seqs,) + small.shape)
        small = jnp.sum(lax.all_to_all(copies, ("hid", "seq"), 0, 0), axis=0)
        rates = (weight_decay, matrix_rate)
        return (
            block_out,
            input_grad,
            *renew(attn_weight, attn_moment, attn_average, attn_grad, *rates),
            *renew(mlp_weight, mlp_moment, mlp_average, mlp_grad, *rates),
            *renew(
                vector_params, vector_moment, vector_average, vector_rows(small), 0.0, vector_rate
            ),
        )

    def shards(
        tokens_in,
        image_lengths,
        attn_weight,
        attn_moment,
        attn_average,
        mlp_weight,
        mlp_moment,
        mlp_average,
        vector_params,
        vector_moment,
        vector_average,
        out_grad,
    ):
        packs, rows, width = tokens_in.shape
        seq_index = lax.axis_index("seq")
        hid_index = lax.axis_index("hid")
        place = jnp.stack([hid_index, seq_index]).astype(jnp.int32)
        attn_piece = attn_weight.shape[0] // seqs
        mlp_piece = mlp_weight.shape[1] // seqs
        pairs = range(width // 128)

        def own_row(matrix, piece, other=0):
            start = (seq_index ^ other) * piece
            return lax.dynamic_slice_in_dim(matrix, start, piece, 0).astype(low)

        attn_half = attn_piece // 2
        attn_own = [own_row(attn_weight, attn_piece, other)[:attn_half] for other in (0, 4)]
        attn_own += [own_row(attn_weight, attn_piece, other)[attn_half:] for other in (0, 2)]
        attn_steps = hid_terms([jnp.stack(attn_own)] * hids)[1:]
        tokens = exchange(tokens_in, packs, rows).reshape(packs * rows, width)
        attn_low = attn_weight.astype(low)
        up_own, down_own = [own_row(matrix, mlp_piece) for matrix in mlp_weight]
        attn_steps = after(attn_steps, attn_low, up_own, down_own, tokens)
        first_here = jnp.stack([step[:2] for step in attn_steps])
        last_here = jnp.stack([step[2:] for step in attn_steps])
        attn_chips = [first_here, swap(first_here, "seq", 2), last_here, swap(last_here, "seq", 4)]
        up_here = jnp.stack(hid_terms([after(up_own, first_here)] * hids)[1:])
        query_seg, valid = image_parts(image_lengths, packs, rows)
        mlp_low = mlp_weight.astype(low)
        bias_pieces = vector_params[8:].reshape(hids, 1, seqs * mlp_piece)
        query_seg_rows, key_seg_rows = query_seg[:, None], query_seg[None, :]
        ready = (up_here, mlp_low, bias_pieces, query_seg_rows, key_seg_rows, valid)
        attn_chips = after(attn_chips, *ready)
        pieces = [attn_low] + spread_pairs(attn_chips)
        grad_low = exchange(after(out_grad, *attn_chips), packs, rows)
        grad_low = grad_low.reshape(packs * rows, width)
        up_here = after(up_here, *attn_chips)
        up_x, up_y = swap(up_here, "seq", 2), swap(up_here, "seq", 4)
        down_steps = hid_terms([after(down_own, *attn_chips)] * hids)[1:]

        whole_attn, first_low, queries, keys, values = project(
            place, tokens, vector_params, pieces, None
        )
        down_here = jnp.stack(after(down_steps, queries))
        down_x, down_y = swap(down_here, "seq", 2), swap(down_here, "seq", 4)
        queries = after(queries, down_here)
        attended = (queries, keys, values, query_seg_rows, key_seg_rows, valid)
        half = len(pairs) // 2
        part = attention_forward(*attended, pairs[:half])
        mixed, log_total = attention_forward(*attended, pairs[half:], part)
        up_far = swap(after(up_x, mixed), "seq", 4)
        down_far = swap(after(down_y, mixed), "seq", 2)
        residual, second_low = join(mixed, tokens, whole_attn, vector_params)
        ups = [up_here, up_x, up_y, up_far]
        downs = [down_here, down_x, down_y, down_far]
        ups = after(ups[:3], mixed) + after(ups[3:], second_low)
        downs = after(downs[:3], mixed) + after(downs[3:], second_low)
        mlp_out, residual_grad, branch_grad, mixed_grad, delta, branch_sums, *mlp_grads = mlp_rows(
            place,
            second_low,
            grad_low,
            residual,
            mixed,
            valid,
            whole_attn,
            vector_params,
            mlp_low,
            bias_pieces,
            spread_pairs(ups),
            spread_pairs(downs),
        )
        even_grad, odd_grad, bias_grad = mlp_grads

        other_grad = swap(odd_grad, "seq", 1)
        block_out = exchange(mlp_out, packs, rows)
        early_rows = jnp.concatenate([branch_sums[:4], bias_grad.reshape(-1, width)])
        attended = (queries, keys, values, mixed_grad, log_total, delta)
        attended += (key_seg_rows, query_seg_rows)
        attended += (branch_grad, first_low, mixed)
        *part, first_even, first_odd = attention_grads(place, seqs, *attended, pairs[:half])
        even_grad = after(even_grad, first_even, block_out)
        up_keep, up_send, down_keep, down_send = fold_mlp(even_grad, other_grad)
        up_other = swap(up_send, "seq", 2)
        down_other = swap(down_send, "seq", 4)
        first_other = swap(first_odd, "seq", 1)
        part = after(part, up_keep)
        *part, last_even, last_odd = attention_grads(place, seqs, *attended, pairs[half:], part)
        up_keep, up_send, down_keep, down_send = fold_chips(
            after(up_keep, last_even), up_other, down_keep, down_other
        )
        up_other = swap(up_send, "seq", 4)
        down_other = swap(down_send, "seq", 2)
        last_other = swap(last_odd, "seq", 1)
        attn_folded = fold_pairs(
            after([first_even, last_even], up_keep), [first_other, last_other]
        )
        attn_terms = seq_terms(attn_folded)
        query_grad, key_grad, value_grad = after(part, attn_folded[0])
        input_grad, input_sums = input_back(
            query_grad, key_grad, value_grad, whole_attn, tokens, residual_grad, vector_params
        )
        mlp_added = fold_last(after(up_keep, input_sums), up_other, down_keep, down_other)
        mlp_terms = hid_terms(mlp_added)
        extra = input_sums.shape[0] + early_rows.shape[0]
        attn_terms = after(attn_terms, mlp_added[0])
        attn_added = sum_steps(attn_terms, hids, input_sums, early_rows)
        mlp_sums = sum_all(after(mlp_terms, attn_added[0]))
        mlp_chips = spread_chips(mlp_sums)
        attn_terms = hid_terms(attn_added)
        input_grad = exchange(after(input_grad, mlp_sums), packs, rows)
        attn_sums = sum_all(attn_terms)
        attn_grad = spread_chips(attn_sums)
        mlp_grad = spread_pairs(after(mlp_chips, attn_sums))
        mlp_new = renew_pieces(
            place,
            mlp_grad,
            [(0, width // seqs)],
            mlp_weight,
            mlp_moment,
            mlp_average,
            turned=True,
        )
        attn_grad = spread_pairs(after(attn_grad, mlp_new[0]))
        group_rows = attn_piece // 2
        attn_new = renew_pieces(
            place,
            [piece[None] for piece in attn_grad],
            [(group * group_rows, group_rows) for group in range(2)],
            attn_weight[None],
            attn_moment[None],
            attn_average[None],
        )
        own = slice(attn_piece, attn_piece + extra)
        small = tree_sum([piece[own].astype(wide) for piece in attn_grad])
        return (
            block_out.astype(wide),
            input_grad.astype(wide),
            *[array[0] for array in attn_new],
            *mlp_new,
            *renew(
                vector_params, vector_moment, vector_average, vector_rows(small), 0.0, vector_rate
            ),
        )

    def whole(*arrays):
        pieces = [arrays[2].shape[0] // seqs, arrays[5].shape[1] // seqs]
        fits = seqs == 8 and arrays[0].shape[0] == 8 and all(n % 96 == 0 for n in pieces)
        return (shards if fits else shards_general)(*arrays)

    return jax.shard_map(
        whole,
        mesh=mesh,
        in_specs=(
            P("hid", "seq", None),
            P("hid", None),
            P("hid", None),
            P("hid", None),
            P("hid", None),
            P(None, "hid", None),
            P(None, "hid", None),
            P(None, "hid", None),
            P(),
            P(),
            P(),
            P("hid", "seq", None),
        ),
        out_specs=(
            P("hid", "seq", None),
            P("hid", "seq", None),
            P("hid", None),
            P("hid", None),
            P("hid", None),
            P("hid", None),
            P(None, "hid", None),
            P(None, "hid", None),
            P(None, "hid", None),
            P(None, "hid", None),
            P(),
            P(),
            P(),
            P(),
        ),
        check_vma=False,
    )
```

profile of v0, /device:TPU:9, one launch (start us, length us, event | category | flops | bytes accessed | tf_op | source)
XLA Modules:
  0.0 352.1 jit_solution(12134653334409503212)
XLA Ops:
  0.7 5.0 %all-to-all-start = ((bf16[8,128,768]{2,1,0:T(8,128)(2,1)}), bf16[8,128,768]{2,1,0:T(8,128)(2,1)}, u32[]{:S(2)}, u32[]{:S(2)}) async-start(bf16[8,128,768]{2,1,0:T(8,128)(2,1)} %param.12), calls=%async_computation | async-start | bytes 3145728 | tf_op jit(solution)/shard_map/all_to_all | solution.py:968
  5.8 1.4 collective-permute-start.2
  10.8 2.6 fusion.6
  14.1 12.8 %collective-permute-done.2 = bf16[4,48,768]{2,1,0:T(8,128)(2,1)S(1)} collective-permute-done((bf16[4,48,768]{2,1,0:T(8,128)(2,1)S(1)}, bf16[4,48,768]{2,1,0:T(8,128)(2,1)S(1)}, u32[]{:S(2)}, u32[]{:S(2)}) %collective-permute-start.2) | collective-permute-done | bytes 294944 | tf_op jit(solution)/shard_map/ppermute | solution.py:940
  26.9 5.4 %collective-permute-done.1 = bf16[4,48,768]{2,1,0:T(8,128)(2,1)S(1)} collective-permute-done((bf16[4,48,768]{2,1,0:T(8,128)(2,1)S(1)}, bf16[4,48,768]{2,1,0:T(8,128)(2,1)S(1)}, u32[]{:S(2)}, u32[]{:S(2)}) %collective-permute-start.1) | collective-permute-done | bytes 294944 | tf_op jit(solution)/shard_map/ppermute | solution.py:940
  35.3 4.0 %collective-permute-start.6 = (bf16[96,768]{1,0:T(8,128)(2,1)S(1)}, bf16[96,768]{1,0:T(8,128)(2,1)S(1)}, u32[]{:S(2)}, u32[]{:S(2)}) collective-permute-start(bf16[96,768]{1,0:T(8,128)(2,1)S(1)} %get-tuple-element.130), channel_id=1, source_target_pairs={{0,2},{1,3},{2,0},{3,1},{4,6},{5,7},{6,4},{7,5},{8,10},{9,11},{10,... | collective-permute-start | bytes 442376 | tf_op jit(solution)/shard_map/ppermute | solution.py:940
  40.0 4.0 %convert_element_type.109.refs_8_ = bf16[2,768,768]{2,1,0:T(8,128)(2,1)} convert(f32[2,768,768]{2,1,0:T(8,128)} %refs_8_.1) | non-fusion elementwise | flops 1179648 | bytes 7077888 | tf_op jit(solution)/shard_map/convert_element_type | solution.py:1124
  44.6 1.5 fusion.valid_ref.refs_4_
  46.1 2.9 collective-permute-done.6
  49.1 1.6 collective-permute-start.8
  52.9 4.2 %all-to-all-start.1 = ((bf16[8,128,768]{2,1,0:T(8,128)(2,1)}), bf16[8,128,768]{2,1,0:T(8,128)(2,1)S(1)}, u32[]{:S(2)}, u32[]{:S(2)}) async-start(bf16[8,128,768]{2,1,0:T(8,128)(2,1)} %param.23), calls=%async_computation.1 | async-start | bytes 3145728 | tf_op jit(solution)/shard_map/all_to_all | solution.py:968
  57.5 4.0 %collective-permute-start.13 = (bf16[96,768]{1,0:T(8,128)(2,1)S(1)}, bf16[96,768]{1,0:T(8,128)(2,1)S(1)}, u32[]{:S(2)}, u32[]{:S(2)}) collective-permute-start(bf16[96,768]{1,0:T(8,128)(2,1)S(1)} %copy-done.11), channel_id=1, source_target_pairs={{0,2},{1,3},{2,0},{3,1},{4,6},{5,7},{6,4},{7,5},{8,10},{9,11},{10,... | collective-permute-start | bytes 442376 | tf_op jit(solution)/shard_map/ppermute | solution.py:940
  61.5 1.5 collective-permute-start.16
  64.2 10.2 %norm_and_project.1 = (bf16[3072,768]{1,0:T(8,128)(2,1)}, bf16[1024,768]{1,0:T(8,128)(2,1)}, bf16[1024,768]{1,0:T(8,128)(2,1)}, bf16[1024,768]{1,0:T(8,128)(2,1)}, bf16[1024,768]{1,0:T(8,128)(2,1)}) custom-call(s32[2]{0:T(128)} %pad_add_fusion.place, bf16[1024,768]{1,0:T(8,128)(2,1)} %bitcast.2.x_ref, f32[12,768]{1,0:T(8,128)} %vec_ref.5, ...), custom_call_target="tpu_custom_call" | custom-call | flops 4000001024 | bytes 1000 | tf_op jit(solution)/shard_map/norm_and_project/pallas_call | solution.py:444
  74.8 11.6 %attention_forward.2 = (bf16[1024,768]{1,0:T(8,128)(2,1)}, f32[6,2,1024]{2,1,0:T(2,128)}) custom-call(bf16[1024,768]{1,0:T(8,128)(2,1)} %get-tuple-element.140.q_ref.refs_0_, bf16[1024,768]{1,0:T(8,128)(2,1)} %get-tuple-element.141.k_ref.refs_1_, bf16[1024,768]{1,0:T(8,128)(2,1)} %get-tuple-element.142.v_ref.refs_2_, s32[1024,1]{1,0:T(8,128)} %copy.39.query_seg.refs_7_, ...), custom_call_target="tpu_custom_call" | custom-call | flops 4800001024 | bytes 1000 | tf_op jit(solution)/shard_map/attention_forward/pallas_call | solution.py:106
  86.5 11.6 %attention_forward.3 = (bf16[1024,768]{1,0:T(8,128)(2,1)}, f32[6,2,1024]{2,1,0:T(2,128)}) custom-call(bf16[1024,768]{1,0:T(8,128)(2,1)} %get-tuple-element.140.q_ref.refs_0_, bf16[1024,768]{1,0:T(8,128)(2,1)} %get-tuple-element.141.k_ref.refs_1_, bf16[1024,768]{1,0:T(8,128)(2,1)} %get-tuple-element.142.v_ref.refs_2_, ...), custom_call_target="tpu_custom_call", output_to_operand_aliasing={{0}: (6, {}), {1}: (7, {})} | custom-call | flops 4800001024 | bytes 1000 | tf_op jit(solution)/shard_map/attention_forward/pallas_call | solution.py:106
  98.1 1.4 collective-permute-start.20
  100.8 2.7 collective-permute-start.17
  103.9 5.9 %join_and_norm.1 = (f32[1024,768]{1,0:T(8,128)}, bf16[1024,768]{1,0:T(8,128)(2,1)}) custom-call(bf16[1024,768]{1,0:T(8,128)(2,1)} %get-tuple-element.145.o_ref.refs_3_.refs_10_, bf16[1024,768]{1,0:T(8,128)(2,1)} %bitcast.2.x_ref, bf16[3072,768]{1,0:T(8,128)(2,1)} %get-tuple-element.146.w_ref.refs_5_, f32[12,768]{1,0:T(8,128)} %vec_ref.5), custom_call_target="tpu_custom_call" | custom-call | flops 2400001024 | bytes 1000 | tf_op jit(solution)/shard_map/join_and_norm/pallas_call | solution.py:471
  110.8 1.5 collective-permute-start.25
  117.0 45.6 %mlp_both_ways.1 = (bf16[1024,768]{1,0:T(8,128)(2,1)}, f32[1024,768]{1,0:T(8,128)}, bf16[1024,768]{1,0:T(8,128)(2,1)}, bf16[1024,768]{1,0:T(8,128)(2,1)}, f32[6,...) custom-call(s32[2]{0:T(128)} %pad_add_fusion.place, ...), custom_call_target="tpu_custom_call" | custom-call | flops 14400001024 | bytes 1000 | tf_op jit(solution)/shard_map/mlp_both_ways/pallas_call | solution.py:670
  163.0 4.1 %all-to-all-start.2 = ((bf16[8,128,768]{2,1,0:T(8,128)(2,1)}), bf16[8,128,768]{2,1,0:T(8,128)(2,1)S(1)}, u32[]{:S(2)}, u32[]{:S(2)}) async-start(bf16[8,128,768]{2,1,0:T(8,128)(2,1)} %bitcast.62), calls=%async_computation.2 | async-start | bytes 3145728 | tf_op jit(solution)/shard_map/all_to_all | solution.py:968
  167.1 24.5 %attention_backward.2 = (bf16[1024,768]{1,0:T(8,128)(2,1)}, bf16[1024,768]{1,0:T(8,128)(2,1)}, bf16[1024,768]{1,0:T(8,128)(2,1)}, bf16[4,4,48,768]{3,2,1,0:T(8,128)(2,1)}, bf16[4,4,48,768]{3,2,1,0:T(8,128)(2,1)}) custom-call(s32[2]{0:T(128)} %pad_add_fusion.place, bf16[1024,768]{1,0:T(8,128)(2,1)} %get-tuple-element.140.q_ref.refs_0_, ...), custom_call_target="tpu_custom_call" | custom-call | flops 8400001024 | bytes 1000 | tf_op jit(solution)/shard_map/attention_backward/pallas_call | solution.py:252
  191.7 6.5 %fold_cores.2 = (bf16[2,4,96,768]{3,2,1,0:T(8,128)(2,1)}, bf16[2,4,96,768]{3,2,1,0:T(8,128)(2,1)}, bf16[2,4,96,768]{3,2,1,0:T(8,128)(2,1)}, bf16[2,4,96,768]{3,2,1,0:T(8,128)(2,1)}) custom-call(bf16[4,4,2,96,768]{4,3,2,1,0:T(8,128)(2,1)} %get-tuple-element.172.even_ref, bf16[4,4,2,96,768]{4,3,2,1,0:T(8,128)(2,1)} %collective-permute-done.29.other_ref), custom_call_target="tpu_custom_call" | custom-call | flops 1600001024 | bytes 1000 | tf_op jit(solution)/shard_map/fold_cores/pallas_call | solution.py:827
  198.3 1.6 collective-permute-start.30
  201.2 24.6 %attention_backward.3 = (bf16[1024,768]{1,0:T(8,128)(2,1)}, bf16[1024,768]{1,0:T(8,128)(2,1)}, bf16[1024,768]{1,0:T(8,128)(2,1)}, bf16[4,4,48,768]{3,2,1,0:T(8,128)(2,1)}, bf16[4,4,48,768]{3,2,1,0:T(8,128)(2,1)}) custom-call(s32[2]{0:T(128)} %pad_add_fusion.place, ...), custom_call_target="tpu_custom_call", output_to_operand_aliasing={{0}: (12, {}), {1}: (13, {}), {2}: (14, {})} | custom-call | flops 8400001024 | bytes 1000 | tf_op jit(solution)/shard_map/attention_backward/pallas_call | solution.py:252
  228.2 3.9 %fold_chips.1 = (bf16[4,96,768]{2,1,0:T(8,128)(2,1)}, bf16[4,96,768]{2,1,0:T(8,128)(2,1)}, bf16[4,96,768]{2,1,0:T(8,128)(2,1)}, bf16[4,96,768]{2,1,0:T(8,128)(2,1)}) custom-call(bf16[2,4,96,768]{3,2,1,0:T(8,128)(2,1)} %get-tuple-element.182.up, bf16[2,4,96,768]{3,2,1,0:T(8,128)(2,1)} %copy-done.25, bf16[2,4,96,768]{3,2,1,0:T(8,128)(2,1)} %get-tuple-element.184.down, ...), custom_call_target="tpu_custom_call" | custom-call | flops 1600001024 | bytes 1000 | tf_op jit(solution)/shard_map/fold_chips/pallas_call | solution.py:848
  236.1 3.9 %fold_cores.3 = (bf16[384,768]{1,0:T(8,128)(2,1)}, bf16[384,768]{1,0:T(8,128)(2,1)}, bf16[384,768]{1,0:T(8,128)(2,1)}, bf16[384,768]{1,0:T(8,128)(2,1)}) custom-call(bf16[4,4,48,768]{3,2,1,0:T(8,128)(2,1)} %get-tuple-element.187.refs_0_, bf16[4,4,48,768]{3,2,1,0:T(8,128)(2,1)} %get-tuple-element.188.refs_1_, bf16[4,4,48,768]{3,2,1,0:T(8,128)(2,1)} %copy-done.24, ...), custom_call_target="tpu_custom_call" | custom-call | flops 1600001024 | bytes 1000 | tf_op jit(solution)/shard_map/fold_cores/pallas_call | solution.py:892
  240.9 1.7 collective-permute-start.41
  242.6 10.2 %input_backward.1 = (bf16[1024,768]{1,0:T(8,128)(2,1)}, f32[8,768]{1,0:T(8,128)}) custom-call(bf16[1024,768]{1,0:T(8,128)(2,1)} %get-tuple-element.192.dq_ref, bf16[1024,768]{1,0:T(8,128)(2,1)} %get-tuple-element.193.dk_ref, bf16[1024,768]{1,0:T(8,128)(2,1)} %get-tuple-element.194.dv_ref, bf16[3072,768]{1,0:T(8,128)(2,1)} %get-tuple-element.146.w_ref.refs_5_, ...), custom_call_target="tpu_custom_call" | custom-call | flops 4000001024 | bytes 1000 | tf_op jit(solution)/shard_map/input_backward/pallas_call | solution.py:734
  253.8 2.7 fold_last.1
  256.5 1.4 collective-permute-start.36
  258.0 1.5 collective-permute-done.39.refs_1_
  260.4 11.5 %collective-permute-done.41.refs_3_ = bf16[384,768]{1,0:T(8,128)(2,1)S(1)} collective-permute-done((bf16[384,768]{1,0:T(8,128)(2,1)}, bf16[384,768]{1,0:T(8,128)(2,1)S(1)}, u32[]{:S(2)}, u32[]{:S(2)}) %collective-permute-start.41) | collective-permute-done | bytes 589856 | tf_op jit(solution)/shard_map/ppermute | solution.py:940
  272.8 2.5 sum_steps.1
  275.3 1.4 collective-permute-start.42
  278.0 12.6 %collective-permute-done.38 = bf16[2,96,768]{2,1,0:T(8,128)(2,1)S(1)} collective-permute-done((bf16[2,96,768]{2,1,0:T(8,128)(2,1)}, bf16[2,96,768]{2,1,0:T(8,128)(2,1)S(1)}, u32[]{:S(2)}, u32[]{:S(2)}) %collective-permute-start.38) | collective-permute-done | bytes 294944 | tf_op jit(solution)/shard_map/ppermute | solution.py:940
  290.9 1.9 collective-permute-start.49
  293.5 4.2 %collective-permute-done.44 = bf16[112,768]{1,0:T(8,128)(2,1)S(1)} collective-permute-done((bf16[112,768]{1,0:T(8,128)(2,1)}, bf16[112,768]{1,0:T(8,128)(2,1)S(1)}, u32[]{:S(2)}, u32[]{:S(2)}) %collective-permute-start.44) | collective-permute-done | bytes 172064 | tf_op jit(solution)/shard_map/ppermute | solution.py:940
  298.5 1.9 collective-permute-done.49.refs_4_
  300.4 7.2 %collective-permute-start.51 = (bf16[2,96,768]{2,1,0:T(8,128)(2,1)S(1)}, bf16[2,96,768]{2,1,0:T(8,128)(2,1)}, u32[]{:S(2)}, u32[]{:S(2)}) collective-permute-start(bf16[2,96,768]{2,1,0:T(8,128)(2,1)S(1)} %add_convert_fusion.refs_0_), channel_id=1, source_target_pairs={{0,4},{4,0},{8,12},{12,8},{16,20},{20,16},{24,28},{28,24},{1,5},{5... | collective-permute-start | bytes 884744 | tf_op jit(solution)/shard_map/ppermute | solution.py:940
  309.0 4.3 %all-to-all-start.3 = ((bf16[8,128,768]{2,1,0:T(8,128)(2,1)}), bf16[8,128,768]{2,1,0:T(8,128)(2,1)S(1)}, u32[]{:S(2)}, u32[]{:S(2)}) async-start(bf16[8,128,768]{2,1,0:T(8,128)(2,1)} %bitcast.60), calls=%async_computation.3 | async-start | bytes 3145728 | tf_op jit(solution)/shard_map/all_to_all | solution.py:968
  313.3 1.4 collective-permute-start.46
  315.9 14.2 %renew_matrices.2 = (f32[2,768,768]{2,1,0:T(8,128)}, f32[2,768,768]{2,1,0:T(8,128)}, f32[2,768,768]{2,1,0:T(8,128)}, f32[2,768,768]{2,1,0:T(8,128)}) custom-call(s32[2]{0:T(128)} %pad_add_fusion.place, bf16[2,96,768]{2,1,0:T(8,128)(2,1)} %copy-done.4, bf16[2,96,768]{2,1,0:T(8,128)(2,1)} %collective-permute-done.51.refs_1_, ...), custom_call_target="tpu_custom_call" | custom-call | flops 4000001024 | bytes 1000 | tf_op jit(solution)/shard_map/renew_matrices/pallas_call | solution.py:795
  330.1 6.1 %collective-permute-done.46 = bf16[112,768]{1,0:T(8,128)(2,1)S(1)} collective-permute-done((bf16[112,768]{1,0:T(8,128)(2,1)}, bf16[112,768]{1,0:T(8,128)(2,1)S(1)}, u32[]{:S(2)}, u32[]{:S(2)}) %collective-permute-start.46) | collective-permute-done | bytes 172064 | tf_op jit(solution)/shard_map/ppermute | solution.py:940
  337.8 1.9 convert_element_type.112
  341.5 8.4 %renew_matrices.3 = (f32[1,768,768]{2,1,0:T(8,128)}, f32[1,768,768]{2,1,0:T(8,128)}, f32[1,768,768]{2,1,0:T(8,128)}, f32[1,768,768]{2,1,0:T(8,128)}) custom-call(s32[2]{0:T(128)} %pad_add_fusion.place, bf16[1,112,768]{2,1,0:T(8,128)(2,1)} %bitcast.28.refs_0_, bf16[1,112,768]{2,1,0:T(8,128)(2,1)} %bitcast.77, bf16[1,112,768]{2,1,0:T(8,128)(2,1)} %bitcast.76, ...), custom_call_target="tpu_custom_call" | custom-call | flops 4000001024 | bytes 1000 | tf_op jit(solution)/shard_map/renew_matrices/pallas_call | solution.py:795
  349.9 1.9 convert_element_type.118
  (227 shorter events, 41.0 us)
Async XLA Ops:
  0.7 31.7 %all-to-all-start = ((bf16[8,128,768]{2,1,0:T(8,128)(2,1)}), bf16[8,128,768]{2,1,0:T(8,128)(2,1)}, u32[]{:S(2)}, u32[]{:S(2)}) async-start(bf16[8,128,768]{2,1,0:T(8,128)(2,1)} %param.12), calls=%async_computation | async-start | bytes 3145728 | tf_op jit(solution)/shard_map/all_to_all | solution.py:968
  5.8 21.2 %collective-permute-start.2 = (bf16[4,48,768]{2,1,0:T(8,128)(2,1)S(1)}, bf16[4,48,768]{2,1,0:T(8,128)(2,1)S(1)}, u32[]{:S(2)}, u32[]{:S(2)}) collective-permute-start(bf16[4,48,768]{2,1,0:T(8,128)(2,1)S(1)} %pad_maximum_fusion.4), channel_id=1, source_target_pairs={{0,3},{1,2},{2,1},{3,0},{4,7},{5,6},{6,5},{7,4},{8,11},{9,10},{10,... | collective-permute-start | bytes 884744 | tf_op jit(solution)/shard_map/ppermute | solution.py:940
  7.1 25.2 %collective-permute-start.1 = (bf16[4,48,768]{2,1,0:T(8,128)(2,1)S(1)}, bf16[4,48,768]{2,1,0:T(8,128)(2,1)S(1)}, u32[]{:S(2)}, u32[]{:S(2)}) collective-permute-start(bf16[4,48,768]{2,1,0:T(8,128)(2,1)S(1)} %pad_maximum_fusion.4), channel_id=1, source_target_pairs={{0,2},{1,3},{2,0},{3,1},{4,6},{5,7},{6,4},{7,5},{8,10},{9,11},{10,... | collective-permute-start | bytes 884744 | tf_op jit(solution)/shard_map/ppermute | solution.py:940
  8.2 24.1 %collective-permute-start = (bf16[4,48,768]{2,1,0:T(8,128)(2,1)S(1)}, bf16[4,48,768]{2,1,0:T(8,128)(2,1)S(1)}, u32[]{:S(2)}, u32[]{:S(2)}) collective-permute-start(bf16[4,48,768]{2,1,0:T(8,128)(2,1)S(1)} %pad_maximum_fusion.4), channel_id=1, source_target_pairs={{0,1},{1,0},{2,3},{3,2},{4,5},{5,4},{6,7},{7,6},{8,9},{9,8},{10,11... | collective-permute-start | bytes 884744 | tf_op jit(solution)/shard_map/ppermute | solution.py:940
  32.5 16.6 %collective-permute-start.3 = (bf16[3,2,48,768]{3,2,1,0:T(8,128)(2,1)S(1)}, bf16[3,2,48,768]{3,2,1,0:T(8,128)(2,1)}, u32[]{:S(2)}, u32[]{:S(2)}) collective-permute-start(bf16[3,2,48,768]{3,2,1,0:T(8,128)(2,1)S(1)} %pad_maximum_fusion.refs_1_), channel_id=1, source_target_pairs={{0,8},{4,12},{8,0},{12,4},{16,24},{20,28},{24,16},{28,20},{1,9},{5... | collective-permute-start | bytes 1327112 | tf_op jit(solution)/shard_map/ppermute | solution.py:940
  33.8 15.3 %collective-permute-start.4 = (bf16[3,2,48,768]{3,2,1,0:T(8,128)(2,1)S(1)}, bf16[3,2,48,768]{3,2,1,0:T(8,128)(2,1)}, u32[]{:S(2)}, u32[]{:S(2)}) collective-permute-start(bf16[3,2,48,768]{3,2,1,0:T(8,128)(2,1)S(1)} %pad_maximum_fusion.1.refs_5_), channel_id=1, source_target_pairs={{0,16},{4,20},{8,24},{12,28},{16,0},{20,4},{24,8},{28,12},{1,17},{... | collective-permute-start | bytes 1327112 | tf_op jit(solution)/shard_map/ppermute | solution.py:940
  35.1 11.0 %collective-permute-start.7 = (bf16[96,768]{1,0:T(8,128)(2,1)S(1)}, bf16[96,768]{1,0:T(8,128)(2,1)S(1)}, u32[]{:S(2)}, u32[]{:S(2)}) collective-permute-start(bf16[96,768]{1,0:T(8,128)(2,1)S(1)} %get-tuple-element.130), channel_id=1, source_target_pairs={{0,3},{1,2},{2,1},{3,0},{4,7},{5,6},{6,5},{7,4},{8,11},{9,10},{10,... | collective-permute-start | bytes 442376 | tf_op jit(solution)/shard_map/ppermute | solution.py:940
  35.3 13.8 %collective-permute-start.6 = (bf16[96,768]{1,0:T(8,128)(2,1)S(1)}, bf16[96,768]{1,0:T(8,128)(2,1)S(1)}, u32[]{:S(2)}, u32[]{:S(2)}) collective-permute-start(bf16[96,768]{1,0:T(8,128)(2,1)S(1)} %get-tuple-element.130), channel_id=1, source_target_pairs={{0,2},{1,3},{2,0},{3,1},{4,6},{5,7},{6,4},{7,5},{8,10},{9,11},{10,... | collective-permute-start | bytes 442376 | tf_op jit(solution)/shard_map/ppermute | solution.py:940
  39.3 9.8 %collective-permute-start.5 = (bf16[96,768]{1,0:T(8,128)(2,1)S(1)}, bf16[96,768]{1,0:T(8,128)(2,1)S(1)}, u32[]{:S(2)}, u32[]{:S(2)}) collective-permute-start(bf16[96,768]{1,0:T(8,128)(2,1)S(1)} %get-tuple-element.130), channel_id=1, source_target_pairs={{0,1},{1,0},{2,3},{3,2},{4,5},{5,4},{6,7},{7,6},{8,9},{9,8},{10,11... | collective-permute-start | bytes 442376 | tf_op jit(solution)/shard_map/ppermute | solution.py:940
  49.1 8.3 %collective-permute-start.8 = (bf16[3,2,48,768]{3,2,1,0:T(8,128)(2,1)S(1)}, bf16[3,2,48,768]{3,2,1,0:T(8,128)(2,1)S(1)}, u32[]{:S(2)}, u32[]{:S(2)}) collective-permute-start(bf16[3,2,48,768]{3,2,1,0:T(8,128)(2,1)S(1)} %pad_maximum_fusion.refs_1_), channel_id=1, source_target_pairs={{0,4},{4,0},{8,12},{12,8},{16,20},{20,16},{24,28},{28,24},{1,5},{5... | collective-permute-start | bytes 1327112 | tf_op jit(solution)/shard_map/ppermute | solution.py:940
  50.7 10.8 %collective-permute-start.9 = (bf16[3,2,48,768]{3,2,1,0:T(8,128)(2,1)}, bf16[3,2,48,768]{3,2,1,0:T(8,128)(2,1)}, u32[]{:S(2)}, u32[]{:S(2)}) collective-permute-start(bf16[3,2,48,768]{3,2,1,0:T(8,128)(2,1)} %collective-permute-done.3.refs_3_), channel_id=1, source_target_pairs={{0,4},{4,0},{8,12},{12,8},{16,20},{20,16},{24,28},{28,24},{1,5},{5... | collective-permute-start | bytes 1327112 | tf_op jit(solution)/shard_map/ppermute | solution.py:940
  50.8 10.7 %collective-permute-start.10 = (bf16[3,2,48,768]{3,2,1,0:T(8,128)(2,1)S(1)}, bf16[3,2,48,768]{3,2,1,0:T(8,128)(2,1)}, u32[]{:S(2)}, u32[]{:S(2)}) collective-permute-start(bf16[3,2,48,768]{3,2,1,0:T(8,128)(2,1)S(1)} %pad_maximum_fusion.1.refs_5_), channel_id=1, source_target_pairs={{0,4},{4,0},{8,12},{12,8},{16,20},{20,16},{24,28},{28,24},{1,5},{5... | collective-permute-start | bytes 1327112 | tf_op jit(solution)/shard_map/ppermute | solution.py:940
  51.2 11.7 %collective-permute-start.11 = (bf16[3,2,48,768]{3,2,1,0:T(8,128)(2,1)}, bf16[3,2,48,768]{3,2,1,0:T(8,128)(2,1)}, u32[]{:S(2)}, u32[]{:S(2)}) collective-permute-start(bf16[3,2,48,768]{3,2,1,0:T(8,128)(2,1)} %collective-permute-done.4.refs_7_), channel_id=1, source_target_pairs={{0,4},{4,0},{8,12},{12,8},{16,20},{20,16},{24,28},{28,24},{1,5},{5... | collective-permute-start | bytes 1327112 | tf_op jit(solution)/shard_map/ppermute | solution.py:940
  52.9 62.6 %all-to-all-start.1 = ((bf16[8,128,768]{2,1,0:T(8,128)(2,1)}), bf16[8,128,768]{2,1,0:T(8,128)(2,1)S(1)}, u32[]{:S(2)}, u32[]{:S(2)}) async-start(bf16[8,128,768]{2,1,0:T(8,128)(2,1)} %param.23), calls=%async_computation.1 | async-start | bytes 3145728 | tf_op jit(solution)/shard_map/all_to_all | solution.py:968
  57.2 17.1 %collective-permute-start.14 = (bf16[96,768]{1,0:T(8,128)(2,1)S(1)}, bf16[96,768]{1,0:T(8,128)(2,1)S(1)}, u32[]{:S(2)}, u32[]{:S(2)}) collective-permute-start(bf16[96,768]{1,0:T(8,128)(2,1)S(1)} %copy-done.11), channel_id=1, source_target_pairs={{0,3},{1,2},{2,1},{3,0},{4,7},{5,6},{6,5},{7,4},{8,11},{9,10},{10,... | collective-permute-start | bytes 442376 | tf_op jit(solution)/shard_map/ppermute | solution.py:940
  57.5 16.8 %collective-permute-start.13 = (bf16[96,768]{1,0:T(8,128)(2,1)S(1)}, bf16[96,768]{1,0:T(8,128)(2,1)S(1)}, u32[]{:S(2)}, u32[]{:S(2)}) collective-permute-start(bf16[96,768]{1,0:T(8,128)(2,1)S(1)} %copy-done.11), channel_id=1, source_target_pairs={{0,2},{1,3},{2,0},{3,1},{4,6},{5,7},{6,4},{7,5},{8,10},{9,11},{10,... | collective-permute-start | bytes 442376 | tf_op jit(solution)/shard_map/ppermute | solution.py:940
  61.5 12.9 %collective-permute-start.12 = (bf16[96,768]{1,0:T(8,128)(2,1)S(1)}, bf16[96,768]{1,0:T(8,128)(2,1)S(1)}, u32[]{:S(2)}, u32[]{:S(2)}) collective-permute-start(bf16[96,768]{1,0:T(8,128)(2,1)S(1)} %copy-done.11), channel_id=1, source_target_pairs={{0,1},{1,0},{2,3},{3,2},{4,5},{5,4},{6,7},{7,6},{8,9},{9,8},{10,11... | collective-permute-start | bytes 442376 | tf_op jit(solution)/shard_map/ppermute | solution.py:940
  61.5 39.3 %collective-permute-start.16 = (bf16[3,96,768]{2,1,0:T(8,128)(2,1)S(1)}, bf16[3,96,768]{2,1,0:T(8,128)(2,1)S(1)}, u32[]{:S(2)}, u32[]{:S(2)}) collective-permute-start(bf16[3,96,768]{2,1,0:T(8,128)(2,1)S(1)} %pad_maximum_fusion.2.refs_9_), channel_id=1, source_target_pairs={{0,16},{4,20},{8,24},{12,28},{16,0},{20,4},{24,8},{28,12},{1,17},{... | collective-permute-start | bytes 1327112 | tf_op jit(solution)/shard_map/ppermute | solution.py:940
  63.0 35.1 %collective-permute-start.15 = (bf16[3,96,768]{2,1,0:T(8,128)(2,1)S(1)}, bf16[3,96,768]{2,1,0:T(8,128)(2,1)S(1)}, u32[]{:S(2)}, u32[]{:S(2)}) collective-permute-start(bf16[3,96,768]{2,1,0:T(8,128)(2,1)S(1)} %pad_maximum_fusion.2.refs_9_), channel_id=1, source_target_pairs={{0,8},{4,12},{8,0},{12,4},{16,24},{20,28},{24,16},{28,20},{1,9},{5... | collective-permute-start | bytes 1327112 | tf_op jit(solution)/shard_map/ppermute | solution.py:940
  74.4 25.1 %collective-permute-start.23 = (bf16[3,96,768]{2,1,0:T(8,128)(2,1)S(1)}, bf16[3,96,768]{2,1,0:T(8,128)(2,1)S(1)}, u32[]{:S(2)}, u32[]{:S(2)}) collective-permute-start(bf16[3,96,768]{2,1,0:T(8,128)(2,1)S(1)} %pad_maximum_fusion.3.refs_17_), channel_id=1, source_target_pairs={{0,16},{4,20},{8,24},{12,28},{16,0},{20,4},{24,8},{28,12},{1,17},{... | collective-permute-start | bytes 1327112 | tf_op jit(solution)/shard_map/ppermute | solution.py:940
  74.7 28.8 %collective-permute-start.22 = (bf16[3,96,768]{2,1,0:T(8,128)(2,1)S(1)}, bf16[3,96,768]{2,1,0:T(8,128)(2,1)S(1)}, u32[]{:S(2)}, u32[]{:S(2)}) collective-permute-start(bf16[3,96,768]{2,1,0:T(8,128)(2,1)S(1)} %pad_maximum_fusion.3.refs_17_), channel_id=1, source_target_pairs={{0,8},{4,12},{8,0},{12,4},{16,24},{20,28},{24,16},{28,20},{1,9},{5... | collective-permute-start | bytes 1327112 | tf_op jit(solution)/shard_map/ppermute | solution.py:940
  98.1 11.8 %collective-permute-start.20 = (bf16[3,96,768]{2,1,0:T(8,128)(2,1)S(1)}, bf16[3,96,768]{2,1,0:T(8,128)(2,1)S(1)}, u32[]{:S(2)}, u32[]{:S(2)}) collective-permute-start(bf16[3,96,768]{2,1,0:T(8,128)(2,1)S(1)} %collective-permute-done.15.refs_11_), channel_id=1, source_target_pairs={{0,16},{4,20},{8,24},{12,28},{16,0},{20,4},{24,8},{28,12},{1,17},{... | collective-permute-start | bytes 1327112 | tf_op jit(solution)/shard_map/ppermute | solution.py:940
  99.6 11.2 %collective-permute-start.27 = (bf16[3,96,768]{2,1,0:T(8,128)(2,1)S(1)}, bf16[3,96,768]{2,1,0:T(8,128)(2,1)}, u32[]{:S(2)}, u32[]{:S(2)}) collective-permute-start(bf16[3,96,768]{2,1,0:T(8,128)(2,1)S(1)} %collective-permute-done.23.refs_21_), channel_id=1, source_target_pairs={{0,8},{4,12},{8,0},{12,4},{16,24},{20,28},{24,16},{28,20},{1,9},{5... | collective-permute-start | bytes 1327112 | tf_op jit(solution)/shard_map/ppermute | solution.py:940
  100.8 11.5 %collective-permute-start.17 = (bf16[3,96,768]{2,1,0:T(8,128)(2,1)S(1)}, bf16[3,96,768]{2,1,0:T(8,128)(2,1)S(1)}, u32[]{:S(2)}, u32[]{:S(2)}) collective-permute-start(bf16[3,96,768]{2,1,0:T(8,128)(2,1)S(1)} %pad_maximum_fusion.2.refs_9_), channel_id=1, source_target_pairs={{0,4},{4,0},{8,12},{12,8},{16,20},{20,16},{24,28},{28,24},{1,5},{5... | collective-permute-start | bytes 1327112 | tf_op jit(solution)/shard_map/ppermute | solution.py:940
  103.4 8.9 %collective-permute-start.18 = (bf16[3,96,768]{2,1,0:T(8,128)(2,1)S(1)}, bf16[3,96,768]{2,1,0:T(8,128)(2,1)S(1)}, u32[]{:S(2)}, u32[]{:S(2)}) collective-permute-start(bf16[3,96,768]{2,1,0:T(8,128)(2,1)S(1)} %collective-permute-done.15.refs_11_), channel_id=1, source_target_pairs={{0,4},{4,0},{8,12},{12,8},{16,20},{20,16},{24,28},{28,24},{1,5},{5... | collective-permute-start | bytes 1327112 | tf_op jit(solution)/shard_map/ppermute | solution.py:940
  103.5 9.3 %collective-permute-start.19 = (bf16[3,96,768]{2,1,0:T(8,128)(2,1)S(1)}, bf16[3,96,768]{2,1,0:T(8,128)(2,1)S(1)}, u32[]{:S(2)}, u32[]{:S(2)}) collective-permute-start(bf16[3,96,768]{2,1,0:T(8,128)(2,1)S(1)} %collective-permute-done.16.refs_13_), channel_id=1, source_target_pairs={{0,4},{4,0},{8,12},{12,8},{16,20},{20,16},{24,28},{28,24},{1,5},{5... | collective-permute-start | bytes 1327112 | tf_op jit(solution)/shard_map/ppermute | solution.py:940
  162.6 29.1 %collective-permute-start.29 = (bf16[4,4,2,96,768]{4,3,2,1,0:T(8,128)(2,1)}, bf16[4,4,2,96,768]{4,3,2,1,0:T(8,128)(2,1)}, u32[]{:S(2)}, u32[]{:S(2)}) collective-permute-start(bf16[4,4,2,96,768]{4,3,2,1,0:T(8,128)(2,1)} %get-tuple-element.173), channel_id=1, source_target_pairs={{0,4},{4,0},{8,12},{12,8},{16,20},{20,16},{24,28},{28,24},{1,5},{5... | collective-permute-start | bytes 14155784 | tf_op jit(solution)/shard_map/ppermute | solution.py:940
  163.0 28.7 %all-to-all-start.2 = ((bf16[8,128,768]{2,1,0:T(8,128)(2,1)}), bf16[8,128,768]{2,1,0:T(8,128)(2,1)S(1)}, u32[]{:S(2)}, u32[]{:S(2)}) async-start(bf16[8,128,768]{2,1,0:T(8,128)(2,1)} %bitcast.62), calls=%async_computation.2 | async-start | bytes 3145728 | tf_op jit(solution)/shard_map/all_to_all | solution.py:968
  191.6 42.5 %collective-permute-start.32 = (bf16[4,4,48,768]{3,2,1,0:T(8,128)(2,1)}, bf16[4,4,48,768]{3,2,1,0:T(8,128)(2,1)S(1)}, u32[]{:S(2)}, u32[]{:S(2)}) collective-permute-start(bf16[4,4,48,768]{3,2,1,0:T(8,128)(2,1)} %get-tuple-element.189), channel_id=1, source_target_pairs={{0,4},{4,0},{8,12},{12,8},{16,20},{20,16},{24,28},{28,24},{1,5},{5... | collective-permute-start | bytes 3538952 | tf_op jit(solution)/shard_map/ppermute | solution.py:940
  198.3 28.3 %collective-permute-start.30 = (bf16[2,4,96,768]{3,2,1,0:T(8,128)(2,1)}, bf16[2,4,96,768]{3,2,1,0:T(8,128)(2,1)S(1)}, u32[]{:S(2)}, u32[]{:S(2)}) collective-permute-start(bf16[2,4,96,768]{3,2,1,0:T(8,128)(2,1)} %get-tuple-element.183), channel_id=1, source_target_pairs={{0,8},{4,12},{8,0},{12,4},{16,24},{20,28},{24,16},{28,20},{1,9},{5... | collective-permute-start | bytes 3538952 | tf_op jit(solution)/shard_map/ppermute | solution.py:940
  199.9 27.3 %collective-permute-start.31 = (bf16[2,4,96,768]{3,2,1,0:T(8,128)(2,1)}, bf16[2,4,96,768]{3,2,1,0:T(8,128)(2,1)S(1)}, u32[]{:S(2)}, u32[]{:S(2)}) collective-permute-start(bf16[2,4,96,768]{3,2,1,0:T(8,128)(2,1)} %get-tuple-element.185), channel_id=1, source_target_pairs={{0,16},{4,20},{8,24},{12,28},{16,0},{20,4},{24,8},{28,12},{1,17},{... | collective-permute-start | bytes 3538952 | tf_op jit(solution)/shard_map/ppermute | solution.py:940
  232.1 20.7 %collective-permute-start.34 = (bf16[4,96,768]{2,1,0:T(8,128)(2,1)}, bf16[4,96,768]{2,1,0:T(8,128)(2,1)S(1)}, u32[]{:S(2)}, u32[]{:S(2)}) collective-permute-start(bf16[4,96,768]{2,1,0:T(8,128)(2,1)} %get-tuple-element.199), channel_id=1, source_target_pairs={{0,16},{4,20},{8,24},{12,28},{16,0},{20,4},{24,8},{28,12},{1,17},{... | collective-permute-start | bytes 1769480 | tf_op jit(solution)/shard_map/ppermute | solution.py:940
  233.4 19.5 %collective-permute-start.35 = (bf16[4,96,768]{2,1,0:T(8,128)(2,1)}, bf16[4,96,768]{2,1,0:T(8,128)(2,1)S(1)}, u32[]{:S(2)}, u32[]{:S(2)}) collective-permute-start(bf16[4,96,768]{2,1,0:T(8,128)(2,1)} %get-tuple-element.201), channel_id=1, source_target_pairs={{0,8},{4,12},{8,0},{12,4},{16,24},{20,28},{24,16},{28,20},{1,9},{5... | collective-permute-start | bytes 1769480 | tf_op jit(solution)/shard_map/ppermute | solution.py:940
  240.0 19.5 %collective-permute-start.39 = (bf16[384,768]{1,0:T(8,128)(2,1)}, bf16[384,768]{1,0:T(8,128)(2,1)S(1)}, u32[]{:S(2)}, u32[]{:S(2)}) collective-permute-start(bf16[384,768]{1,0:T(8,128)(2,1)} %get-tuple-element.206), channel_id=1, source_target_pairs={{0,8},{4,12},{8,0},{12,4},{16,24},{20,28},{24,16},{28,20},{1,9},{5... | collective-permute-start | bytes 1769480 | tf_op jit(solution)/shard_map/ppermute | solution.py:940
  240.7 19.7 %collective-permute-start.40 = (bf16[384,768]{1,0:T(8,128)(2,1)}, bf16[384,768]{1,0:T(8,128)(2,1)S(1)}, u32[]{:S(2)}, u32[]{:S(2)}) collective-permute-start(bf16[384,768]{1,0:T(8,128)(2,1)} %get-tuple-element.207), channel_id=1, source_target_pairs={{0,16},{4,20},{8,24},{12,28},{16,0},{20,4},{24,8},{28,12},{1,17},{... | collective-permute-start | bytes 1769480 | tf_op jit(solution)/shard_map/ppermute | solution.py:940
  240.9 31.1 %collective-permute-start.41 = (bf16[384,768]{1,0:T(8,128)(2,1)}, bf16[384,768]{1,0:T(8,128)(2,1)S(1)}, u32[]{:S(2)}, u32[]{:S(2)}) collective-permute-start(bf16[384,768]{1,0:T(8,128)(2,1)} %get-tuple-element.208), channel_id=1, source_target_pairs={{0,24},{4,28},{8,16},{12,20},{16,8},{20,12},{24,0},{28,4},{1,25},{... | collective-permute-start | bytes 1769480 | tf_op jit(solution)/shard_map/ppermute | solution.py:940
  256.5 20.3 %collective-permute-start.36 = (bf16[2,96,768]{2,1,0:T(8,128)(2,1)}, bf16[2,96,768]{2,1,0:T(8,128)(2,1)S(1)}, u32[]{:S(2)}, u32[]{:S(2)}) collective-permute-start(bf16[2,96,768]{2,1,0:T(8,128)(2,1)} %get-tuple-element.203), channel_id=1, source_target_pairs={{0,1},{1,0},{2,3},{3,2},{4,5},{5,4},{6,7},{7,6},{8,9},{9,8},{10,11... | collective-permute-start | bytes 884744 | tf_op jit(solution)/shard_map/ppermute | solution.py:940
  257.9 20.1 %collective-permute-start.37 = (bf16[2,96,768]{2,1,0:T(8,128)(2,1)}, bf16[2,96,768]{2,1,0:T(8,128)(2,1)S(1)}, u32[]{:S(2)}, u32[]{:S(2)}) collective-permute-start(bf16[2,96,768]{2,1,0:T(8,128)(2,1)} %get-tuple-element.204), channel_id=1, source_target_pairs={{0,2},{1,3},{2,0},{3,1},{4,6},{5,7},{6,4},{7,5},{8,10},{9,11},{10,... | collective-permute-start | bytes 884744 | tf_op jit(solution)/shard_map/ppermute | solution.py:940
  259.5 31.2 %collective-permute-start.38 = (bf16[2,96,768]{2,1,0:T(8,128)(2,1)}, bf16[2,96,768]{2,1,0:T(8,128)(2,1)S(1)}, u32[]{:S(2)}, u32[]{:S(2)}) collective-permute-start(bf16[2,96,768]{2,1,0:T(8,128)(2,1)} %get-tuple-element.205), channel_id=1, source_target_pairs={{0,3},{1,2},{2,1},{3,0},{4,7},{5,6},{6,5},{7,4},{8,11},{9,10},{10,... | collective-permute-start | bytes 884744 | tf_op jit(solution)/shard_map/ppermute | solution.py:940
  275.3 17.5 %collective-permute-start.42 = (bf16[112,768]{1,0:T(8,128)(2,1)}, bf16[112,768]{1,0:T(8,128)(2,1)S(1)}, u32[]{:S(2)}, u32[]{:S(2)}) collective-permute-start(bf16[112,768]{1,0:T(8,128)(2,1)} %get-tuple-element.221), channel_id=1, source_target_pairs={{0,1},{1,0},{2,3},{3,2},{4,5},{5,4},{6,7},{7,6},{8,9},{9,8},{10,11... | collective-permute-start | bytes 516104 | tf_op jit(solution)/shard_map/ppermute | solution.py:940
  276.7 16.8 %collective-permute-start.43 = (bf16[112,768]{1,0:T(8,128)(2,1)}, bf16[112,768]{1,0:T(8,128)(2,1)S(1)}, u32[]{:S(2)}, u32[]{:S(2)}) collective-permute-start(bf16[112,768]{1,0:T(8,128)(2,1)} %get-tuple-element.222), channel_id=1, source_target_pairs={{0,2},{1,3},{2,0},{3,1},{4,6},{5,7},{6,4},{7,5},{8,10},{9,11},{10,... | collective-permute-start | bytes 516104 | tf_op jit(solution)/shard_map/ppermute | solution.py:940
  276.8 20.9 %collective-permute-start.44 = (bf16[112,768]{1,0:T(8,128)(2,1)}, bf16[112,768]{1,0:T(8,128)(2,1)S(1)}, u32[]{:S(2)}, u32[]{:S(2)}) collective-permute-start(bf16[112,768]{1,0:T(8,128)(2,1)} %get-tuple-element.223), channel_id=1, source_target_pairs={{0,3},{1,2},{2,1},{3,0},{4,7},{5,6},{6,5},{7,4},{8,11},{9,10},{10,... | collective-permute-start | bytes 516104 | tf_op jit(solution)/shard_map/ppermute | solution.py:940
  290.9 9.5 %collective-permute-start.49 = (bf16[2,96,768]{2,1,0:T(8,128)(2,1)S(1)}, bf16[2,96,768]{2,1,0:T(8,128)(2,1)}, u32[]{:S(2)}, u32[]{:S(2)}) collective-permute-start(bf16[2,96,768]{2,1,0:T(8,128)(2,1)S(1)} %add_convert_fusion.refs_0_), channel_id=1, source_target_pairs={{0,16},{4,20},{8,24},{12,28},{16,0},{20,4},{24,8},{28,12},{1,17},{... | collective-permute-start | bytes 884744 | tf_op jit(solution)/shard_map/ppermute | solution.py:940
  300.4 12.9 %collective-permute-start.51 = (bf16[2,96,768]{2,1,0:T(8,128)(2,1)S(1)}, bf16[2,96,768]{2,1,0:T(8,128)(2,1)}, u32[]{:S(2)}, u32[]{:S(2)}) collective-permute-start(bf16[2,96,768]{2,1,0:T(8,128)(2,1)S(1)} %add_convert_fusion.refs_0_), channel_id=1, source_target_pairs={{0,4},{4,0},{8,12},{12,8},{16,20},{20,16},{24,28},{28,24},{1,5},{5... | collective-permute-start | bytes 884744 | tf_op jit(solution)/shard_map/ppermute | solution.py:940
  308.1 22.0 %collective-permute-start.47 = (bf16[112,768]{1,0:T(8,128)(2,1)}, bf16[112,768]{1,0:T(8,128)(2,1)}, u32[]{:S(2)}, u32[]{:S(2)}) collective-permute-start(bf16[112,768]{1,0:T(8,128)(2,1)} %add_convert_fusion.1), channel_id=1, source_target_pairs={{0,24},{4,28},{8,16},{12,20},{16,8},{20,12},{24,0},{28,4},{1,25},{... | collective-permute-start | bytes 516104 | tf_op jit(solution)/shard_map/ppermute | solution.py:940
  309.0 41.0 %all-to-all-start.3 = ((bf16[8,128,768]{2,1,0:T(8,128)(2,1)}), bf16[8,128,768]{2,1,0:T(8,128)(2,1)S(1)}, u32[]{:S(2)}, u32[]{:S(2)}) async-start(bf16[8,128,768]{2,1,0:T(8,128)(2,1)} %bitcast.60), calls=%async_computation.3 | async-start | bytes 3145728 | tf_op jit(solution)/shard_map/all_to_all | solution.py:968
  313.3 22.9 %collective-permute-start.46 = (bf16[112,768]{1,0:T(8,128)(2,1)}, bf16[112,768]{1,0:T(8,128)(2,1)S(1)}, u32[]{:S(2)}, u32[]{:S(2)}) collective-permute-start(bf16[112,768]{1,0:T(8,128)(2,1)} %add_convert_fusion.1), channel_id=1, source_target_pairs={{0,16},{4,20},{8,24},{12,28},{16,0},{20,4},{24,8},{28,12},{1,17},{... | collective-permute-start | bytes 516104 | tf_op jit(solution)/shard_map/ppermute | solution.py:940
  314.7 21.6 %collective-permute-start.45 = (bf16[112,768]{1,0:T(8,128)(2,1)}, bf16[112,768]{1,0:T(8,128)(2,1)S(1)}, u32[]{:S(2)}, u32[]{:S(2)}) collective-permute-start(bf16[112,768]{1,0:T(8,128)(2,1)} %add_convert_fusion.1), channel_id=1, source_target_pairs={{0,8},{4,12},{8,0},{12,4},{16,24},{20,28},{24,16},{28,20},{1,9},{5... | collective-permute-start | bytes 516104 | tf_op jit(solution)/shard_map/ppermute | solution.py:940
  (63 other events, 445.3 us)
where the time goes:
time: 356 us; the launch traced here: 352 us
  Pallas kernels  186 us (52%)
  starting transfers between devices  75 us (21%)
  waiting for transfers between devices  62.5 us (18%)
  other arithmetic  14.8 us (4%)
  local copies, waits for them, and re-layouts  12.1 us (3%)
    ppermute x59, waiting for transfers between devices, swap(): return lax.ppermute(value, axis, [(i, i ^ step) for i in range(count)])  62.5 us
    ppermute x59, starting transfers between devices, swap(): return lax.ppermute(value, axis, [(i, i ^ step) for i in range(count)])  57.4 us
    pallas_call x2, Pallas kernels, attention_grads(): pl.pallas_call(functools.partial(attention_grads_kernel, min(256, rows),...  49.1 us
    pallas_call x1, Pallas kernels, mlp_rows(): pl.pallas_call(functools.partial(mlp_rows_kernel, count, steps), grid_spe...  45.6 us
    pallas_call x2, Pallas kernels, attention_forward(): pl.pallas_call(functools.partial(attention_forward_kernel, min(128, rows)...  23.3 us
    pallas_call x2, Pallas kernels, renew_pieces(): pl.pallas_call(functools.partial(renew_kernel, len(pieces), parts, turned...  22.6 us
    all_to_all x4, starting transfers between devices, exchange(): return lax.all_to_all(array, 'seq', 0, 0, axis_index_groups=teams)  17.6 us
    pallas_call x1, Pallas kernels, input_back(): pl.pallas_call(input_back_kernel, grid=(rows // tile,), in_specs=[strip,...  10.2 us
  transfers between devices with their start and end apart: 63, of which 15 were waited for; matrix products, arithmetic and copies ran while one was open for 5% of the time, Pallas kernels for 40%

commit v1 on v0

--- a/solution.py
+++ b/solution.py
@@ -435,7 +435,7 @@
 
 def project(place, x, vec, pieces, whole):
     rows, width = x.shape
-    tile = row_tile(rows)
+    tile = min(512, rows)
     strip = pl.BlockSpec((tile, width), lambda i, p: (i, 0))
     fixed = lambda a: pl.BlockSpec(a.shape, lambda i, p: (0,) * len(a.shape))
     arrays = pieces if whole is None else [whole]
@@ -466,7 +466,7 @@
 
 def join(o, x, w, vec):
     rows, width = x.shape
-    tile = row_tile(rows)
+    tile = min(512, rows)
     strip = pl.BlockSpec((tile, width), lambda i: (i, 0))
     return pl.pallas_call(
         join_kernel,
@@ -757,8 +757,7 @@
 def renew_kernel(count, parts, turned, place, *refs):
     pieces = refs[:count]
     weight, moment, average = refs[count : count + 3]
-    outs = refs[count + 3 : count + 7]
-    grads = refs[count + 7]
+    outs, grads = refs[-5:-1], refs[-1]
     block = weight.shape[1]
 
     @pl.when(pl.program_id(0) == 0)
@@ -787,25 +786,29 @@
         out[...] = value
 
 
-def renew_pieces(place, pieces, parts, weight, moment, average, turned=False):
+def renew_pieces(
+    place, pieces, parts, weight, moment, average, turned=False, only=None, earlier=()
+):
     matrices, rows, width = weight.shape
+    count, at = (matrices, 0) if only is None else (1, only)
     steps = 4
-    block = pl.BlockSpec((matrices, rows // steps, width), lambda i, p: (0, i, 0))
-    fixed = pl.BlockSpec(pieces[0].shape, lambda i, p: (0, 0, 0))
+    block = pl.BlockSpec((count, rows // steps, width), lambda i, p: (at, i, 0))
+    fixed = pl.BlockSpec((count,) + pieces[0].shape[1:], lambda i, p: (at, 0, 0))
     return pl.pallas_call(
         functools.partial(renew_kernel, len(pieces), parts, turned),
         grid_spec=pltpu.PrefetchScalarGridSpec(
             num_scalar_prefetch=1,
             grid=(steps,),
-            in_specs=[fixed] * len(pieces) + [block] * 3,
+            in_specs=[fixed] * len(pieces) + [block] * 3 + [in_place()] * len(earlier),
             out_specs=[block] * 4,
-            scratch_shapes=[pltpu.VMEM(weight.shape, low)],
+            scratch_shapes=[pltpu.VMEM((count, rows, width), low)],
         ),
         out_shape=[jax.ShapeDtypeStruct(weight.shape, wide)] * 4,
+        input_output_aliases={4 + len(pieces) + i: i for i in range(len(earlier))},
         compiler_params=params(),
         cost_estimate=cost(10),
         name="renew_matrices",
-    )(place, *pieces, weight, moment, average)
+    )(place, *pieces, weight, moment, average, *earlier)
 
 
 def add_low(a, b):
@@ -1127,7 +1130,7 @@
         ready = (up_here, mlp_low, bias_pieces, query_seg_rows, key_seg_rows, valid)
         attn_chips = after(attn_chips, *ready)
         pieces = [attn_low] + spread_pairs(attn_chips)
-        grad_low = exchange(after(out_grad, *attn_chips), packs, rows)
+        grad_low = exchange(after(out_grad, first_here), packs, rows)
         grad_low = grad_low.reshape(packs * rows, width)
         up_here = after(up_here, *attn_chips)
         up_x, up_y = swap(up_here, "seq", 2), swap(up_here, "seq", 4)
@@ -1197,25 +1200,23 @@
         mlp_added = fold_last(after(up_keep, input_sums), up_other, down_keep, down_other)
         mlp_terms = hid_terms(mlp_added)
         extra = input_sums.shape[0] + early_rows.shape[0]
-        attn_terms = after(attn_terms, mlp_added[0])
+        attn_terms = after(attn_terms, *mlp_terms[:3])
         attn_added = sum_steps(attn_terms, hids, input_sums, early_rows)
         mlp_sums = sum_all(after(mlp_terms, attn_added[0]))
         mlp_chips = spread_chips(mlp_sums)
         attn_terms = hid_terms(attn_added)
-        input_grad = exchange(after(input_grad, mlp_sums), packs, rows)
-        attn_sums = sum_all(attn_terms)
+        block_out = block_out.astype(wide)
+        attn_sums = sum_all(after(attn_terms, block_out))
         attn_grad = spread_chips(attn_sums)
         mlp_grad = spread_pairs(after(mlp_chips, attn_sums))
-        mlp_new = renew_pieces(
-            place,
-            mlp_grad,
-            [(0, width // seqs)],
-            mlp_weight,
-            mlp_moment,
-            mlp_average,
-            turned=True,
-        )
-        attn_grad = spread_pairs(after(attn_grad, mlp_new[0]))
+        mlp_rest = ([(0, width // seqs)], mlp_weight, mlp_moment, mlp_average, True)
+        mlp_new = renew_pieces(place, mlp_grad, *mlp_rest, 0)
+        attn_grad = after(attn_grad, mlp_new[0])
+        input_grad = exchange(after(input_grad, *attn_grad), packs, rows)
+        mlp_grad = after(mlp_grad, *attn_grad)
+        mlp_new = renew_pieces(place, mlp_grad, *mlp_rest, 1, mlp_new)
+        attn_grad = after(attn_grad, mlp_new[0])
+        attn_grad = spread_pairs(attn_grad)
         group_rows = attn_piece // 2
         attn_new = renew_pieces(
             place,
@@ -1228,8 +1229,8 @@
         own = slice(attn_piece, attn_piece + extra)
         small = tree_sum([piece[own].astype(wide) for piece in attn_grad])
         return (
-            block_out.astype(wide),
-            input_grad.astype(wide),
+            block_out,
+            after(input_grad, attn_new[0]).astype(wide),
             *[array[0] for array in attn_new],
             *mlp_new,
             *renew(

time: 356 us -> 350 us (0.983)
  waiting for transfers between devices: 62.5 us -> 55.9 us
  starting transfers between devices: 75 us -> 69.5 us
    ppermute x59, waiting for transfers between devices: 62.5 us -> 55.9 us  [swap(): return lax.ppermute(value, axis, [(i, i ^ step) for i in range(count)])]
    ppermute x59, starting transfers between devices: 57.4 us -> 51.5 us  [swap(): return lax.ppermute(value, axis, [(i, i ^ step) for i in range(count)])]
    pallas_call x2 -> x3, Pallas kernels: 22.6 us -> 26 us  [renew_pieces(): pl.pallas_call(functools.partial(renew_kernel, len(pieces), parts, turned...]
    unnamed x95 -> x109, local copies, waits for them, and re-layouts: 6.35 us -> 9.6 us
  transfers between devices with their start and end apart: 63 -> 63, of which waited for: 15 -> 15; matrix products, arithmetic and copies ran while one was open for 5% -> 5% of each run, Pallas kernels for 40% -> 41%
where the time goes in v1:
time: 350 us; the launch traced here: 344 us
  Pallas kernels  188 us (54%)
  starting transfers between devices  69.5 us (20%)
  waiting for transfers between devices  55.9 us (16%)
  local copies, waits for them, and re-layouts  15.3 us (4%)
  other arithmetic  13.3 us (4%)
    ppermute x59, waiting for transfers between devices, swap(): return lax.ppermute(value, axis, [(i, i ^ step) for i in range(count)])  55.9 us
    ppermute x59, starting transfers between devices, swap(): return lax.ppermute(value, axis, [(i, i ^ step) for i in range(count)])  51.5 us
    pallas_call x2, Pallas kernels, attention_grads(): pl.pallas_call(functools.partial(attention_grads_kernel, min(256, rows),...  49.1 us
    pallas_call x1, Pallas kernels, mlp_rows(): pl.pallas_call(functools.partial(mlp_rows_kernel, count, steps), grid_spe...  45.6 us
    pallas_call x3, Pallas kernels, renew_pieces(): pl.pallas_call(functools.partial(renew_kernel, len(pieces), parts, turned...  26 us
    pallas_call x2, Pallas kernels, attention_forward(): pl.pallas_call(functools.partial(attention_forward_kernel, min(128, rows)...  23.2 us
    all_to_all x4, starting transfers between devices, exchange(): return lax.all_to_all(array, 'seq', 0, 0, axis_index_groups=teams)  18 us
    pallas_call x1, Pallas kernels, input_back(): pl.pallas_call(input_back_kernel, grid=(rows // tile,), in_specs=[strip,...  10.2 us
  transfers between devices with their start and end apart: 63, of which 15 were waited for; matrix products, arithmetic and copies ran while one was open for 5% of the time, Pallas kernels for 41%

profile of v1, /device:TPU:9, one launch (start us, length us, event | category | flops | bytes accessed | tf_op | source)
XLA Modules:
  0.0 344.0 jit_solution(14082079979714476266)
XLA Ops:
  0.7 5.0 %all-to-all-start = ((bf16[8,128,768]{2,1,0:T(8,128)(2,1)}), bf16[8,128,768]{2,1,0:T(8,128)(2,1)}, u32[]{:S(2)}, u32[]{:S(2)}) async-start(bf16[8,128,768]{2,1,0:T(8,128)(2,1)} %param.12), calls=%async_computation | async-start | bytes 3145728 | tf_op jit(solution)/shard_map/all_to_all | solution.py:971
  5.8 1.4 collective-permute-start.2
  10.8 2.6 fusion.6
  14.1 12.8 %collective-permute-done.2 = bf16[4,48,768]{2,1,0:T(8,128)(2,1)S(1)} collective-permute-done((bf16[4,48,768]{2,1,0:T(8,128)(2,1)S(1)}, bf16[4,48,768]{2,1,0:T(8,128)(2,1)S(1)}, u32[]{:S(2)}, u32[]{:S(2)}) %collective-permute-start.2) | collective-permute-done | bytes 294944 | tf_op jit(solution)/shard_map/ppermute | solution.py:943
  26.9 5.4 %collective-permute-done.1 = bf16[4,48,768]{2,1,0:T(8,128)(2,1)S(1)} collective-permute-done((bf16[4,48,768]{2,1,0:T(8,128)(2,1)S(1)}, bf16[4,48,768]{2,1,0:T(8,128)(2,1)S(1)}, u32[]{:S(2)}, u32[]{:S(2)}) %collective-permute-start.1) | collective-permute-done | bytes 294944 | tf_op jit(solution)/shard_map/ppermute | solution.py:943
  35.3 4.0 %collective-permute-start.6 = (bf16[96,768]{1,0:T(8,128)(2,1)S(1)}, bf16[96,768]{1,0:T(8,128)(2,1)S(1)}, u32[]{:S(2)}, u32[]{:S(2)}) collective-permute-start(bf16[96,768]{1,0:T(8,128)(2,1)S(1)} %get-tuple-element.151), channel_id=1, source_target_pairs={{0,2},{1,3},{2,0},{3,1},{4,6},{5,7},{6,4},{7,5},{8,10},{9,11},{10,... | collective-permute-start | bytes 442376 | tf_op jit(solution)/shard_map/ppermute | solution.py:943
  40.0 4.0 %convert_element_type.109.refs_8_ = bf16[2,768,768]{2,1,0:T(8,128)(2,1)} convert(f32[2,768,768]{2,1,0:T(8,128)} %refs_8_.3) | non-fusion elementwise | flops 1179648 | bytes 7077888 | tf_op jit(solution)/shard_map/convert_element_type | solution.py:1127
  44.6 1.5 fusion.valid_ref.refs_4_
  46.1 2.9 collective-permute-done.6
  49.1 1.6 collective-permute-start.8
  53.0 4.2 %all-to-all-start.1 = ((bf16[8,128,768]{2,1,0:T(8,128)(2,1)}), bf16[8,128,768]{2,1,0:T(8,128)(2,1)S(1)}, u32[]{:S(2)}, u32[]{:S(2)}) async-start(bf16[8,128,768]{2,1,0:T(8,128)(2,1)} %param.23), calls=%async_computation.1 | async-start | bytes 3145728 | tf_op jit(solution)/shard_map/all_to_all | solution.py:971
  57.5 4.0 %collective-permute-start.13 = (bf16[96,768]{1,0:T(8,128)(2,1)S(1)}, bf16[96,768]{1,0:T(8,128)(2,1)S(1)}, u32[]{:S(2)}, u32[]{:S(2)}) collective-permute-start(bf16[96,768]{1,0:T(8,128)(2,1)S(1)} %copy-done.19), channel_id=1, source_target_pairs={{0,2},{1,3},{2,0},{3,1},{4,6},{5,7},{6,4},{7,5},{8,10},{9,11},{10,... | collective-permute-start | bytes 442376 | tf_op jit(solution)/shard_map/ppermute | solution.py:943
  61.6 1.5 collective-permute-start.16
  64.2 9.4 %norm_and_project.1 = (bf16[3072,768]{1,0:T(8,128)(2,1)}, bf16[1024,768]{1,0:T(8,128)(2,1)}, bf16[1024,768]{1,0:T(8,128)(2,1)}, bf16[1024,768]{1,0:T(8,128)(2,1)}, bf16[1024,768]{1,0:T(8,128)(2,1)}) custom-call(s32[2]{0:T(128)} %pad_add_fusion.place, bf16[1024,768]{1,0:T(8,128)(2,1)} %bitcast.2.x_ref, f32[12,768]{1,0:T(8,128)} %vec_ref.5, ...), custom_call_target="tpu_custom_call" | custom-call | flops 4000001024 | bytes 1000 | tf_op jit(solution)/shard_map/norm_and_project/pallas_call | solution.py:444
  74.1 11.6 %attention_forward.2 = (bf16[1024,768]{1,0:T(8,128)(2,1)}, f32[6,2,1024]{2,1,0:T(2,128)}) custom-call(bf16[1024,768]{1,0:T(8,128)(2,1)} %get-tuple-element.161.q_ref.refs_0_, bf16[1024,768]{1,0:T(8,128)(2,1)} %get-tuple-element.162.k_ref.refs_1_, bf16[1024,768]{1,0:T(8,128)(2,1)} %get-tuple-element.163.v_ref.refs_2_, s32[1024,1]{1,0:T(8,128)} %copy.43.query_seg.refs_7_, ...), custom_call_target="tpu_custom_call" | custom-call | flops 4800001024 | bytes 1000 | tf_op jit(solution)/shard_map/attention_forward/pallas_call | solution.py:106
  85.7 11.6 %attention_forward.3 = (bf16[1024,768]{1,0:T(8,128)(2,1)}, f32[6,2,1024]{2,1,0:T(2,128)}) custom-call(bf16[1024,768]{1,0:T(8,128)(2,1)} %get-tuple-element.161.q_ref.refs_0_, bf16[1024,768]{1,0:T(8,128)(2,1)} %get-tuple-element.162.k_ref.refs_1_, bf16[1024,768]{1,0:T(8,128)(2,1)} %get-tuple-element.163.v_ref.refs_2_, ...), custom_call_target="tpu_custom_call", output_to_operand_aliasing={{0}: (6, {}), {1}: (7, {})} | custom-call | flops 4800001024 | bytes 1000 | tf_op jit(solution)/shard_map/attention_forward/pallas_call | solution.py:106
  97.3 1.4 collective-permute-start.20
  100.0 2.7 collective-permute-start.17
  103.2 5.3 %join_and_norm.1 = (f32[1024,768]{1,0:T(8,128)}, bf16[1024,768]{1,0:T(8,128)(2,1)}) custom-call(bf16[1024,768]{1,0:T(8,128)(2,1)} %get-tuple-element.166.o_ref.refs_3_.refs_10_, bf16[1024,768]{1,0:T(8,128)(2,1)} %bitcast.2.x_ref, bf16[3072,768]{1,0:T(8,128)(2,1)} %get-tuple-element.167.w_ref.refs_5_, f32[12,768]{1,0:T(8,128)} %vec_ref.5), custom_call_target="tpu_custom_call" | custom-call | flops 2400001024 | bytes 1000 | tf_op jit(solution)/shard_map/join_and_norm/pallas_call | solution.py:471
  108.5 1.6 collective-permute-start.24
  110.1 1.6 collective-permute-start.25
  116.2 45.6 %mlp_both_ways.1 = (bf16[1024,768]{1,0:T(8,128)(2,1)}, f32[1024,768]{1,0:T(8,128)}, bf16[1024,768]{1,0:T(8,128)(2,1)}, bf16[1024,768]{1,0:T(8,128)(2,1)}, f32[6,...) custom-call(s32[2]{0:T(128)} %pad_add_fusion.place, ...), custom_call_target="tpu_custom_call" | custom-call | flops 14400001024 | bytes 1000 | tf_op jit(solution)/shard_map/mlp_both_ways/pallas_call | solution.py:670
  162.1 4.1 %all-to-all-start.2 = ((bf16[8,128,768]{2,1,0:T(8,128)(2,1)}), bf16[8,128,768]{2,1,0:T(8,128)(2,1)S(1)}, u32[]{:S(2)}, u32[]{:S(2)}) async-start(bf16[8,128,768]{2,1,0:T(8,128)(2,1)} %bitcast.61), calls=%async_computation.2 | async-start | bytes 3145728 | tf_op jit(solution)/shard_map/all_to_all | solution.py:971
  166.2 24.5 %attention_backward.2 = (bf16[1024,768]{1,0:T(8,128)(2,1)}, bf16[1024,768]{1,0:T(8,128)(2,1)}, bf16[1024,768]{1,0:T(8,128)(2,1)}, bf16[4,4,48,768]{3,2,1,0:T(8,128)(2,1)}, bf16[4,4,48,768]{3,2,1,0:T(8,128)(2,1)}) custom-call(s32[2]{0:T(128)} %pad_add_fusion.place, bf16[1024,768]{1,0:T(8,128)(2,1)} %get-tuple-element.161.q_ref.refs_0_, ...), custom_call_target="tpu_custom_call" | custom-call | flops 8400001024 | bytes 1000 | tf_op jit(solution)/shard_map/attention_backward/pallas_call | solution.py:252
  190.9 6.5 %fold_cores.2 = (bf16[2,4,96,768]{3,2,1,0:T(8,128)(2,1)}, bf16[2,4,96,768]{3,2,1,0:T(8,128)(2,1)}, bf16[2,4,96,768]{3,2,1,0:T(8,128)(2,1)}, bf16[2,4,96,768]{3,2,1,0:T(8,128)(2,1)}) custom-call(bf16[4,4,2,96,768]{4,3,2,1,0:T(8,128)(2,1)} %get-tuple-element.193.even_ref, bf16[4,4,2,96,768]{4,3,2,1,0:T(8,128)(2,1)} %collective-permute-done.29.other_ref), custom_call_target="tpu_custom_call" | custom-call | flops 1600001024 | bytes 1000 | tf_op jit(solution)/shard_map/fold_cores/pallas_call | solution.py:830
  197.4 1.6 collective-permute-start.30
  200.2 24.6 %attention_backward.3 = (bf16[1024,768]{1,0:T(8,128)(2,1)}, bf16[1024,768]{1,0:T(8,128)(2,1)}, bf16[1024,768]{1,0:T(8,128)(2,1)}, bf16[4,4,48,768]{3,2,1,0:T(8,128)(2,1)}, bf16[4,4,48,768]{3,2,1,0:T(8,128)(2,1)}) custom-call(s32[2]{0:T(128)} %pad_add_fusion.place, ...), custom_call_target="tpu_custom_call", output_to_operand_aliasing={{0}: (12, {}), {1}: (13, {}), {2}: (14, {})} | custom-call | flops 8400001024 | bytes 1000 | tf_op jit(solution)/shard_map/attention_backward/pallas_call | solution.py:252
  227.3 3.9 %fold_chips.1 = (bf16[4,96,768]{2,1,0:T(8,128)(2,1)}, bf16[4,96,768]{2,1,0:T(8,128)(2,1)}, bf16[4,96,768]{2,1,0:T(8,128)(2,1)}, bf16[4,96,768]{2,1,0:T(8,128)(2,1)}) custom-call(bf16[2,4,96,768]{3,2,1,0:T(8,128)(2,1)} %get-tuple-element.203.up, bf16[2,4,96,768]{3,2,1,0:T(8,128)(2,1)} %copy-done.37, bf16[2,4,96,768]{3,2,1,0:T(8,128)(2,1)} %get-tuple-element.205.down, ...), custom_call_target="tpu_custom_call" | custom-call | flops 1600001024 | bytes 1000 | tf_op jit(solution)/shard_map/fold_chips/pallas_call | solution.py:851
  231.2 1.3 collective-permute-start.37
  235.2 3.9 %fold_cores.3 = (bf16[384,768]{1,0:T(8,128)(2,1)}, bf16[384,768]{1,0:T(8,128)(2,1)}, bf16[384,768]{1,0:T(8,128)(2,1)}, bf16[384,768]{1,0:T(8,128)(2,1)}) custom-call(bf16[4,4,48,768]{3,2,1,0:T(8,128)(2,1)} %get-tuple-element.208.refs_0_, bf16[4,4,48,768]{3,2,1,0:T(8,128)(2,1)} %get-tuple-element.209.refs_1_, bf16[4,4,48,768]{3,2,1,0:T(8,128)(2,1)} %copy-done.36, ...), custom_call_target="tpu_custom_call" | custom-call | flops 1600001024 | bytes 1000 | tf_op jit(solution)/shard_map/fold_cores/pallas_call | solution.py:895
  240.0 1.7 collective-permute-start.36
  241.7 10.2 %input_backward.1 = (bf16[1024,768]{1,0:T(8,128)(2,1)}, f32[8,768]{1,0:T(8,128)}) custom-call(bf16[1024,768]{1,0:T(8,128)(2,1)} %get-tuple-element.213.dq_ref, bf16[1024,768]{1,0:T(8,128)(2,1)} %get-tuple-element.214.dk_ref, bf16[1024,768]{1,0:T(8,128)(2,1)} %get-tuple-element.215.dv_ref, bf16[3072,768]{1,0:T(8,128)(2,1)} %get-tuple-element.167.w_ref.refs_5_, ...), custom_call_target="tpu_custom_call" | custom-call | flops 4000001024 | bytes 1000 | tf_op jit(solution)/shard_map/input_backward/pallas_call | solution.py:734
  252.9 2.7 fold_last.1
  255.6 1.4 collective-permute-start.39
  257.1 1.5 collective-permute-done.34.refs_1_
  259.5 11.6 %collective-permute-done.36.refs_3_ = bf16[384,768]{1,0:T(8,128)(2,1)S(1)} collective-permute-done((bf16[384,768]{1,0:T(8,128)(2,1)}, bf16[384,768]{1,0:T(8,128)(2,1)S(1)}, u32[]{:S(2)}, u32[]{:S(2)}) %collective-permute-start.36) | collective-permute-done | bytes 589856 | tf_op jit(solution)/shard_map/ppermute | solution.py:943
  271.9 2.6 sum_steps.1
  274.4 7.9 %collective-permute-done.47 = bf16[2,96,768]{2,1,0:T(8,128)(2,1)S(1)} collective-permute-done((bf16[2,96,768]{2,1,0:T(8,128)(2,1)}, bf16[2,96,768]{2,1,0:T(8,128)(2,1)S(1)}, u32[]{:S(2)}, u32[]{:S(2)}) %collective-permute-start.47) | collective-permute-done | bytes 294944 | tf_op jit(solution)/shard_map/ppermute | solution.py:943
  283.4 1.6 collective-permute-start.43
  285.9 1.3 collective-permute-start.49
  287.9 1.9 convert_element_type.112
  289.9 10.4 %collective-permute-done.43 = bf16[112,768]{1,0:T(8,128)(2,1)S(1)} collective-permute-done((bf16[112,768]{1,0:T(8,128)(2,1)}, bf16[112,768]{1,0:T(8,128)(2,1)S(1)}, u32[]{:S(2)}, u32[]{:S(2)}) %collective-permute-start.43) | collective-permute-done | bytes 172064 | tf_op jit(solution)/shard_map/ppermute | solution.py:943
  300.4 1.5 collective-permute-start.51
  306.6 8.7 %renew_matrices.3 = (f32[2,768,768]{2,1,0:T(8,128)}, f32[2,768,768]{2,1,0:T(8,128)}, f32[2,768,768]{2,1,0:T(8,128)}, f32[2,768,768]{2,1,0:T(8,128)}) custom-call(s32[2]{0:T(128)} %pad_add_fusion.place, bf16[2,96,768]{2,1,0:T(8,128)(2,1)} %copy-done.3, bf16[2,96,768]{2,1,0:T(8,128)(2,1)} %copy-done.8, bf16[2,96,768]{2,1,0:T(8,128)(2,1)} %copy-done.7, ...), custom_call_target="tpu_custom_call" | custom-call | flops 4000001024 | bytes 1000 | tf_op jit(solution)/shard_map/renew_matrices/pallas_call | solution.py:797
  316.7 4.8 %all-to-all-start.3 = ((bf16[8,128,768]{2,1,0:T(8,128)(2,1)}), bf16[8,128,768]{2,1,0:T(8,128)(2,1)S(1)}, u32[]{:S(2)}, u32[]{:S(2)}) async-start(bf16[8,128,768]{2,1,0:T(8,128)(2,1)} %bitcast.27), calls=%async_computation.3 | async-start | bytes 3145728 | tf_op jit(solution)/shard_map/all_to_all | solution.py:971
  321.5 8.9 %renew_matrices.4 = (f32[2,768,768]{2,1,0:T(8,128)}, f32[2,768,768]{2,1,0:T(8,128)}, f32[2,768,768]{2,1,0:T(8,128)}, f32[2,768,768]{2,1,0:T(8,128)}) custom-call(s32[2]{0:T(128)} %pad_add_fusion.place, bf16[2,96,768]{2,1,0:T(8,128)(2,1)} %copy-done.3, ...), custom_call_target="tpu_custom_call", output_to_operand_aliasing={{0}: (12, {}), {1}: (13, {}), {2}: (14, {}), {3}: (15, {})} | custom-call | flops 4000001024 | bytes 1000 | tf_op jit(solution)/shard_map/renew_matrices/pallas_call | solution.py:797
  333.4 8.4 %renew_matrices.5 = (f32[1,768,768]{2,1,0:T(8,128)}, f32[1,768,768]{2,1,0:T(8,128)}, f32[1,768,768]{2,1,0:T(8,128)}, f32[1,768,768]{2,1,0:T(8,128)}) custom-call(s32[2]{0:T(128)} %pad_add_fusion.place, bf16[1,112,768]{2,1,0:T(8,128)(2,1)} %bitcast.62, bf16[1,112,768]{2,1,0:T(8,128)(2,1)} %bitcast.78, bf16[1,112,768]{2,1,0:T(8,128)(2,1)} %bitcast.77, ...), custom_call_target="tpu_custom_call" | custom-call | flops 4000001024 | bytes 1000 | tf_op jit(solution)/shard_map/renew_matrices/pallas_call | solution.py:797
  341.8 1.9 convert_element_type.123
  (242 shorter events, 41.5 us)
Async XLA Ops:
  0.7 31.7 %all-to-all-start = ((bf16[8,128,768]{2,1,0:T(8,128)(2,1)}), bf16[8,128,768]{2,1,0:T(8,128)(2,1)}, u32[]{:S(2)}, u32[]{:S(2)}) async-start(bf16[8,128,768]{2,1,0:T(8,128)(2,1)} %param.12), calls=%async_computation | async-start | bytes 3145728 | tf_op jit(solution)/shard_map/all_to_all | solution.py:971
  5.8 21.2 %collective-permute-start.2 = (bf16[4,48,768]{2,1,0:T(8,128)(2,1)S(1)}, bf16[4,48,768]{2,1,0:T(8,128)(2,1)S(1)}, u32[]{:S(2)}, u32[]{:S(2)}) collective-permute-start(bf16[4,48,768]{2,1,0:T(8,128)(2,1)S(1)} %pad_maximum_fusion.4), channel_id=1, source_target_pairs={{0,3},{1,2},{2,1},{3,0},{4,7},{5,6},{6,5},{7,4},{8,11},{9,10},{10,... | collective-permute-start | bytes 884744 | tf_op jit(solution)/shard_map/ppermute | solution.py:943
  7.1 25.2 %collective-permute-start.1 = (bf16[4,48,768]{2,1,0:T(8,128)(2,1)S(1)}, bf16[4,48,768]{2,1,0:T(8,128)(2,1)S(1)}, u32[]{:S(2)}, u32[]{:S(2)}) collective-permute-start(bf16[4,48,768]{2,1,0:T(8,128)(2,1)S(1)} %pad_maximum_fusion.4), channel_id=1, source_target_pairs={{0,2},{1,3},{2,0},{3,1},{4,6},{5,7},{6,4},{7,5},{8,10},{9,11},{10,... | collective-permute-start | bytes 884744 | tf_op jit(solution)/shard_map/ppermute | solution.py:943
  8.2 24.1 %collective-permute-start = (bf16[4,48,768]{2,1,0:T(8,128)(2,1)S(1)}, bf16[4,48,768]{2,1,0:T(8,128)(2,1)S(1)}, u32[]{:S(2)}, u32[]{:S(2)}) collective-permute-start(bf16[4,48,768]{2,1,0:T(8,128)(2,1)S(1)} %pad_maximum_fusion.4), channel_id=1, source_target_pairs={{0,1},{1,0},{2,3},{3,2},{4,5},{5,4},{6,7},{7,6},{8,9},{9,8},{10,11... | collective-permute-start | bytes 884744 | tf_op jit(solution)/shard_map/ppermute | solution.py:943
  32.5 16.6 %collective-permute-start.3 = (bf16[3,2,48,768]{3,2,1,0:T(8,128)(2,1)S(1)}, bf16[3,2,48,768]{3,2,1,0:T(8,128)(2,1)S(1)}, u32[]{:S(2)}, u32[]{:S(2)}) collective-permute-start(bf16[3,2,48,768]{3,2,1,0:T(8,128)(2,1)S(1)} %pad_maximum_fusion.refs_1_), channel_id=1, source_target_pairs={{0,8},{4,12},{8,0},{12,4},{16,24},{20,28},{24,16},{28,20},{1,9},{5... | collective-permute-start | bytes 1327112 | tf_op jit(solution)/shard_map/ppermute | solution.py:943
  33.8 15.3 %collective-permute-start.4 = (bf16[3,2,48,768]{3,2,1,0:T(8,128)(2,1)S(1)}, bf16[3,2,48,768]{3,2,1,0:T(8,128)(2,1)}, u32[]{:S(2)}, u32[]{:S(2)}) collective-permute-start(bf16[3,2,48,768]{3,2,1,0:T(8,128)(2,1)S(1)} %pad_maximum_fusion.1.refs_5_), channel_id=1, source_target_pairs={{0,16},{4,20},{8,24},{12,28},{16,0},{20,4},{24,8},{28,12},{1,17},{... | collective-permute-start | bytes 1327112 | tf_op jit(solution)/shard_map/ppermute | solution.py:943
  35.1 11.1 %collective-permute-start.7 = (bf16[96,768]{1,0:T(8,128)(2,1)S(1)}, bf16[96,768]{1,0:T(8,128)(2,1)S(1)}, u32[]{:S(2)}, u32[]{:S(2)}) collective-permute-start(bf16[96,768]{1,0:T(8,128)(2,1)S(1)} %get-tuple-element.151), channel_id=1, source_target_pairs={{0,3},{1,2},{2,1},{3,0},{4,7},{5,6},{6,5},{7,4},{8,11},{9,10},{10,... | collective-permute-start | bytes 442376 | tf_op jit(solution)/shard_map/ppermute | solution.py:943
  35.3 13.8 %collective-permute-start.6 = (bf16[96,768]{1,0:T(8,128)(2,1)S(1)}, bf16[96,768]{1,0:T(8,128)(2,1)S(1)}, u32[]{:S(2)}, u32[]{:S(2)}) collective-permute-start(bf16[96,768]{1,0:T(8,128)(2,1)S(1)} %get-tuple-element.151), channel_id=1, source_target_pairs={{0,2},{1,3},{2,0},{3,1},{4,6},{5,7},{6,4},{7,5},{8,10},{9,11},{10,... | collective-permute-start | bytes 442376 | tf_op jit(solution)/shard_map/ppermute | solution.py:943
  39.3 9.8 %collective-permute-start.5 = (bf16[96,768]{1,0:T(8,128)(2,1)S(1)}, bf16[96,768]{1,0:T(8,128)(2,1)S(1)}, u32[]{:S(2)}, u32[]{:S(2)}) collective-permute-start(bf16[96,768]{1,0:T(8,128)(2,1)S(1)} %get-tuple-element.151), channel_id=1, source_target_pairs={{0,1},{1,0},{2,3},{3,2},{4,5},{5,4},{6,7},{7,6},{8,9},{9,8},{10,11... | collective-permute-start | bytes 442376 | tf_op jit(solution)/shard_map/ppermute | solution.py:943
  49.1 8.4 %collective-permute-start.8 = (bf16[3,2,48,768]{3,2,1,0:T(8,128)(2,1)S(1)}, bf16[3,2,48,768]{3,2,1,0:T(8,128)(2,1)}, u32[]{:S(2)}, u32[]{:S(2)}) collective-permute-start(bf16[3,2,48,768]{3,2,1,0:T(8,128)(2,1)S(1)} %pad_maximum_fusion.refs_1_), channel_id=1, source_target_pairs={{0,4},{4,0},{8,12},{12,8},{16,20},{20,16},{24,28},{28,24},{1,5},{5... | collective-permute-start | bytes 1327112 | tf_op jit(solution)/shard_map/ppermute | solution.py:943
  50.7 10.8 %collective-permute-start.9 = (bf16[3,2,48,768]{3,2,1,0:T(8,128)(2,1)S(1)}, bf16[3,2,48,768]{3,2,1,0:T(8,128)(2,1)}, u32[]{:S(2)}, u32[]{:S(2)}) collective-permute-start(bf16[3,2,48,768]{3,2,1,0:T(8,128)(2,1)S(1)} %collective-permute-done.3.refs_3_), channel_id=1, source_target_pairs={{0,4},{4,0},{8,12},{12,8},{16,20},{20,16},{24,28},{28,24},{1,5},{5... | collective-permute-start | bytes 1327112 | tf_op jit(solution)/shard_map/ppermute | solution.py:943
  50.8 10.8 %collective-permute-start.10 = (bf16[3,2,48,768]{3,2,1,0:T(8,128)(2,1)S(1)}, bf16[3,2,48,768]{3,2,1,0:T(8,128)(2,1)}, u32[]{:S(2)}, u32[]{:S(2)}) collective-permute-start(bf16[3,2,48,768]{3,2,1,0:T(8,128)(2,1)S(1)} %pad_maximum_fusion.1.refs_5_), channel_id=1, source_target_pairs={{0,4},{4,0},{8,12},{12,8},{16,20},{20,16},{24,28},{28,24},{1,5},{5... | collective-permute-start | bytes 1327112 | tf_op jit(solution)/shard_map/ppermute | solution.py:943
  51.2 11.8 %collective-permute-start.11 = (bf16[3,2,48,768]{3,2,1,0:T(8,128)(2,1)}, bf16[3,2,48,768]{3,2,1,0:T(8,128)(2,1)}, u32[]{:S(2)}, u32[]{:S(2)}) collective-permute-start(bf16[3,2,48,768]{3,2,1,0:T(8,128)(2,1)} %collective-permute-done.4.refs_7_), channel_id=1, source_target_pairs={{0,4},{4,0},{8,12},{12,8},{16,20},{20,16},{24,28},{28,24},{1,5},{5... | collective-permute-start | bytes 1327112 | tf_op jit(solution)/shard_map/ppermute | solution.py:943
  53.0 60.7 %all-to-all-start.1 = ((bf16[8,128,768]{2,1,0:T(8,128)(2,1)}), bf16[8,128,768]{2,1,0:T(8,128)(2,1)S(1)}, u32[]{:S(2)}, u32[]{:S(2)}) async-start(bf16[8,128,768]{2,1,0:T(8,128)(2,1)} %param.23), calls=%async_computation.1 | async-start | bytes 3145728 | tf_op jit(solution)/shard_map/all_to_all | solution.py:971
  57.3 16.3 %collective-permute-start.14 = (bf16[96,768]{1,0:T(8,128)(2,1)S(1)}, bf16[96,768]{1,0:T(8,128)(2,1)S(1)}, u32[]{:S(2)}, u32[]{:S(2)}) collective-permute-start(bf16[96,768]{1,0:T(8,128)(2,1)S(1)} %copy-done.19), channel_id=1, source_target_pairs={{0,3},{1,2},{2,1},{3,0},{4,7},{5,6},{6,5},{7,4},{8,11},{9,10},{10,... | collective-permute-start | bytes 442376 | tf_op jit(solution)/shard_map/ppermute | solution.py:943
  57.5 16.0 %collective-permute-start.13 = (bf16[96,768]{1,0:T(8,128)(2,1)S(1)}, bf16[96,768]{1,0:T(8,128)(2,1)S(1)}, u32[]{:S(2)}, u32[]{:S(2)}) collective-permute-start(bf16[96,768]{1,0:T(8,128)(2,1)S(1)} %copy-done.19), channel_id=1, source_target_pairs={{0,2},{1,3},{2,0},{3,1},{4,6},{5,7},{6,4},{7,5},{8,10},{9,11},{10,... | collective-permute-start | bytes 442376 | tf_op jit(solution)/shard_map/ppermute | solution.py:943
  61.5 12.1 %collective-permute-start.12 = (bf16[96,768]{1,0:T(8,128)(2,1)S(1)}, bf16[96,768]{1,0:T(8,128)(2,1)S(1)}, u32[]{:S(2)}, u32[]{:S(2)}) collective-permute-start(bf16[96,768]{1,0:T(8,128)(2,1)S(1)} %copy-done.19), channel_id=1, source_target_pairs={{0,1},{1,0},{2,3},{3,2},{4,5},{5,4},{6,7},{7,6},{8,9},{9,8},{10,11... | collective-permute-start | bytes 442376 | tf_op jit(solution)/shard_map/ppermute | solution.py:943
  61.6 38.4 %collective-permute-start.16 = (bf16[3,96,768]{2,1,0:T(8,128)(2,1)S(1)}, bf16[3,96,768]{2,1,0:T(8,128)(2,1)S(1)}, u32[]{:S(2)}, u32[]{:S(2)}) collective-permute-start(bf16[3,96,768]{2,1,0:T(8,128)(2,1)S(1)} %pad_maximum_fusion.2.refs_9_), channel_id=1, source_target_pairs={{0,16},{4,20},{8,24},{12,28},{16,0},{20,4},{24,8},{28,12},{1,17},{... | collective-permute-start | bytes 1327112 | tf_op jit(solution)/shard_map/ppermute | solution.py:943
  63.0 34.3 %collective-permute-start.15 = (bf16[3,96,768]{2,1,0:T(8,128)(2,1)S(1)}, bf16[3,96,768]{2,1,0:T(8,128)(2,1)S(1)}, u32[]{:S(2)}, u32[]{:S(2)}) collective-permute-start(bf16[3,96,768]{2,1,0:T(8,128)(2,1)S(1)} %pad_maximum_fusion.2.refs_9_), channel_id=1, source_target_pairs={{0,8},{4,12},{8,0},{12,4},{16,24},{20,28},{24,16},{28,20},{1,9},{5... | collective-permute-start | bytes 1327112 | tf_op jit(solution)/shard_map/ppermute | solution.py:943
  73.7 25.1 %collective-permute-start.23 = (bf16[3,96,768]{2,1,0:T(8,128)(2,1)S(1)}, bf16[3,96,768]{2,1,0:T(8,128)(2,1)}, u32[]{:S(2)}, u32[]{:S(2)}) collective-permute-start(bf16[3,96,768]{2,1,0:T(8,128)(2,1)S(1)} %pad_maximum_fusion.3.refs_17_), channel_id=1, source_target_pairs={{0,16},{4,20},{8,24},{12,28},{16,0},{20,4},{24,8},{28,12},{1,17},{... | collective-permute-start | bytes 1327112 | tf_op jit(solution)/shard_map/ppermute | solution.py:943
  74.0 28.7 %collective-permute-start.22 = (bf16[3,96,768]{2,1,0:T(8,128)(2,1)S(1)}, bf16[3,96,768]{2,1,0:T(8,128)(2,1)}, u32[]{:S(2)}, u32[]{:S(2)}) collective-permute-start(bf16[3,96,768]{2,1,0:T(8,128)(2,1)S(1)} %pad_maximum_fusion.3.refs_17_), channel_id=1, source_target_pairs={{0,8},{4,12},{8,0},{12,4},{16,24},{20,28},{24,16},{28,20},{1,9},{5... | collective-permute-start | bytes 1327112 | tf_op jit(solution)/shard_map/ppermute | solution.py:943
  97.3 11.2 %collective-permute-start.20 = (bf16[3,96,768]{2,1,0:T(8,128)(2,1)S(1)}, bf16[3,96,768]{2,1,0:T(8,128)(2,1)}, u32[]{:S(2)}, u32[]{:S(2)}) collective-permute-start(bf16[3,96,768]{2,1,0:T(8,128)(2,1)S(1)} %collective-permute-done.15.refs_11_), channel_id=1, source_target_pairs={{0,16},{4,20},{8,24},{12,28},{16,0},{20,4},{24,8},{28,12},{1,17},{... | collective-permute-start | bytes 1327112 | tf_op jit(solution)/shard_map/ppermute | solution.py:943
  98.8 11.3 %collective-permute-start.27 = (bf16[3,96,768]{2,1,0:T(8,128)(2,1)}, bf16[3,96,768]{2,1,0:T(8,128)(2,1)}, u32[]{:S(2)}, u32[]{:S(2)}) collective-permute-start(bf16[3,96,768]{2,1,0:T(8,128)(2,1)} %collective-permute-done.23.refs_21_), channel_id=1, source_target_pairs={{0,8},{4,12},{8,0},{12,4},{16,24},{20,28},{24,16},{28,20},{1,9},{5... | collective-permute-start | bytes 1327112 | tf_op jit(solution)/shard_map/ppermute | solution.py:943
  100.0 11.7 %collective-permute-start.17 = (bf16[3,96,768]{2,1,0:T(8,128)(2,1)S(1)}, bf16[3,96,768]{2,1,0:T(8,128)(2,1)S(1)}, u32[]{:S(2)}, u32[]{:S(2)}) collective-permute-start(bf16[3,96,768]{2,1,0:T(8,128)(2,1)S(1)} %pad_maximum_fusion.2.refs_9_), channel_id=1, source_target_pairs={{0,4},{4,0},{8,12},{12,8},{16,20},{20,16},{24,28},{28,24},{1,5},{5... | collective-permute-start | bytes 1327112 | tf_op jit(solution)/shard_map/ppermute | solution.py:943
  102.7 9.1 %collective-permute-start.18 = (bf16[3,96,768]{2,1,0:T(8,128)(2,1)S(1)}, bf16[3,96,768]{2,1,0:T(8,128)(2,1)S(1)}, u32[]{:S(2)}, u32[]{:S(2)}) collective-permute-start(bf16[3,96,768]{2,1,0:T(8,128)(2,1)S(1)} %collective-permute-done.15.refs_11_), channel_id=1, source_target_pairs={{0,4},{4,0},{8,12},{12,8},{16,20},{20,16},{24,28},{28,24},{1,5},{5... | collective-permute-start | bytes 1327112 | tf_op jit(solution)/shard_map/ppermute | solution.py:943
  102.7 9.5 %collective-permute-start.19 = (bf16[3,96,768]{2,1,0:T(8,128)(2,1)S(1)}, bf16[3,96,768]{2,1,0:T(8,128)(2,1)S(1)}, u32[]{:S(2)}, u32[]{:S(2)}) collective-permute-start(bf16[3,96,768]{2,1,0:T(8,128)(2,1)S(1)} %collective-permute-done.16.refs_13_), channel_id=1, source_target_pairs={{0,4},{4,0},{8,12},{12,8},{16,20},{20,16},{24,28},{28,24},{1,5},{5... | collective-permute-start | bytes 1327112 | tf_op jit(solution)/shard_map/ppermute | solution.py:943
  161.7 29.2 %collective-permute-start.29 = (bf16[4,4,2,96,768]{4,3,2,1,0:T(8,128)(2,1)}, bf16[4,4,2,96,768]{4,3,2,1,0:T(8,128)(2,1)}, u32[]{:S(2)}, u32[]{:S(2)}) collective-permute-start(bf16[4,4,2,96,768]{4,3,2,1,0:T(8,128)(2,1)} %get-tuple-element.194), channel_id=1, source_target_pairs={{0,4},{4,0},{8,12},{12,8},{16,20},{20,16},{24,28},{28,24},{1,5},{5... | collective-permute-start | bytes 14155784 | tf_op jit(solution)/shard_map/ppermute | solution.py:943
  162.1 28.7 %all-to-all-start.2 = ((bf16[8,128,768]{2,1,0:T(8,128)(2,1)}), bf16[8,128,768]{2,1,0:T(8,128)(2,1)S(1)}, u32[]{:S(2)}, u32[]{:S(2)}) async-start(bf16[8,128,768]{2,1,0:T(8,128)(2,1)} %bitcast.61), calls=%async_computation.2 | async-start | bytes 3145728 | tf_op jit(solution)/shard_map/all_to_all | solution.py:971
  190.7 42.4 %collective-permute-start.32 = (bf16[4,4,48,768]{3,2,1,0:T(8,128)(2,1)}, bf16[4,4,48,768]{3,2,1,0:T(8,128)(2,1)S(1)}, u32[]{:S(2)}, u32[]{:S(2)}) collective-permute-start(bf16[4,4,48,768]{3,2,1,0:T(8,128)(2,1)} %get-tuple-element.210), channel_id=1, source_target_pairs={{0,4},{4,0},{8,12},{12,8},{16,20},{20,16},{24,28},{28,24},{1,5},{5... | collective-permute-start | bytes 3538952 | tf_op jit(solution)/shard_map/ppermute | solution.py:943
  197.4 28.3 %collective-permute-start.30 = (bf16[2,4,96,768]{3,2,1,0:T(8,128)(2,1)}, bf16[2,4,96,768]{3,2,1,0:T(8,128)(2,1)S(1)}, u32[]{:S(2)}, u32[]{:S(2)}) collective-permute-start(bf16[2,4,96,768]{3,2,1,0:T(8,128)(2,1)} %get-tuple-element.204), channel_id=1, source_target_pairs={{0,8},{4,12},{8,0},{12,4},{16,24},{20,28},{24,16},{28,20},{1,9},{5... | collective-permute-start | bytes 3538952 | tf_op jit(solution)/shard_map/ppermute | solution.py:943
  199.0 27.3 %collective-permute-start.31 = (bf16[2,4,96,768]{3,2,1,0:T(8,128)(2,1)}, bf16[2,4,96,768]{3,2,1,0:T(8,128)(2,1)S(1)}, u32[]{:S(2)}, u32[]{:S(2)}) collective-permute-start(bf16[2,4,96,768]{3,2,1,0:T(8,128)(2,1)} %get-tuple-element.206), channel_id=1, source_target_pairs={{0,16},{4,20},{8,24},{12,28},{16,0},{20,4},{24,8},{28,12},{1,17},{... | collective-permute-start | bytes 3538952 | tf_op jit(solution)/shard_map/ppermute | solution.py:943
  224.9 8.3 %collective-permute-start.33 = (bf16[4,4,48,768]{3,2,1,0:T(8,128)(2,1)}, bf16[4,4,48,768]{3,2,1,0:T(8,128)(2,1)S(1)}, u32[]{:S(2)}, u32[]{:S(2)}) collective-permute-start(bf16[4,4,48,768]{3,2,1,0:T(8,128)(2,1)} %get-tuple-element.211), channel_id=1, source_target_pairs={{0,4},{4,0},{8,12},{12,8},{16,20},{20,16},{24,28},{28,24},{1,5},{5... | collective-permute-start | bytes 3538952 | tf_op jit(solution)/shard_map/ppermute | solution.py:943
  231.2 20.8 %collective-permute-start.37 = (bf16[4,96,768]{2,1,0:T(8,128)(2,1)}, bf16[4,96,768]{2,1,0:T(8,128)(2,1)S(1)}, u32[]{:S(2)}, u32[]{:S(2)}) collective-permute-start(bf16[4,96,768]{2,1,0:T(8,128)(2,1)} %get-tuple-element.223), channel_id=1, source_target_pairs={{0,16},{4,20},{8,24},{12,28},{16,0},{20,4},{24,8},{28,12},{1,17},{... | collective-permute-start | bytes 1769480 | tf_op jit(solution)/shard_map/ppermute | solution.py:943
  232.4 19.5 %collective-permute-start.38 = (bf16[4,96,768]{2,1,0:T(8,128)(2,1)}, bf16[4,96,768]{2,1,0:T(8,128)(2,1)S(1)}, u32[]{:S(2)}, u32[]{:S(2)}) collective-permute-start(bf16[4,96,768]{2,1,0:T(8,128)(2,1)} %get-tuple-element.225), channel_id=1, source_target_pairs={{0,8},{4,12},{8,0},{12,4},{16,24},{20,28},{24,16},{28,20},{1,9},{5... | collective-permute-start | bytes 1769480 | tf_op jit(solution)/shard_map/ppermute | solution.py:943
  239.1 19.5 %collective-permute-start.34 = (bf16[384,768]{1,0:T(8,128)(2,1)}, bf16[384,768]{1,0:T(8,128)(2,1)S(1)}, u32[]{:S(2)}, u32[]{:S(2)}) collective-permute-start(bf16[384,768]{1,0:T(8,128)(2,1)} %get-tuple-element.218), channel_id=1, source_target_pairs={{0,8},{4,12},{8,0},{12,4},{16,24},{20,28},{24,16},{28,20},{1,9},{5... | collective-permute-start | bytes 1769480 | tf_op jit(solution)/shard_map/ppermute | solution.py:943
  239.8 19.7 %collective-permute-start.35 = (bf16[384,768]{1,0:T(8,128)(2,1)}, bf16[384,768]{1,0:T(8,128)(2,1)S(1)}, u32[]{:S(2)}, u32[]{:S(2)}) collective-permute-start(bf16[384,768]{1,0:T(8,128)(2,1)} %get-tuple-element.219), channel_id=1, source_target_pairs={{0,16},{4,20},{8,24},{12,28},{16,0},{20,4},{24,8},{28,12},{1,17},{... | collective-permute-start | bytes 1769480 | tf_op jit(solution)/shard_map/ppermute | solution.py:943
  240.0 31.1 %collective-permute-start.36 = (bf16[384,768]{1,0:T(8,128)(2,1)}, bf16[384,768]{1,0:T(8,128)(2,1)S(1)}, u32[]{:S(2)}, u32[]{:S(2)}) collective-permute-start(bf16[384,768]{1,0:T(8,128)(2,1)} %get-tuple-element.220), channel_id=1, source_target_pairs={{0,24},{4,28},{8,16},{12,20},{16,8},{20,12},{24,0},{28,4},{1,25},{... | collective-permute-start | bytes 1769480 | tf_op jit(solution)/shard_map/ppermute | solution.py:943
  255.6 15.4 %collective-permute-start.39 = (bf16[2,96,768]{2,1,0:T(8,128)(2,1)}, bf16[2,96,768]{2,1,0:T(8,128)(2,1)S(1)}, u32[]{:S(2)}, u32[]{:S(2)}) collective-permute-start(bf16[2,96,768]{2,1,0:T(8,128)(2,1)} %get-tuple-element.227), channel_id=1, source_target_pairs={{0,1},{1,0},{2,3},{3,2},{4,5},{5,4},{6,7},{7,6},{8,9},{9,8},{10,11... | collective-permute-start | bytes 884744 | tf_op jit(solution)/shard_map/ppermute | solution.py:943
  257.0 14.0 %collective-permute-start.40 = (bf16[2,96,768]{2,1,0:T(8,128)(2,1)}, bf16[2,96,768]{2,1,0:T(8,128)(2,1)S(1)}, u32[]{:S(2)}, u32[]{:S(2)}) collective-permute-start(bf16[2,96,768]{2,1,0:T(8,128)(2,1)} %get-tuple-element.228), channel_id=1, source_target_pairs={{0,2},{1,3},{2,0},{3,1},{4,6},{5,7},{6,4},{7,5},{8,10},{9,11},{10,... | collective-permute-start | bytes 884744 | tf_op jit(solution)/shard_map/ppermute | solution.py:943
  258.6 23.8 %collective-permute-start.47 = (bf16[2,96,768]{2,1,0:T(8,128)(2,1)}, bf16[2,96,768]{2,1,0:T(8,128)(2,1)S(1)}, u32[]{:S(2)}, u32[]{:S(2)}) collective-permute-start(bf16[2,96,768]{2,1,0:T(8,128)(2,1)} %get-tuple-element.243), channel_id=1, source_target_pairs={{0,3},{1,2},{2,1},{3,0},{4,7},{5,6},{6,5},{7,4},{8,11},{9,10},{10,... | collective-permute-start | bytes 884744 | tf_op jit(solution)/shard_map/ppermute | solution.py:943
  283.4 16.9 %collective-permute-start.43 = (bf16[112,768]{1,0:T(8,128)(2,1)}, bf16[112,768]{1,0:T(8,128)(2,1)S(1)}, u32[]{:S(2)}, u32[]{:S(2)}) collective-permute-start(bf16[112,768]{1,0:T(8,128)(2,1)} %get-tuple-element.238), channel_id=1, source_target_pairs={{0,3},{1,2},{2,1},{3,0},{4,7},{5,6},{6,5},{7,4},{8,11},{9,10},{10,... | collective-permute-start | bytes 516104 | tf_op jit(solution)/shard_map/ppermute | solution.py:943
  285.2 15.2 %collective-permute-start.50 = (bf16[2,96,768]{2,1,0:T(8,128)(2,1)S(1)}, bf16[2,96,768]{2,1,0:T(8,128)(2,1)S(1)}, u32[]{:S(2)}, u32[]{:S(2)}) collective-permute-start(bf16[2,96,768]{2,1,0:T(8,128)(2,1)S(1)} %add_convert_fusion.refs_0_), channel_id=1, source_target_pairs={{0,24},{4,28},{8,16},{12,20},{16,8},{20,12},{24,0},{28,4},{1,25},{... | collective-permute-start | bytes 884744 | tf_op jit(solution)/shard_map/ppermute | solution.py:943
  285.9 14.5 %collective-permute-start.49 = (bf16[2,96,768]{2,1,0:T(8,128)(2,1)S(1)}, bf16[2,96,768]{2,1,0:T(8,128)(2,1)S(1)}, u32[]{:S(2)}, u32[]{:S(2)}) collective-permute-start(bf16[2,96,768]{2,1,0:T(8,128)(2,1)S(1)} %add_convert_fusion.refs_0_), channel_id=1, source_target_pairs={{0,16},{4,20},{8,24},{12,28},{16,0},{20,4},{24,8},{28,12},{1,17},{... | collective-permute-start | bytes 884744 | tf_op jit(solution)/shard_map/ppermute | solution.py:943
  287.2 13.2 %collective-permute-start.48 = (bf16[2,96,768]{2,1,0:T(8,128)(2,1)S(1)}, bf16[2,96,768]{2,1,0:T(8,128)(2,1)S(1)}, u32[]{:S(2)}, u32[]{:S(2)}) collective-permute-start(bf16[2,96,768]{2,1,0:T(8,128)(2,1)S(1)} %add_convert_fusion.refs_0_), channel_id=1, source_target_pairs={{0,8},{4,12},{8,0},{12,4},{16,24},{20,28},{24,16},{28,20},{1,9},{5... | collective-permute-start | bytes 884744 | tf_op jit(solution)/shard_map/ppermute | solution.py:943
  302.5 12.8 %collective-permute-start.46 = (bf16[112,768]{1,0:T(8,128)(2,1)S(1)}, bf16[112,768]{1,0:T(8,128)(2,1)S(1)}, u32[]{:S(2)}, u32[]{:S(2)}) collective-permute-start(bf16[112,768]{1,0:T(8,128)(2,1)S(1)} %add_convert_fusion.1), channel_id=1, source_target_pairs={{0,24},{4,28},{8,16},{12,20},{16,8},{20,12},{24,0},{28,4},{1,25},{... | collective-permute-start | bytes 516104 | tf_op jit(solution)/shard_map/ppermute | solution.py:943
  303.3 12.0 %collective-permute-start.45 = (bf16[112,768]{1,0:T(8,128)(2,1)S(1)}, bf16[112,768]{1,0:T(8,128)(2,1)S(1)}, u32[]{:S(2)}, u32[]{:S(2)}) collective-permute-start(bf16[112,768]{1,0:T(8,128)(2,1)S(1)} %add_convert_fusion.1), channel_id=1, source_target_pairs={{0,16},{4,20},{8,24},{12,28},{16,0},{20,4},{24,8},{28,12},{1,17},{... | collective-permute-start | bytes 516104 | tf_op jit(solution)/shard_map/ppermute | solution.py:943
  304.4 10.9 %collective-permute-start.44 = (bf16[112,768]{1,0:T(8,128)(2,1)S(1)}, bf16[112,768]{1,0:T(8,128)(2,1)S(1)}, u32[]{:S(2)}, u32[]{:S(2)}) collective-permute-start(bf16[112,768]{1,0:T(8,128)(2,1)S(1)} %add_convert_fusion.1), channel_id=1, source_target_pairs={{0,8},{4,12},{8,0},{12,4},{16,24},{20,28},{24,16},{28,20},{1,9},{5... | collective-permute-start | bytes 516104 | tf_op jit(solution)/shard_map/ppermute | solution.py:943
  316.7 25.1 %all-to-all-start.3 = ((bf16[8,128,768]{2,1,0:T(8,128)(2,1)}), bf16[8,128,768]{2,1,0:T(8,128)(2,1)S(1)}, u32[]{:S(2)}, u32[]{:S(2)}) async-start(bf16[8,128,768]{2,1,0:T(8,128)(2,1)} %bitcast.27), calls=%async_computation.3 | async-start | bytes 3145728 | tf_op jit(solution)/shard_map/all_to_all | solution.py:971
  (70 other events, 453.6 us)

commit v2 on v1

--- a/solution.py
+++ b/solution.py
@@ -1132,13 +1132,13 @@
         pieces = [attn_low] + spread_pairs(attn_chips)
         grad_low = exchange(after(out_grad, first_here), packs, rows)
         grad_low = grad_low.reshape(packs * rows, width)
-        up_here = after(up_here, *attn_chips)
-        up_x, up_y = swap(up_here, "seq", 2), swap(up_here, "seq", 4)
         down_steps = hid_terms([after(down_own, *attn_chips)] * hids)[1:]
 
         whole_attn, first_low, queries, keys, values = project(
             place, tokens, vector_params, pieces, None
         )
+        up_here = after(up_here, queries)
+        up_x, up_y = swap(up_here, "seq", 2), swap(up_here, "seq", 4)
         down_here = jnp.stack(after(down_steps, queries))
         down_x, down_y = swap(down_here, "seq", 2), swap(down_here, "seq", 4)
         queries = after(queries, down_here)

time: 350 us -> 350 us (level)
  no operation moved by 1% of the time
where the time goes in v2:
time: 350 us; the launch traced here: 344 us
  Pallas kernels  188 us (54%)
  starting transfers between devices  71.4 us (20%)
  waiting for transfers between devices  55.3 us (16%)
  local copies, waits for them, and re-layouts  14.5 us (4%)
  other arithmetic  13.3 us (4%)
    ppermute x59, waiting for transfers between devices, swap(): return lax.ppermute(value, axis, [(i, i ^ step) for i in range(count)])  55.2 us
    ppermute x59, starting transfers between devices, swap(): return lax.ppermute(value, axis, [(i, i ^ step) for i in range(count)])  53.4 us
    pallas_call x2, Pallas kernels, attention_grads(): pl.pallas_call(functools.partial(attention_grads_kernel, min(256, rows),...  49.1 us
    pallas_call x1, Pallas kernels, mlp_rows(): pl.pallas_call(functools.partial(mlp_rows_kernel, count, steps), grid_spe...  45.6 us
    pallas_call x3, Pallas kernels, renew_pieces(): pl.pallas_call(functools.partial(renew_kernel, len(pieces), parts, turned...  26 us
    pallas_call x2, Pallas kernels, attention_forward(): pl.pallas_call(functools.partial(attention_forward_kernel, min(128, rows)...  23.2 us
    all_to_all x4, starting transfers between devices, exchange(): return lax.all_to_all(array, 'seq', 0, 0, axis_index_groups=teams)  18 us
    pallas_call x1, Pallas kernels, input_back(): pl.pallas_call(input_back_kernel, grid=(rows // tile,), in_specs=[strip,...  10.2 us
  transfers between devices with their start and end apart: 63, of which 15 were waited for; matrix products, arithmetic and copies ran while one was open for 5% of the time, Pallas kernels for 41%

profile of v2, /device:TPU:9, one launch (start us, length us, event | category | flops | bytes accessed | tf_op | source)
XLA Modules:
  0.0 344.5 jit_solution(4494657992116654684)
XLA Ops:
  0.7 5.0 %all-to-all-start = ((bf16[8,128,768]{2,1,0:T(8,128)(2,1)}), bf16[8,128,768]{2,1,0:T(8,128)(2,1)}, u32[]{:S(2)}, u32[]{:S(2)}) async-start(bf16[8,128,768]{2,1,0:T(8,128)(2,1)} %param.12), calls=%async_computation | async-start | bytes 3145728 | tf_op jit(solution)/shard_map/all_to_all | solution.py:971
  5.8 1.4 collective-permute-start.2
  10.8 2.6 fusion.6
  14.1 12.8 %collective-permute-done.2 = bf16[4,48,768]{2,1,0:T(8,128)(2,1)S(1)} collective-permute-done((bf16[4,48,768]{2,1,0:T(8,128)(2,1)S(1)}, bf16[4,48,768]{2,1,0:T(8,128)(2,1)S(1)}, u32[]{:S(2)}, u32[]{:S(2)}) %collective-permute-start.2) | collective-permute-done | bytes 294944 | tf_op jit(solution)/shard_map/ppermute | solution.py:943
  26.9 5.4 %collective-permute-done.1 = bf16[4,48,768]{2,1,0:T(8,128)(2,1)S(1)} collective-permute-done((bf16[4,48,768]{2,1,0:T(8,128)(2,1)S(1)}, bf16[4,48,768]{2,1,0:T(8,128)(2,1)S(1)}, u32[]{:S(2)}, u32[]{:S(2)}) %collective-permute-start.1) | collective-permute-done | bytes 294944 | tf_op jit(solution)/shard_map/ppermute | solution.py:943
  33.8 1.3 collective-permute-start.4
  35.3 4.0 %collective-permute-start.6 = (bf16[96,768]{1,0:T(8,128)(2,1)S(1)}, bf16[96,768]{1,0:T(8,128)(2,1)S(1)}, u32[]{:S(2)}, u32[]{:S(2)}) collective-permute-start(bf16[96,768]{1,0:T(8,128)(2,1)S(1)} %get-tuple-element.151), channel_id=1, source_target_pairs={{0,2},{1,3},{2,0},{3,1},{4,6},{5,7},{6,4},{7,5},{8,10},{9,11},{10,... | collective-permute-start | bytes 442376 | tf_op jit(solution)/shard_map/ppermute | solution.py:943
  40.0 4.0 %convert_element_type.109.refs_8_ = bf16[2,768,768]{2,1,0:T(8,128)(2,1)} convert(f32[2,768,768]{2,1,0:T(8,128)} %refs_8_.3) | non-fusion elementwise | flops 1179648 | bytes 7077888 | tf_op jit(solution)/shard_map/convert_element_type | solution.py:1127
  44.6 1.5 fusion.valid_ref.refs_4_
  46.1 2.9 collective-permute-done.6
  49.1 1.6 collective-permute-start.8
  53.0 4.2 %all-to-all-start.1 = ((bf16[8,128,768]{2,1,0:T(8,128)(2,1)}), bf16[8,128,768]{2,1,0:T(8,128)(2,1)S(1)}, u32[]{:S(2)}, u32[]{:S(2)}) async-start(bf16[8,128,768]{2,1,0:T(8,128)(2,1)} %param.23), calls=%async_computation.1 | async-start | bytes 3145728 | tf_op jit(solution)/shard_map/all_to_all | solution.py:971
  57.5 4.0 %collective-permute-start.13 = (bf16[96,768]{1,0:T(8,128)(2,1)S(1)}, bf16[96,768]{1,0:T(8,128)(2,1)S(1)}, u32[]{:S(2)}, u32[]{:S(2)}) collective-permute-start(bf16[96,768]{1,0:T(8,128)(2,1)S(1)} %copy-done.19), channel_id=1, source_target_pairs={{0,2},{1,3},{2,0},{3,1},{4,6},{5,7},{6,4},{7,5},{8,10},{9,11},{10,... | collective-permute-start | bytes 442376 | tf_op jit(solution)/shard_map/ppermute | solution.py:943
  61.6 9.4 %norm_and_project.1 = (bf16[3072,768]{1,0:T(8,128)(2,1)}, bf16[1024,768]{1,0:T(8,128)(2,1)}, bf16[1024,768]{1,0:T(8,128)(2,1)}, bf16[1024,768]{1,0:T(8,128)(2,1)}, bf16[1024,768]{1,0:T(8,128)(2,1)}) custom-call(s32[2]{0:T(128)} %pad_add_fusion.place, bf16[1024,768]{1,0:T(8,128)(2,1)} %bitcast.2.x_ref, f32[12,768]{1,0:T(8,128)} %vec_ref.5, ...), custom_call_target="tpu_custom_call" | custom-call | flops 4000001024 | bytes 1000 | tf_op jit(solution)/shard_map/norm_and_project/pallas_call | solution.py:444
  71.0 1.5 collective-permute-start.23
  74.0 11.6 %attention_forward.2 = (bf16[1024,768]{1,0:T(8,128)(2,1)}, f32[6,2,1024]{2,1,0:T(2,128)}) custom-call(bf16[1024,768]{1,0:T(8,128)(2,1)} %get-tuple-element.161.q_ref.refs_0_, bf16[1024,768]{1,0:T(8,128)(2,1)} %get-tuple-element.162.k_ref.refs_1_, bf16[1024,768]{1,0:T(8,128)(2,1)} %get-tuple-element.163.v_ref.refs_2_, s32[1024,1]{1,0:T(8,128)} %copy.43.query_seg.refs_7_, ...), custom_call_target="tpu_custom_call" | custom-call | flops 4800001024 | bytes 1000 | tf_op jit(solution)/shard_map/attention_forward/pallas_call | solution.py:106
  85.6 11.6 %attention_forward.3 = (bf16[1024,768]{1,0:T(8,128)(2,1)}, f32[6,2,1024]{2,1,0:T(2,128)}) custom-call(bf16[1024,768]{1,0:T(8,128)(2,1)} %get-tuple-element.161.q_ref.refs_0_, bf16[1024,768]{1,0:T(8,128)(2,1)} %get-tuple-element.162.k_ref.refs_1_, bf16[1024,768]{1,0:T(8,128)(2,1)} %get-tuple-element.163.v_ref.refs_2_, ...), custom_call_target="tpu_custom_call", output_to_operand_aliasing={{0}: (6, {}), {1}: (7, {})} | custom-call | flops 4800001024 | bytes 1000 | tf_op jit(solution)/shard_map/attention_forward/pallas_call | solution.py:106
  97.3 1.4 collective-permute-start.27
  100.0 2.7 collective-permute-start.17
  103.1 5.3 %join_and_norm.1 = (f32[1024,768]{1,0:T(8,128)}, bf16[1024,768]{1,0:T(8,128)(2,1)}) custom-call(bf16[1024,768]{1,0:T(8,128)(2,1)} %get-tuple-element.166.o_ref.refs_3_.refs_10_, bf16[1024,768]{1,0:T(8,128)(2,1)} %bitcast.2.x_ref, bf16[3072,768]{1,0:T(8,128)(2,1)} %get-tuple-element.167.w_ref.refs_5_, f32[12,768]{1,0:T(8,128)} %vec_ref.5), custom_call_target="tpu_custom_call" | custom-call | flops 2400001024 | bytes 1000 | tf_op jit(solution)/shard_map/join_and_norm/pallas_call | solution.py:471
  108.5 1.6 collective-permute-start.24
  110.1 1.4 collective-permute-start.25
  115.3 45.6 %mlp_both_ways.1 = (bf16[1024,768]{1,0:T(8,128)(2,1)}, f32[1024,768]{1,0:T(8,128)}, bf16[1024,768]{1,0:T(8,128)(2,1)}, bf16[1024,768]{1,0:T(8,128)(2,1)}, f32[6,...) custom-call(s32[2]{0:T(128)} %pad_add_fusion.place, ...), custom_call_target="tpu_custom_call" | custom-call | flops 14400001024 | bytes 1000 | tf_op jit(solution)/shard_map/mlp_both_ways/pallas_call | solution.py:670
  161.3 4.1 %all-to-all-start.2 = ((bf16[8,128,768]{2,1,0:T(8,128)(2,1)}), bf16[8,128,768]{2,1,0:T(8,128)(2,1)S(1)}, u32[]{:S(2)}, u32[]{:S(2)}) async-start(bf16[8,128,768]{2,1,0:T(8,128)(2,1)} %bitcast.61), calls=%async_computation.2 | async-start | bytes 3145728 | tf_op jit(solution)/shard_map/all_to_all | solution.py:971
  165.4 24.5 %attention_backward.2 = (bf16[1024,768]{1,0:T(8,128)(2,1)}, bf16[1024,768]{1,0:T(8,128)(2,1)}, bf16[1024,768]{1,0:T(8,128)(2,1)}, bf16[4,4,48,768]{3,2,1,0:T(8,128)(2,1)}, bf16[4,4,48,768]{3,2,1,0:T(8,128)(2,1)}) custom-call(s32[2]{0:T(128)} %pad_add_fusion.place, bf16[1024,768]{1,0:T(8,128)(2,1)} %get-tuple-element.161.q_ref.refs_0_, ...), custom_call_target="tpu_custom_call" | custom-call | flops 8400001024 | bytes 1000 | tf_op jit(solution)/shard_map/attention_backward/pallas_call | solution.py:252
  190.0 6.5 %fold_cores.2 = (bf16[2,4,96,768]{3,2,1,0:T(8,128)(2,1)}, bf16[2,4,96,768]{3,2,1,0:T(8,128)(2,1)}, bf16[2,4,96,768]{3,2,1,0:T(8,128)(2,1)}, bf16[2,4,96,768]{3,2,1,0:T(8,128)(2,1)}) custom-call(bf16[4,4,2,96,768]{4,3,2,1,0:T(8,128)(2,1)} %get-tuple-element.193.even_ref, bf16[4,4,2,96,768]{4,3,2,1,0:T(8,128)(2,1)} %collective-permute-done.29.other_ref), custom_call_target="tpu_custom_call" | custom-call | flops 1600001024 | bytes 1000 | tf_op jit(solution)/shard_map/fold_cores/pallas_call | solution.py:830
  196.5 1.6 collective-permute-start.30
  199.4 24.6 %attention_backward.3 = (bf16[1024,768]{1,0:T(8,128)(2,1)}, bf16[1024,768]{1,0:T(8,128)(2,1)}, bf16[1024,768]{1,0:T(8,128)(2,1)}, bf16[4,4,48,768]{3,2,1,0:T(8,128)(2,1)}, bf16[4,4,48,768]{3,2,1,0:T(8,128)(2,1)}) custom-call(s32[2]{0:T(128)} %pad_add_fusion.place, ...), custom_call_target="tpu_custom_call", output_to_operand_aliasing={{0}: (12, {}), {1}: (13, {}), {2}: (14, {})} | custom-call | flops 8400001024 | bytes 1000 | tf_op jit(solution)/shard_map/attention_backward/pallas_call | solution.py:252
  226.4 3.9 %fold_chips.1 = (bf16[4,96,768]{2,1,0:T(8,128)(2,1)}, bf16[4,96,768]{2,1,0:T(8,128)(2,1)}, bf16[4,96,768]{2,1,0:T(8,128)(2,1)}, bf16[4,96,768]{2,1,0:T(8,128)(2,1)}) custom-call(bf16[2,4,96,768]{3,2,1,0:T(8,128)(2,1)} %get-tuple-element.203.up, bf16[2,4,96,768]{3,2,1,0:T(8,128)(2,1)} %copy-done.37, bf16[2,4,96,768]{3,2,1,0:T(8,128)(2,1)} %get-tuple-element.205.down, ...), custom_call_target="tpu_custom_call" | custom-call | flops 1600001024 | bytes 1000 | tf_op jit(solution)/shard_map/fold_chips/pallas_call | solution.py:851
  230.3 1.3 collective-permute-start.37
  234.3 3.9 %fold_cores.3 = (bf16[384,768]{1,0:T(8,128)(2,1)}, bf16[384,768]{1,0:T(8,128)(2,1)}, bf16[384,768]{1,0:T(8,128)(2,1)}, bf16[384,768]{1,0:T(8,128)(2,1)}) custom-call(bf16[4,4,48,768]{3,2,1,0:T(8,128)(2,1)} %get-tuple-element.208.refs_0_, bf16[4,4,48,768]{3,2,1,0:T(8,128)(2,1)} %get-tuple-element.209.refs_1_, bf16[4,4,48,768]{3,2,1,0:T(8,128)(2,1)} %copy-done.36, ...), custom_call_target="tpu_custom_call" | custom-call | flops 1600001024 | bytes 1000 | tf_op jit(solution)/shard_map/fold_cores/pallas_call | solution.py:895
  239.2 1.7 collective-permute-start.36
  240.9 10.2 %input_backward.1 = (bf16[1024,768]{1,0:T(8,128)(2,1)}, f32[8,768]{1,0:T(8,128)}) custom-call(bf16[1024,768]{1,0:T(8,128)(2,1)} %get-tuple-element.213.dq_ref, bf16[1024,768]{1,0:T(8,128)(2,1)} %get-tuple-element.214.dk_ref, bf16[1024,768]{1,0:T(8,128)(2,1)} %get-tuple-element.215.dv_ref, bf16[3072,768]{1,0:T(8,128)(2,1)} %get-tuple-element.167.w_ref.refs_5_, ...), custom_call_target="tpu_custom_call" | custom-call | flops 4000001024 | bytes 1000 | tf_op jit(solution)/shard_map/input_backward/pallas_call | solution.py:734
  252.1 2.7 fold_last.1
  254.8 2.6 collective-permute-start.39
  259.3 10.9 %collective-permute-done.36.refs_3_ = bf16[384,768]{1,0:T(8,128)(2,1)S(1)} collective-permute-done((bf16[384,768]{1,0:T(8,128)(2,1)}, bf16[384,768]{1,0:T(8,128)(2,1)S(1)}, u32[]{:S(2)}, u32[]{:S(2)}) %collective-permute-start.36) | collective-permute-done | bytes 589856 | tf_op jit(solution)/shard_map/ppermute | solution.py:943
  271.0 2.6 sum_steps.1
  273.6 9.2 %collective-permute-done.47 = bf16[2,96,768]{2,1,0:T(8,128)(2,1)S(1)} collective-permute-done((bf16[2,96,768]{2,1,0:T(8,128)(2,1)}, bf16[2,96,768]{2,1,0:T(8,128)(2,1)S(1)}, u32[]{:S(2)}, u32[]{:S(2)}) %collective-permute-start.47) | collective-permute-done | bytes 294944 | tf_op jit(solution)/shard_map/ppermute | solution.py:943
  284.0 1.4 collective-permute-start.43
  286.4 1.3 collective-permute-start.49
  288.4 1.9 convert_element_type.112
  290.3 10.2 %collective-permute-done.43 = bf16[112,768]{1,0:T(8,128)(2,1)S(1)} collective-permute-done((bf16[112,768]{1,0:T(8,128)(2,1)}, bf16[112,768]{1,0:T(8,128)(2,1)S(1)}, u32[]{:S(2)}, u32[]{:S(2)}) %collective-permute-start.43) | collective-permute-done | bytes 172064 | tf_op jit(solution)/shard_map/ppermute | solution.py:943
  300.7 1.7 collective-permute-start.51
  307.1 8.7 %renew_matrices.3 = (f32[2,768,768]{2,1,0:T(8,128)}, f32[2,768,768]{2,1,0:T(8,128)}, f32[2,768,768]{2,1,0:T(8,128)}, f32[2,768,768]{2,1,0:T(8,128)}) custom-call(s32[2]{0:T(128)} %pad_add_fusion.place, bf16[2,96,768]{2,1,0:T(8,128)(2,1)} %copy-done.3, bf16[2,96,768]{2,1,0:T(8,128)(2,1)} %copy-done.8, bf16[2,96,768]{2,1,0:T(8,128)(2,1)} %copy-done.7, ...), custom_call_target="tpu_custom_call" | custom-call | flops 4000001024 | bytes 1000 | tf_op jit(solution)/shard_map/renew_matrices/pallas_call | solution.py:797
  317.1 4.8 %all-to-all-start.3 = ((bf16[8,128,768]{2,1,0:T(8,128)(2,1)}), bf16[8,128,768]{2,1,0:T(8,128)(2,1)S(1)}, u32[]{:S(2)}, u32[]{:S(2)}) async-start(bf16[8,128,768]{2,1,0:T(8,128)(2,1)} %bitcast.27), calls=%async_computation.3 | async-start | bytes 3145728 | tf_op jit(solution)/shard_map/all_to_all | solution.py:971
  321.9 8.9 %renew_matrices.4 = (f32[2,768,768]{2,1,0:T(8,128)}, f32[2,768,768]{2,1,0:T(8,128)}, f32[2,768,768]{2,1,0:T(8,128)}, f32[2,768,768]{2,1,0:T(8,128)}) custom-call(s32[2]{0:T(128)} %pad_add_fusion.place, bf16[2,96,768]{2,1,0:T(8,128)(2,1)} %copy-done.3, ...), custom_call_target="tpu_custom_call", output_to_operand_aliasing={{0}: (12, {}), {1}: (13, {}), {2}: (14, {}), {3}: (15, {})} | custom-call | flops 4000001024 | bytes 1000 | tf_op jit(solution)/shard_map/renew_matrices/pallas_call | solution.py:797
  333.8 8.4 %renew_matrices.5 = (f32[1,768,768]{2,1,0:T(8,128)}, f32[1,768,768]{2,1,0:T(8,128)}, f32[1,768,768]{2,1,0:T(8,128)}, f32[1,768,768]{2,1,0:T(8,128)}) custom-call(s32[2]{0:T(128)} %pad_add_fusion.place, bf16[1,112,768]{2,1,0:T(8,128)(2,1)} %bitcast.62, bf16[1,112,768]{2,1,0:T(8,128)(2,1)} %bitcast.78, bf16[1,112,768]{2,1,0:T(8,128)(2,1)} %bitcast.77, ...), custom_call_target="tpu_custom_call" | custom-call | flops 4000001024 | bytes 1000 | tf_op jit(solution)/shard_map/renew_matrices/pallas_call | solution.py:797
  342.3 1.9 convert_element_type.123
  (242 shorter events, 40.7 us)
Async XLA Ops:
  0.7 31.7 %all-to-all-start = ((bf16[8,128,768]{2,1,0:T(8,128)(2,1)}), bf16[8,128,768]{2,1,0:T(8,128)(2,1)}, u32[]{:S(2)}, u32[]{:S(2)}) async-start(bf16[8,128,768]{2,1,0:T(8,128)(2,1)} %param.12), calls=%async_computation | async-start | bytes 3145728 | tf_op jit(solution)/shard_map/all_to_all | solution.py:971
  5.8 21.2 %collective-permute-start.2 = (bf16[4,48,768]{2,1,0:T(8,128)(2,1)S(1)}, bf16[4,48,768]{2,1,0:T(8,128)(2,1)S(1)}, u32[]{:S(2)}, u32[]{:S(2)}) collective-permute-start(bf16[4,48,768]{2,1,0:T(8,128)(2,1)S(1)} %pad_maximum_fusion.4), channel_id=1, source_target_pairs={{0,3},{1,2},{2,1},{3,0},{4,7},{5,6},{6,5},{7,4},{8,11},{9,10},{10,... | collective-permute-start | bytes 884744 | tf_op jit(solution)/shard_map/ppermute | solution.py:943
  7.1 25.2 %collective-permute-start.1 = (bf16[4,48,768]{2,1,0:T(8,128)(2,1)S(1)}, bf16[4,48,768]{2,1,0:T(8,128)(2,1)S(1)}, u32[]{:S(2)}, u32[]{:S(2)}) collective-permute-start(bf16[4,48,768]{2,1,0:T(8,128)(2,1)S(1)} %pad_maximum_fusion.4), channel_id=1, source_target_pairs={{0,2},{1,3},{2,0},{3,1},{4,6},{5,7},{6,4},{7,5},{8,10},{9,11},{10,... | collective-permute-start | bytes 884744 | tf_op jit(solution)/shard_map/ppermute | solution.py:943
  8.2 24.1 %collective-permute-start = (bf16[4,48,768]{2,1,0:T(8,128)(2,1)S(1)}, bf16[4,48,768]{2,1,0:T(8,128)(2,1)S(1)}, u32[]{:S(2)}, u32[]{:S(2)}) collective-permute-start(bf16[4,48,768]{2,1,0:T(8,128)(2,1)S(1)} %pad_maximum_fusion.4), channel_id=1, source_target_pairs={{0,1},{1,0},{2,3},{3,2},{4,5},{5,4},{6,7},{7,6},{8,9},{9,8},{10,11... | collective-permute-start | bytes 884744 | tf_op jit(solution)/shard_map/ppermute | solution.py:943
  32.5 16.6 %collective-permute-start.3 = (bf16[3,2,48,768]{3,2,1,0:T(8,128)(2,1)S(1)}, bf16[3,2,48,768]{3,2,1,0:T(8,128)(2,1)S(1)}, u32[]{:S(2)}, u32[]{:S(2)}) collective-permute-start(bf16[3,2,48,768]{3,2,1,0:T(8,128)(2,1)S(1)} %pad_maximum_fusion.refs_1_), channel_id=1, source_target_pairs={{0,8},{4,12},{8,0},{12,4},{16,24},{20,28},{24,16},{28,20},{1,9},{5... | collective-permute-start | bytes 1327112 | tf_op jit(solution)/shard_map/ppermute | solution.py:943
  33.8 15.3 %collective-permute-start.4 = (bf16[3,2,48,768]{3,2,1,0:T(8,128)(2,1)S(1)}, bf16[3,2,48,768]{3,2,1,0:T(8,128)(2,1)}, u32[]{:S(2)}, u32[]{:S(2)}) collective-permute-start(bf16[3,2,48,768]{3,2,1,0:T(8,128)(2,1)S(1)} %pad_maximum_fusion.1.refs_5_), channel_id=1, source_target_pairs={{0,16},{4,20},{8,24},{12,28},{16,0},{20,4},{24,8},{28,12},{1,17},{... | collective-permute-start | bytes 1327112 | tf_op jit(solution)/shard_map/ppermute | solution.py:943
  35.1 11.1 %collective-permute-start.7 = (bf16[96,768]{1,0:T(8,128)(2,1)S(1)}, bf16[96,768]{1,0:T(8,128)(2,1)S(1)}, u32[]{:S(2)}, u32[]{:S(2)}) collective-permute-start(bf16[96,768]{1,0:T(8,128)(2,1)S(1)} %get-tuple-element.151), channel_id=1, source_target_pairs={{0,3},{1,2},{2,1},{3,0},{4,7},{5,6},{6,5},{7,4},{8,11},{9,10},{10,... | collective-permute-start | bytes 442376 | tf_op jit(solution)/shard_map/ppermute | solution.py:943
  35.3 13.8 %collective-permute-start.6 = (bf16[96,768]{1,0:T(8,128)(2,1)S(1)}, bf16[96,768]{1,0:T(8,128)(2,1)S(1)}, u32[]{:S(2)}, u32[]{:S(2)}) collective-permute-start(bf16[96,768]{1,0:T(8,128)(2,1)S(1)} %get-tuple-element.151), channel_id=1, source_target_pairs={{0,2},{1,3},{2,0},{3,1},{4,6},{5,7},{6,4},{7,5},{8,10},{9,11},{10,... | collective-permute-start | bytes 442376 | tf_op jit(solution)/shard_map/ppermute | solution.py:943
  39.3 9.8 %collective-permute-start.5 = (bf16[96,768]{1,0:T(8,128)(2,1)S(1)}, bf16[96,768]{1,0:T(8,128)(2,1)S(1)}, u32[]{:S(2)}, u32[]{:S(2)}) collective-permute-start(bf16[96,768]{1,0:T(8,128)(2,1)S(1)} %get-tuple-element.151), channel_id=1, source_target_pairs={{0,1},{1,0},{2,3},{3,2},{4,5},{5,4},{6,7},{7,6},{8,9},{9,8},{10,11... | collective-permute-start | bytes 442376 | tf_op jit(solution)/shard_map/ppermute | solution.py:943
  49.1 8.4 %collective-permute-start.8 = (bf16[3,2,48,768]{3,2,1,0:T(8,128)(2,1)S(1)}, bf16[3,2,48,768]{3,2,1,0:T(8,128)(2,1)}, u32[]{:S(2)}, u32[]{:S(2)}) collective-permute-start(bf16[3,2,48,768]{3,2,1,0:T(8,128)(2,1)S(1)} %pad_maximum_fusion.refs_1_), channel_id=1, source_target_pairs={{0,4},{4,0},{8,12},{12,8},{16,20},{20,16},{24,28},{28,24},{1,5},{5... | collective-permute-start | bytes 1327112 | tf_op jit(solution)/shard_map/ppermute | solution.py:943
  50.7 10.8 %collective-permute-start.9 = (bf16[3,2,48,768]{3,2,1,0:T(8,128)(2,1)S(1)}, bf16[3,2,48,768]{3,2,1,0:T(8,128)(2,1)}, u32[]{:S(2)}, u32[]{:S(2)}) collective-permute-start(bf16[3,2,48,768]{3,2,1,0:T(8,128)(2,1)S(1)} %collective-permute-done.3.refs_3_), channel_id=1, source_target_pairs={{0,4},{4,0},{8,12},{12,8},{16,20},{20,16},{24,28},{28,24},{1,5},{5... | collective-permute-start | bytes 1327112 | tf_op jit(solution)/shard_map/ppermute | solution.py:943
  50.8 10.8 %collective-permute-start.10 = (bf16[3,2,48,768]{3,2,1,0:T(8,128)(2,1)S(1)}, bf16[3,2,48,768]{3,2,1,0:T(8,128)(2,1)}, u32[]{:S(2)}, u32[]{:S(2)}) collective-permute-start(bf16[3,2,48,768]{3,2,1,0:T(8,128)(2,1)S(1)} %pad_maximum_fusion.1.refs_5_), channel_id=1, source_target_pairs={{0,4},{4,0},{8,12},{12,8},{16,20},{20,16},{24,28},{28,24},{1,5},{5... | collective-permute-start | bytes 1327112 | tf_op jit(solution)/shard_map/ppermute | solution.py:943
  51.2 10.3 %collective-permute-start.11 = (bf16[3,2,48,768]{3,2,1,0:T(8,128)(2,1)}, bf16[3,2,48,768]{3,2,1,0:T(8,128)(2,1)}, u32[]{:S(2)}, u32[]{:S(2)}) collective-permute-start(bf16[3,2,48,768]{3,2,1,0:T(8,128)(2,1)} %collective-permute-done.4.refs_7_), channel_id=1, source_target_pairs={{0,4},{4,0},{8,12},{12,8},{16,20},{20,16},{24,28},{28,24},{1,5},{5... | collective-permute-start | bytes 1327112 | tf_op jit(solution)/shard_map/ppermute | solution.py:943
  53.0 60.5 %all-to-all-start.1 = ((bf16[8,128,768]{2,1,0:T(8,128)(2,1)}), bf16[8,128,768]{2,1,0:T(8,128)(2,1)S(1)}, u32[]{:S(2)}, u32[]{:S(2)}) async-start(bf16[8,128,768]{2,1,0:T(8,128)(2,1)} %param.23), calls=%async_computation.1 | async-start | bytes 3145728 | tf_op jit(solution)/shard_map/all_to_all | solution.py:971
  57.3 13.7 %collective-permute-start.14 = (bf16[96,768]{1,0:T(8,128)(2,1)S(1)}, bf16[96,768]{1,0:T(8,128)(2,1)S(1)}, u32[]{:S(2)}, u32[]{:S(2)}) collective-permute-start(bf16[96,768]{1,0:T(8,128)(2,1)S(1)} %copy-done.19), channel_id=1, source_target_pairs={{0,3},{1,2},{2,1},{3,0},{4,7},{5,6},{6,5},{7,4},{8,11},{9,10},{10,... | collective-permute-start | bytes 442376 | tf_op jit(solution)/shard_map/ppermute | solution.py:943
  57.5 13.4 %collective-permute-start.13 = (bf16[96,768]{1,0:T(8,128)(2,1)S(1)}, bf16[96,768]{1,0:T(8,128)(2,1)S(1)}, u32[]{:S(2)}, u32[]{:S(2)}) collective-permute-start(bf16[96,768]{1,0:T(8,128)(2,1)S(1)} %copy-done.19), channel_id=1, source_target_pairs={{0,2},{1,3},{2,0},{3,1},{4,6},{5,7},{6,4},{7,5},{8,10},{9,11},{10,... | collective-permute-start | bytes 442376 | tf_op jit(solution)/shard_map/ppermute | solution.py:943
  61.5 9.4 %collective-permute-start.12 = (bf16[96,768]{1,0:T(8,128)(2,1)S(1)}, bf16[96,768]{1,0:T(8,128)(2,1)S(1)}, u32[]{:S(2)}, u32[]{:S(2)}) collective-permute-start(bf16[96,768]{1,0:T(8,128)(2,1)S(1)} %copy-done.19), channel_id=1, source_target_pairs={{0,1},{1,0},{2,3},{3,2},{4,5},{5,4},{6,7},{7,6},{8,9},{9,8},{10,11... | collective-permute-start | bytes 442376 | tf_op jit(solution)/shard_map/ppermute | solution.py:943
  71.0 26.3 %collective-permute-start.23 = (bf16[3,96,768]{2,1,0:T(8,128)(2,1)S(1)}, bf16[3,96,768]{2,1,0:T(8,128)(2,1)S(1)}, u32[]{:S(2)}, u32[]{:S(2)}) collective-permute-start(bf16[3,96,768]{2,1,0:T(8,128)(2,1)S(1)} %pad_maximum_fusion.3.refs_17_), channel_id=1, source_target_pairs={{0,16},{4,20},{8,24},{12,28},{16,0},{20,4},{24,8},{28,12},{1,17},{... | collective-permute-start | bytes 1327112 | tf_op jit(solution)/shard_map/ppermute | solution.py:943
  72.5 30.2 %collective-permute-start.22 = (bf16[3,96,768]{2,1,0:T(8,128)(2,1)S(1)}, bf16[3,96,768]{2,1,0:T(8,128)(2,1)S(1)}, u32[]{:S(2)}, u32[]{:S(2)}) collective-permute-start(bf16[3,96,768]{2,1,0:T(8,128)(2,1)S(1)} %pad_maximum_fusion.3.refs_17_), channel_id=1, source_target_pairs={{0,8},{4,12},{8,0},{12,4},{16,24},{20,28},{24,16},{28,20},{1,9},{5... | collective-permute-start | bytes 1327112 | tf_op jit(solution)/shard_map/ppermute | solution.py:943
  73.7 26.3 %collective-permute-start.16 = (bf16[3,96,768]{2,1,0:T(8,128)(2,1)S(1)}, bf16[3,96,768]{2,1,0:T(8,128)(2,1)S(1)}, u32[]{:S(2)}, u32[]{:S(2)}) collective-permute-start(bf16[3,96,768]{2,1,0:T(8,128)(2,1)S(1)} %pad_maximum_fusion.2.refs_9_), channel_id=1, source_target_pairs={{0,16},{4,20},{8,24},{12,28},{16,0},{20,4},{24,8},{28,12},{1,17},{... | collective-permute-start | bytes 1327112 | tf_op jit(solution)/shard_map/ppermute | solution.py:943
  74.0 24.8 %collective-permute-start.15 = (bf16[3,96,768]{2,1,0:T(8,128)(2,1)S(1)}, bf16[3,96,768]{2,1,0:T(8,128)(2,1)S(1)}, u32[]{:S(2)}, u32[]{:S(2)}) collective-permute-start(bf16[3,96,768]{2,1,0:T(8,128)(2,1)S(1)} %pad_maximum_fusion.2.refs_9_), channel_id=1, source_target_pairs={{0,8},{4,12},{8,0},{12,4},{16,24},{20,28},{24,16},{28,20},{1,9},{5... | collective-permute-start | bytes 1327112 | tf_op jit(solution)/shard_map/ppermute | solution.py:943
  97.3 11.2 %collective-permute-start.27 = (bf16[3,96,768]{2,1,0:T(8,128)(2,1)S(1)}, bf16[3,96,768]{2,1,0:T(8,128)(2,1)}, u32[]{:S(2)}, u32[]{:S(2)}) collective-permute-start(bf16[3,96,768]{2,1,0:T(8,128)(2,1)S(1)} %collective-permute-done.23.refs_21_), channel_id=1, source_target_pairs={{0,8},{4,12},{8,0},{12,4},{16,24},{20,28},{24,16},{28,20},{1,9},{5... | collective-permute-start | bytes 1327112 | tf_op jit(solution)/shard_map/ppermute | solution.py:943
  98.7 11.3 %collective-permute-start.20 = (bf16[3,96,768]{2,1,0:T(8,128)(2,1)S(1)}, bf16[3,96,768]{2,1,0:T(8,128)(2,1)}, u32[]{:S(2)}, u32[]{:S(2)}) collective-permute-start(bf16[3,96,768]{2,1,0:T(8,128)(2,1)S(1)} %collective-permute-done.15.refs_11_), channel_id=1, source_target_pairs={{0,16},{4,20},{8,24},{12,28},{16,0},{20,4},{24,8},{28,12},{1,17},{... | collective-permute-start | bytes 1327112 | tf_op jit(solution)/shard_map/ppermute | solution.py:943
  100.0 11.5 %collective-permute-start.17 = (bf16[3,96,768]{2,1,0:T(8,128)(2,1)S(1)}, bf16[3,96,768]{2,1,0:T(8,128)(2,1)S(1)}, u32[]{:S(2)}, u32[]{:S(2)}) collective-permute-start(bf16[3,96,768]{2,1,0:T(8,128)(2,1)S(1)} %pad_maximum_fusion.2.refs_9_), channel_id=1, source_target_pairs={{0,4},{4,0},{8,12},{12,8},{16,20},{20,16},{24,28},{28,24},{1,5},{5... | collective-permute-start | bytes 1327112 | tf_op jit(solution)/shard_map/ppermute | solution.py:943
  102.6 8.9 %collective-permute-start.18 = (bf16[3,96,768]{2,1,0:T(8,128)(2,1)S(1)}, bf16[3,96,768]{2,1,0:T(8,128)(2,1)S(1)}, u32[]{:S(2)}, u32[]{:S(2)}) collective-permute-start(bf16[3,96,768]{2,1,0:T(8,128)(2,1)S(1)} %collective-permute-done.15.refs_11_), channel_id=1, source_target_pairs={{0,4},{4,0},{8,12},{12,8},{16,20},{20,16},{24,28},{28,24},{1,5},{5... | collective-permute-start | bytes 1327112 | tf_op jit(solution)/shard_map/ppermute | solution.py:943
  102.7 9.3 %collective-permute-start.19 = (bf16[3,96,768]{2,1,0:T(8,128)(2,1)S(1)}, bf16[3,96,768]{2,1,0:T(8,128)(2,1)S(1)}, u32[]{:S(2)}, u32[]{:S(2)}) collective-permute-start(bf16[3,96,768]{2,1,0:T(8,128)(2,1)S(1)} %collective-permute-done.16.refs_13_), channel_id=1, source_target_pairs={{0,4},{4,0},{8,12},{12,8},{16,20},{20,16},{24,28},{28,24},{1,5},{5... | collective-permute-start | bytes 1327112 | tf_op jit(solution)/shard_map/ppermute | solution.py:943
  160.9 29.2 %collective-permute-start.29 = (bf16[4,4,2,96,768]{4,3,2,1,0:T(8,128)(2,1)}, bf16[4,4,2,96,768]{4,3,2,1,0:T(8,128)(2,1)}, u32[]{:S(2)}, u32[]{:S(2)}) collective-permute-start(bf16[4,4,2,96,768]{4,3,2,1,0:T(8,128)(2,1)} %get-tuple-element.194), channel_id=1, source_target_pairs={{0,4},{4,0},{8,12},{12,8},{16,20},{20,16},{24,28},{28,24},{1,5},{5... | collective-permute-start | bytes 14155784 | tf_op jit(solution)/shard_map/ppermute | solution.py:943
  161.3 28.7 %all-to-all-start.2 = ((bf16[8,128,768]{2,1,0:T(8,128)(2,1)}), bf16[8,128,768]{2,1,0:T(8,128)(2,1)S(1)}, u32[]{:S(2)}, u32[]{:S(2)}) async-start(bf16[8,128,768]{2,1,0:T(8,128)(2,1)} %bitcast.61), calls=%async_computation.2 | async-start | bytes 3145728 | tf_op jit(solution)/shard_map/all_to_all | solution.py:971
  189.9 42.4 %collective-permute-start.32 = (bf16[4,4,48,768]{3,2,1,0:T(8,128)(2,1)}, bf16[4,4,48,768]{3,2,1,0:T(8,128)(2,1)S(1)}, u32[]{:S(2)}, u32[]{:S(2)}) collective-permute-start(bf16[4,4,48,768]{3,2,1,0:T(8,128)(2,1)} %get-tuple-element.210), channel_id=1, source_target_pairs={{0,4},{4,0},{8,12},{12,8},{16,20},{20,16},{24,28},{28,24},{1,5},{5... | collective-permute-start | bytes 3538952 | tf_op jit(solution)/shard_map/ppermute | solution.py:943
  196.5 28.3 %collective-permute-start.30 = (bf16[2,4,96,768]{3,2,1,0:T(8,128)(2,1)}, bf16[2,4,96,768]{3,2,1,0:T(8,128)(2,1)S(1)}, u32[]{:S(2)}, u32[]{:S(2)}) collective-permute-start(bf16[2,4,96,768]{3,2,1,0:T(8,128)(2,1)} %get-tuple-element.204), channel_id=1, source_target_pairs={{0,8},{4,12},{8,0},{12,4},{16,24},{20,28},{24,16},{28,20},{1,9},{5... | collective-permute-start | bytes 3538952 | tf_op jit(solution)/shard_map/ppermute | solution.py:943
  198.2 27.3 %collective-permute-start.31 = (bf16[2,4,96,768]{3,2,1,0:T(8,128)(2,1)}, bf16[2,4,96,768]{3,2,1,0:T(8,128)(2,1)S(1)}, u32[]{:S(2)}, u32[]{:S(2)}) collective-permute-start(bf16[2,4,96,768]{3,2,1,0:T(8,128)(2,1)} %get-tuple-element.206), channel_id=1, source_target_pairs={{0,16},{4,20},{8,24},{12,28},{16,0},{20,4},{24,8},{28,12},{1,17},{... | collective-permute-start | bytes 3538952 | tf_op jit(solution)/shard_map/ppermute | solution.py:943
  224.0 8.3 %collective-permute-start.33 = (bf16[4,4,48,768]{3,2,1,0:T(8,128)(2,1)}, bf16[4,4,48,768]{3,2,1,0:T(8,128)(2,1)S(1)}, u32[]{:S(2)}, u32[]{:S(2)}) collective-permute-start(bf16[4,4,48,768]{3,2,1,0:T(8,128)(2,1)} %get-tuple-element.211), channel_id=1, source_target_pairs={{0,4},{4,0},{8,12},{12,8},{16,20},{20,16},{24,28},{28,24},{1,5},{5... | collective-permute-start | bytes 3538952 | tf_op jit(solution)/shard_map/ppermute | solution.py:943
  230.3 20.8 %collective-permute-start.37 = (bf16[4,96,768]{2,1,0:T(8,128)(2,1)}, bf16[4,96,768]{2,1,0:T(8,128)(2,1)S(1)}, u32[]{:S(2)}, u32[]{:S(2)}) collective-permute-start(bf16[4,96,768]{2,1,0:T(8,128)(2,1)} %get-tuple-element.223), channel_id=1, source_target_pairs={{0,16},{4,20},{8,24},{12,28},{16,0},{20,4},{24,8},{28,12},{1,17},{... | collective-permute-start | bytes 1769480 | tf_op jit(solution)/shard_map/ppermute | solution.py:943
  231.6 19.5 %collective-permute-start.38 = (bf16[4,96,768]{2,1,0:T(8,128)(2,1)}, bf16[4,96,768]{2,1,0:T(8,128)(2,1)S(1)}, u32[]{:S(2)}, u32[]{:S(2)}) collective-permute-start(bf16[4,96,768]{2,1,0:T(8,128)(2,1)} %get-tuple-element.225), channel_id=1, source_target_pairs={{0,8},{4,12},{8,0},{12,4},{16,24},{20,28},{24,16},{28,20},{1,9},{5... | collective-permute-start | bytes 1769480 | tf_op jit(solution)/shard_map/ppermute | solution.py:943
  238.2 19.5 %collective-permute-start.34 = (bf16[384,768]{1,0:T(8,128)(2,1)}, bf16[384,768]{1,0:T(8,128)(2,1)S(1)}, u32[]{:S(2)}, u32[]{:S(2)}) collective-permute-start(bf16[384,768]{1,0:T(8,128)(2,1)} %get-tuple-element.218), channel_id=1, source_target_pairs={{0,8},{4,12},{8,0},{12,4},{16,24},{20,28},{24,16},{28,20},{1,9},{5... | collective-permute-start | bytes 1769480 | tf_op jit(solution)/shard_map/ppermute | solution.py:943
  239.0 20.4 %collective-permute-start.35 = (bf16[384,768]{1,0:T(8,128)(2,1)}, bf16[384,768]{1,0:T(8,128)(2,1)S(1)}, u32[]{:S(2)}, u32[]{:S(2)}) collective-permute-start(bf16[384,768]{1,0:T(8,128)(2,1)} %get-tuple-element.219), channel_id=1, source_target_pairs={{0,16},{4,20},{8,24},{12,28},{16,0},{20,4},{24,8},{28,12},{1,17},{... | collective-permute-start | bytes 1769480 | tf_op jit(solution)/shard_map/ppermute | solution.py:943
  239.2 31.1 %collective-permute-start.36 = (bf16[384,768]{1,0:T(8,128)(2,1)}, bf16[384,768]{1,0:T(8,128)(2,1)S(1)}, u32[]{:S(2)}, u32[]{:S(2)}) collective-permute-start(bf16[384,768]{1,0:T(8,128)(2,1)} %get-tuple-element.220), channel_id=1, source_target_pairs={{0,24},{4,28},{8,16},{12,20},{16,8},{20,12},{24,0},{28,4},{1,25},{... | collective-permute-start | bytes 1769480 | tf_op jit(solution)/shard_map/ppermute | solution.py:943
  254.8 15.4 %collective-permute-start.39 = (bf16[2,96,768]{2,1,0:T(8,128)(2,1)}, bf16[2,96,768]{2,1,0:T(8,128)(2,1)S(1)}, u32[]{:S(2)}, u32[]{:S(2)}) collective-permute-start(bf16[2,96,768]{2,1,0:T(8,128)(2,1)} %get-tuple-element.227), channel_id=1, source_target_pairs={{0,1},{1,0},{2,3},{3,2},{4,5},{5,4},{6,7},{7,6},{8,9},{9,8},{10,11... | collective-permute-start | bytes 884744 | tf_op jit(solution)/shard_map/ppermute | solution.py:943
  257.4 12.8 %collective-permute-start.40 = (bf16[2,96,768]{2,1,0:T(8,128)(2,1)}, bf16[2,96,768]{2,1,0:T(8,128)(2,1)S(1)}, u32[]{:S(2)}, u32[]{:S(2)}) collective-permute-start(bf16[2,96,768]{2,1,0:T(8,128)(2,1)} %get-tuple-element.228), channel_id=1, source_target_pairs={{0,2},{1,3},{2,0},{3,1},{4,6},{5,7},{6,4},{7,5},{8,10},{9,11},{10,... | collective-permute-start | bytes 884744 | tf_op jit(solution)/shard_map/ppermute | solution.py:943
  257.7 25.1 %collective-permute-start.47 = (bf16[2,96,768]{2,1,0:T(8,128)(2,1)}, bf16[2,96,768]{2,1,0:T(8,128)(2,1)S(1)}, u32[]{:S(2)}, u32[]{:S(2)}) collective-permute-start(bf16[2,96,768]{2,1,0:T(8,128)(2,1)} %get-tuple-element.243), channel_id=1, source_target_pairs={{0,3},{1,2},{2,1},{3,0},{4,7},{5,6},{6,5},{7,4},{8,11},{9,10},{10,... | collective-permute-start | bytes 884744 | tf_op jit(solution)/shard_map/ppermute | solution.py:943
  284.0 16.5 %collective-permute-start.43 = (bf16[112,768]{1,0:T(8,128)(2,1)}, bf16[112,768]{1,0:T(8,128)(2,1)S(1)}, u32[]{:S(2)}, u32[]{:S(2)}) collective-permute-start(bf16[112,768]{1,0:T(8,128)(2,1)} %get-tuple-element.238), channel_id=1, source_target_pairs={{0,3},{1,2},{2,1},{3,0},{4,7},{5,6},{6,5},{7,4},{8,11},{9,10},{10,... | collective-permute-start | bytes 516104 | tf_op jit(solution)/shard_map/ppermute | solution.py:943
  285.7 15.0 %collective-permute-start.50 = (bf16[2,96,768]{2,1,0:T(8,128)(2,1)S(1)}, bf16[2,96,768]{2,1,0:T(8,128)(2,1)S(1)}, u32[]{:S(2)}, u32[]{:S(2)}) collective-permute-start(bf16[2,96,768]{2,1,0:T(8,128)(2,1)S(1)} %add_convert_fusion.refs_0_), channel_id=1, source_target_pairs={{0,24},{4,28},{8,16},{12,20},{16,8},{20,12},{24,0},{28,4},{1,25},{... | collective-permute-start | bytes 884744 | tf_op jit(solution)/shard_map/ppermute | solution.py:943
  286.4 14.3 %collective-permute-start.49 = (bf16[2,96,768]{2,1,0:T(8,128)(2,1)S(1)}, bf16[2,96,768]{2,1,0:T(8,128)(2,1)S(1)}, u32[]{:S(2)}, u32[]{:S(2)}) collective-permute-start(bf16[2,96,768]{2,1,0:T(8,128)(2,1)S(1)} %add_convert_fusion.refs_0_), channel_id=1, source_target_pairs={{0,16},{4,20},{8,24},{12,28},{16,0},{20,4},{24,8},{28,12},{1,17},{... | collective-permute-start | bytes 884744 | tf_op jit(solution)/shard_map/ppermute | solution.py:943
  287.7 13.0 %collective-permute-start.48 = (bf16[2,96,768]{2,1,0:T(8,128)(2,1)S(1)}, bf16[2,96,768]{2,1,0:T(8,128)(2,1)S(1)}, u32[]{:S(2)}, u32[]{:S(2)}) collective-permute-start(bf16[2,96,768]{2,1,0:T(8,128)(2,1)S(1)} %add_convert_fusion.refs_0_), channel_id=1, source_target_pairs={{0,8},{4,12},{8,0},{12,4},{16,24},{20,28},{24,16},{28,20},{1,9},{5... | collective-permute-start | bytes 884744 | tf_op jit(solution)/shard_map/ppermute | solution.py:943
  303.0 12.8 %collective-permute-start.46 = (bf16[112,768]{1,0:T(8,128)(2,1)S(1)}, bf16[112,768]{1,0:T(8,128)(2,1)S(1)}, u32[]{:S(2)}, u32[]{:S(2)}) collective-permute-start(bf16[112,768]{1,0:T(8,128)(2,1)S(1)} %add_convert_fusion.1), channel_id=1, source_target_pairs={{0,24},{4,28},{8,16},{12,20},{16,8},{20,12},{24,0},{28,4},{1,25},{... | collective-permute-start | bytes 516104 | tf_op jit(solution)/shard_map/ppermute | solution.py:943
  303.8 12.0 %collective-permute-start.45 = (bf16[112,768]{1,0:T(8,128)(2,1)S(1)}, bf16[112,768]{1,0:T(8,128)(2,1)S(1)}, u32[]{:S(2)}, u32[]{:S(2)}) collective-permute-start(bf16[112,768]{1,0:T(8,128)(2,1)S(1)} %add_convert_fusion.1), channel_id=1, source_target_pairs={{0,16},{4,20},{8,24},{12,28},{16,0},{20,4},{24,8},{28,12},{1,17},{... | collective-permute-start | bytes 516104 | tf_op jit(solution)/shard_map/ppermute | solution.py:943
  304.9 10.9 %collective-permute-start.44 = (bf16[112,768]{1,0:T(8,128)(2,1)S(1)}, bf16[112,768]{1,0:T(8,128)(2,1)S(1)}, u32[]{:S(2)}, u32[]{:S(2)}) collective-permute-start(bf16[112,768]{1,0:T(8,128)(2,1)S(1)} %add_convert_fusion.1), channel_id=1, source_target_pairs={{0,8},{4,12},{8,0},{12,4},{16,24},{20,28},{24,16},{28,20},{1,9},{5... | collective-permute-start | bytes 516104 | tf_op jit(solution)/shard_map/ppermute | solution.py:943
  317.1 25.1 %all-to-all-start.3 = ((bf16[8,128,768]{2,1,0:T(8,128)(2,1)}), bf16[8,128,768]{2,1,0:T(8,128)(2,1)S(1)}, u32[]{:S(2)}, u32[]{:S(2)}) async-start(bf16[8,128,768]{2,1,0:T(8,128)(2,1)} %bitcast.27), calls=%async_computation.3 | async-start | bytes 3145728 | tf_op jit(solution)/shard_map/all_to_all | solution.py:971
  (70 other events, 477.6 us)
